TPU v7x, 32 devices: a whole 2x2x4 slice. The times are simulated.
32 devices in a mesh: blk: 4 (over y, x), uly: 8 (over z, core).
Axes of the slice: x: 2, y: 2, z: 4, core: 2. Of those that a mesh axis runs over, the one named last changes fastest.
Arguments:
- hidden_in: bfloat16 [4096, 2048], P(('blk', 'uly')), may hold values from -18 to 18
- queries: bfloat16 [4096, 2048], P(('blk', 'uly')), may hold values from -41 to 41
- keys: bfloat16 [4096, 256], P(('blk', 'uly')), may hold values from -4 to 4
- values: bfloat16 [4096, 256], P(('blk', 'uly')), may hold values from -24 to 24
- segment_ids: int32 [4096], P(('blk', 'uly')), may hold values from 0 to 63, never falling along the last dimension, each value on 1 to 512 neighbouring positions
- prefix_ids: int32 [64], replicated, may hold values from 0 to 63
- o_weight: bfloat16 [2048, 2048], replicated, may hold values from -0.125 to 0.125
- post_gain: float32 [2048], replicated, may hold values from 0.1 to 1.9
- expert_ids: int32 [4096, 8], P(('blk', 'uly')), may hold values from 0 to 31, all different within a row; in each aligned block of 128 rows (0 to 127, 128 to 255, ...) at most 36 rows name the same one
- gates: float32 [4096, 8], P(('blk', 'uly')), may hold values from 0.05 to 1
- w_gate: bfloat16 [32, 2048, 768], P(('blk', 'uly')), may hold values from -0.125 to 0.125
- w_up: bfloat16 [32, 2048, 768], P(('blk', 'uly')), may hold values from -0.125 to 0.125
- w_down: bfloat16 [32, 768, 2048], P(('blk', 'uly')), may hold values from -0.21875 to 0.21875
Outputs:
- layer_out: bfloat16 [4096, 2048], P(('blk', 'uly'))
Inputs may be any that keep to these rules, and one draw needn't show every extreme that they name: `segment_ids`: never falling along the window; each segment holds 1 to 512 positions, one exactly 512. `expert_ids`: each row names 8 different experts; within the rows of one device (aligned blocks of 128 tokens) no expert is named more than 36 times.
All inputs are finite; a program needn't handle non-finite values.
Results may differ from a plain program's by a relative error of at most 0.006.
Values may be sent and summed in bfloat16 or wider, within the bound.
No kernel may reach another device: no remote copies, remote signals or barrier semaphores. Data moves between devices by JAX's collectives and lax.ppermute only.
A program may use at most 128 MiB of HBM per device.

v0:
```python
import math

import jax
import jax.numpy as jnp
from jax import lax
from jax.sharding import PartitionSpec as P

HEAD_SIZE = 128


floor_score = -1e30


def shards(
    hidden_in,
    queries,
    keys,
    values,
    segment_ids,
    prefix_ids,
    o_weight,
    post_gain,
    expert_ids,
    gates,
    w_gate,
    w_up,
    w_down,
):
    tok_rows, model_width = hidden_in.shape
    n_blk = lax.axis_size("blk")
    n_uly = lax.axis_size("uly")
    experts_all = n_blk * n_uly
    top_count = expert_ids.shape[1]
    heads_all = queries.shape[1] // HEAD_SIZE
    kv_count = keys.shape[1] // HEAD_SIZE
    heads_here = heads_all // n_uly
    group_width = heads_all // kv_count
    query_rows = tok_rows * n_uly
    all_segments = lax.all_gather(segment_ids, ("blk", "uly"), axis=0, tiled=True)
    key_wide = jnp.repeat(keys.reshape(tok_rows, kv_count, HEAD_SIZE), group_width, axis=1).reshape(
        tok_rows, heads_all * HEAD_SIZE
    )
    value_wide = jnp.repeat(
        values.reshape(tok_rows, kv_count, HEAD_SIZE), group_width, axis=1
    ).reshape(tok_rows, heads_all * HEAD_SIZE)
    query_here, key_here, value_here = (
        lax.all_to_all(queries, "uly", split_axis=1, concat_axis=0, tiled=True),
        lax.all_to_all(key_wide, "uly", split_axis=1, concat_axis=0, tiled=True),
        lax.all_to_all(value_wide, "uly", split_axis=1, concat_axis=0, tiled=True),
    )
    block_start = lax.axis_index("blk") * query_rows
    query_pos = block_start + jnp.arange(query_rows, dtype=jnp.int32)
    query_seg = lax.dynamic_slice_in_dim(all_segments, block_start, query_rows, 0)
    seg_table = jnp.arange(prefix_ids.shape[0], dtype=jnp.int32)
    query_pre = jnp.sum(
        jnp.where(query_seg[:, None] == seg_table[None, :], prefix_ids[None, :], 0), axis=1
    )
    query_three = query_here.reshape(query_rows, heads_here, HEAD_SIZE)
    score_scale = 1.0 / math.sqrt(HEAD_SIZE)

    def key_tile(carry_now, key_tile_rows, value_tile_rows, key_pos, key_seg):
        visible = (key_pos[None, :] <= query_pos[:, None]) & (
            (key_seg[None, :] == query_seg[:, None]) | (key_seg[None, :] == query_pre[:, None])
        )
        row_top, weight_sum, weighted = carry_now
        scores = (
            jnp.einsum(
                "qhd,khd->qhk", query_three, key_tile_rows, preferred_element_type=jnp.float32
            )
            * score_scale
        )
        score_mask = visible[:, None, :]
        tile_top = jnp.max(jnp.where(score_mask, scores, floor_score), axis=2)
        new_top = jnp.maximum(row_top, tile_top)
        exp_scores = jnp.where(score_mask, jnp.exp(scores - new_top[:, :, None]), 0.0)
        rescale = jnp.exp(row_top - new_top)
        weight_sum = weight_sum * rescale + jnp.sum(exp_scores, axis=2)
        weighted = weighted * rescale[:, :, None] + jnp.einsum(
            "qhk,khd->qhd",
            exp_scores.astype(jnp.bfloat16),
            value_tile_rows,
            preferred_element_type=jnp.float32,
        )
        return (new_top, weight_sum, weighted)

    start_state = (
        jnp.full((query_rows, heads_here), floor_score, jnp.float32),
        jnp.zeros((query_rows, heads_here), jnp.float32),
        jnp.zeros((query_rows, heads_here, HEAD_SIZE), jnp.float32),
    )
    key_piece = lax.all_gather(key_here, "blk", axis=0, tiled=True)
    value_piece = lax.all_gather(value_here, "blk", axis=0, tiled=True)
    piece_rows = key_piece.shape[0]
    tile_rows = math.gcd(piece_rows, 512)

    def tile_step(tile_number, state_now):
        tile_start = tile_number * tile_rows
        key_tile_rows = lax.dynamic_slice_in_dim(key_piece, tile_start, tile_rows, 0).reshape(
            tile_rows, heads_here, HEAD_SIZE
        )
        value_tile_rows = lax.dynamic_slice_in_dim(value_piece, tile_start, tile_rows, 0).reshape(
            tile_rows, heads_here, HEAD_SIZE
        )
        key_pos = tile_start + jnp.arange(tile_rows, dtype=jnp.int32)
        key_seg = lax.dynamic_slice_in_dim(all_segments, tile_start, tile_rows, 0)
        return key_tile(state_now, key_tile_rows, value_tile_rows, key_pos, key_seg)

    row_top, weight_sum, weighted = lax.fori_loop(
        0, piece_rows // tile_rows, tile_step, start_state
    )
    attended = (
        (weighted / weight_sum[:, :, None])
        .reshape(query_rows, heads_here * HEAD_SIZE)
        .astype(jnp.bfloat16)
    )
    attended_rows = lax.all_to_all(attended, "uly", split_axis=0, concat_axis=1, tiled=True)
    mixed = hidden_in.astype(jnp.float32) + jnp.dot(
        attended_rows, o_weight, preferred_element_type=jnp.float32
    )
    normed = (
        mixed * lax.rsqrt(jnp.mean(mixed * mixed, axis=1, keepdims=True) + 1e-06) * post_gain
    ).astype(jnp.bfloat16)
    share = gates / jnp.sum(gates, axis=1, keepdims=True)
    capacity = max(2, 9 * tok_rows * top_count // (8 * experts_all))
    flat_experts = expert_ids.reshape(-1)
    expert_hits = (
        flat_experts[:, None] == jnp.arange(experts_all, dtype=jnp.int32)[None, :]
    ).astype(jnp.int32)
    earlier = jnp.cumsum(expert_hits, axis=0) - expert_hits
    slot_rank = jnp.sum(earlier * expert_hits, axis=1)
    slot_index = flat_experts * capacity + slot_rank
    sent_rows = jnp.repeat(normed, top_count, axis=0)
    outbox = (
        jnp.zeros((experts_all * capacity, model_width), jnp.bfloat16).at[slot_index].set(sent_rows)
    )
    received = lax.all_to_all(
        outbox.reshape(experts_all, capacity, model_width),
        ("blk", "uly"),
        split_axis=0,
        concat_axis=0,
        tiled=True,
    )
    sources, item_count, _ = received.shape
    flat_rows = received.reshape(sources * item_count, model_width)
    gate_proj = jnp.dot(flat_rows, w_gate[0], preferred_element_type=jnp.float32)
    up_proj = jnp.dot(flat_rows, w_up[0], preferred_element_type=jnp.float32)
    hidden_act = (jax.nn.silu(gate_proj) * up_proj).astype(jnp.bfloat16)
    expert_answer = jnp.dot(hidden_act, w_down[0], preferred_element_type=jnp.float32).astype(
        jnp.bfloat16
    )
    returned = lax.all_to_all(
        expert_answer.reshape(sources, item_count, model_width),
        ("blk", "uly"),
        split_axis=0,
        concat_axis=0,
        tiled=True,
    )
    back_rows = returned.reshape(experts_all * capacity, model_width)
    picked_rows = back_rows[slot_index].astype(jnp.float32) * share.reshape(-1)[:, None]
    routed = jnp.sum(picked_rows.reshape(tok_rows, top_count, model_width), axis=1)
    return (mixed + routed).astype(jnp.bfloat16)


def solution(mesh):
    in_specs = (
        P(("blk", "uly"), None),
        P(("blk", "uly"), None),
        P(("blk", "uly"), None),
        P(("blk", "uly"), None),
        P(("blk", "uly")),
        P(),
        P(),
        P(),
        P(("blk", "uly"), None),
        P(("blk", "uly"), None),
        P(("blk", "uly"), None, None),
        P(("blk", "uly"), None, None),
        P(("blk", "uly"), None, None),
    )
    out_specs = P(("blk", "uly"), None)
    return jax.shard_map(shards, mesh=mesh, in_specs=in_specs, out_specs=out_specs, check_vma=False)
```

profile of v0, /device:TPU:0, one launch (start us, length us, event | category | flops | bytes accessed | tf_op | source)
XLA Modules:
  0.0 609.4 jit_solution(17436746515026450208)
XLA Ops:
  7.8 21.6 %all_to_all.80 = bf16[128,8,256]{0,2,1:T(8,128)(2,1)} all-to-all(bf16[128,8,256]{0,2,1:T(8,128)(2,1)S(1)} %bitcast.113), channel_id=1, replica_groups=mesh['blk'=4,'uly'=8] {'uly'}, dimensions={1} | all-to-all | bytes 1048576 | tf_op jit(solution)/shard_map/all_to_all | solution.py:48
  32.6 18.4 %all_to_all.81 = bf16[128,8,256]{0,2,1:T(8,128)(2,1)} all-to-all(bf16[128,8,256]{0,2,1:T(8,128)(2,1)S(1)} %bitcast.115), channel_id=1, replica_groups=mesh['blk'=4,'uly'=8] {'uly'}, dimensions={1} | all-to-all | bytes 1048576 | tf_op jit(solution)/shard_map/all_to_all | solution.py:49
  59.6 43.8 %all-gather = s32[32,1,128]{2,1,0:T(1,128)S(1)} all-gather(s32[1,1,128]{2,1,0:T(1,128)S(1)} %bitcast.127), channel_id=1, replica_groups=mesh['blk'=4,'uly'=8] {'blk','uly'}, dimensions={0}, use_global_device_ids=true | all-gather | bytes 16896 | tf_op jit(solution)/shard_map/all_gather | solution.py:39
  109.9 147.3 %while.18 = (s32[]{:T(128)}, f32[1024,2]{0,1:T(2,128)S(1)}, f32[1024,2]{0,1:T(2,128)S(1)}, f32[1024,2,128]{0,2,1:T(8,128)}, s32[4096]{0:T(1024)S(1)}, /*index=5*...) while((s32[]{:T(128)}, f32[1024,2]{0,1:T(2,128)S(1)}, ...), condition=%wide.region_4.5_spmd.clone, body=%wide.region_1.4_spmd.clone.sunk | while | flops 551824896 | bytes 20080856 | solution.py:108
  141.3 5.1 fusion.62
  159.8 5.1 fusion.62
  178.2 5.1 fusion.62
  196.7 5.1 fusion.62
  215.1 5.1 fusion.62
  233.6 5.1 fusion.62
  252.0 5.1 fusion.62
  263.8 9.0 %reduce-window.6 = s32[32,8,128]{2,1,0:T(8,128)S(1)} reduce-window(s32[32,8,128]{2,1,0:T(8,128)S(1)} %fusion.36, s32[]{:T(128)} %constant.76.clone.1), window={size=1x1x128 pad=0_0x0_0x127_0}, to_apply=%region_5.6 | reduce-window | flops 4161536 | bytes 262148 | tf_op jit(solution)/shard_map/reduce-window
  273.5 5.4 all-to-all-done.3
  285.8 9.8 %scatter_custom_fusion = bf16[1152,2048]{1,0:T(8,128)(2,1)} fusion(s32[1024]{0:T(1024)S(1)} %bitcast.125, bf16[]{:T(256)} %constant.82.clone.1, bf16[128,2048]{1,0:T(8,128)(2,1)} %multiply_convert_fusion), kind=kCustom, calls=%fused_computation.33 | custom fusion | bytes 5242882 | tf_op jit(solution)/shard_map/scatter | solution.py:134
  295.7 7.2 %reshape.207 = bf16[32,36,2048]{2,1,0:T(8,128)(2,1)} reshape(bf16[1152,2048]{1,0:T(8,128)(2,1)} %scatter_custom_fusion) | data formatting | bytes 9437184 | tf_op jit(solution)/shard_map/reshape | solution.py:137
  302.9 121.0 %all_to_all.82 = bf16[32,36,2048]{2,1,0:T(8,128)(2,1)} all-to-all(bf16[32,36,2048]{2,1,0:T(8,128)(2,1)} %reshape.207), channel_id=1, replica_groups=mesh['blk'=4,'uly'=8] {'blk','uly'}, dimensions={0} | all-to-all | bytes 9437184 | tf_op jit(solution)/shard_map/all_to_all | solution.py:136
  423.9 7.2 %reshape.208 = bf16[1152,2048]{1,0:T(8,128)(2,1)} reshape(bf16[32,36,2048]{2,1,0:T(8,128)(2,1)} %all_to_all.82) | data formatting | bytes 9437184 | tf_op jit(solution)/shard_map/reshape | solution.py:144
  431.1 6.8 %fusion.29 = f32[1152,768]{1,0:T(8,128)S(1)} fusion(bf16[1152,2048]{1,0:T(8,128)(2,1)} %reshape.208, bf16[1,2048,768]{2,1,0:T(8,128)(2,1)} %param.25), kind=kOutput, calls=%fused_computation.39 | convolution fusion | flops 3623878656 | bytes 11403264 | tf_op jit(solution)/shard_map/dot_general | solution.py:145
  442.1 5.5 convolution_convert_fusion
  447.6 7.2 %reshape.209 = bf16[32,36,2048]{2,1,0:T(8,128)(2,1)} reshape(bf16[1152,2048]{1,0:T(8,128)(2,1)} %convolution_convert_fusion) | data formatting | bytes 9437184 | tf_op jit(solution)/shard_map/reshape | solution.py:152
  459.0 117.1 %all-to-all-done.5 = bf16[32,36,2048]{2,1,0:T(8,128)(2,1)} async-done(((bf16[32,36,2048]{2,1,0:T(8,128)(2,1)}), bf16[32,36,2048]{2,1,0:T(8,128)(2,1)}, u32[]{:S(2)}, u32[]{:S(2)}) %all-to-all-start.5) | async-done | bytes 4718624 | tf_op jit(solution)/shard_map/all_to_all | solution.py:151
  576.1 7.2 %reshape.210 = bf16[1152,2048]{1,0:T(8,128)(2,1)} reshape(bf16[32,36,2048]{2,1,0:T(8,128)(2,1)} %all-to-all-done.5) | data formatting | bytes 9437184 | tf_op jit(solution)/shard_map/reshape | solution.py:158
  583.3 11.8 %gather_fusion = bf16[1024,2048]{1,0:T(8,128)(2,1)} fusion(bf16[1152,2048]{1,0:T(8,128)(2,1)} %reshape.210, s32[1024]{0:T(1024)S(1)} %broadcast_clamp_fusion), kind=kCustom, calls=%fused_computation | custom fusion | bytes 8392704 | tf_op jit(solution)/shard_map/gather | solution.py:159
  595.1 6.6 %fusion.23 = f32[128,2048]{1,0:T(8,128)S(1)} fusion(bf16[1024,2048]{1,0:T(8,128)(2,1)} %gather_fusion, f32[128,8]{1,0:T(8,128)S(1)} %copy.80), kind=kLoop, calls=%fused_computation.31 | loop fusion | flops 6029312 | bytes 5246976 | tf_op jit(solution)/shard_map/reduce_sum | solution.py:160
  (169 shorter events, 154.2 us)
Async XLA Ops:
  6.5 435.6 %copy-start = (bf16[1,768,2048]{2,1,0:T(8,128)(2,1)S(1)}, bf16[1,768,2048]{2,1,0:T(8,128)(2,1)}, u32[]{:S(2)}) copy-start(bf16[1,768,2048]{2,1,0:T(8,128)(2,1)} %param.27) | copy-start | bytes 9437188
  6.5 103.3 %all-gather.4.cloned.1.call-start = ((), (), s32[]{:S(2)}) async-start(), calls=%async_computation.6 | async-start | bytes 2621440 | tf_op jit(solution)/shard_map/all_gather | solution.py:91
  7.6 51.7 %copy-start.4 = (s32[128,8]{0,1:T(8,128)S(1)}, s32[128,8]{0,1:T(8,128)}, u32[]{:S(2)}) copy-start(s32[128,8]{0,1:T(8,128)} %param.23) | copy-start | bytes 12292
  7.8 51.8 %copy-start.7 = (s32[128]{0:T(128)S(1)}, s32[128]{0:T(128)}, u32[]{:S(2)}) copy-start(s32[128]{0:T(128)} %param.19) | copy-start | bytes 1540
  7.8 95.7 %copy-start.8 = (s32[64]{0:T(128)S(1)}, s32[64]{0:T(128)}, u32[]{:S(2)}) copy-start(s32[64]{0:T(128)} %param.20) | copy-start | bytes 772
  31.4 78.4 %all-gather.6.cloned.1.call-start = ((), (), s32[]{:S(2)}) async-start(), calls=%async_computation.7 | async-start | bytes 2621440 | tf_op jit(solution)/shard_map/all_gather | solution.py:92
  55.1 48.4 %all-to-all-start.1 = ((bf16[128,8,256]{0,2,1:T(8,128)(2,1)}), bf16[128,8,256]{0,2,1:T(8,128)(2,1)}, u32[]{:S(2)}, u32[]{:S(2)}) async-start(bf16[128,8,256]{0,2,1:T(8,128)(2,1)} %bitcast.112), calls=%async_computation.1 | async-start | bytes 1048576 | tf_op jit(solution)/shard_map/all_to_all | solution.py:47
  259.4 19.5 %all-to-all-start.3 = ((bf16[8,128,256]{1,2,0:T(8,128)(2,1)}), bf16[8,128,256]{1,2,0:T(8,128)(2,1)}, u32[]{:S(2)}, u32[]{:S(2)}) async-start(bf16[8,128,256]{1,2,0:T(8,128)(2,1)} %copy.74), calls=%async_computation.3 | async-start | bytes 1048576 | tf_op jit(solution)/shard_map/all_to_all | solution.py:116
  279.0 5.9 copy-start.6
  283.9 1.0 copy-start.1
  431.1 6.8 %copy-start.3 = (bf16[1152,2048]{1,0:T(8,128)(2,1)S(1)}, bf16[1152,2048]{1,0:T(8,128)(2,1)}, u32[]{:S(2)}) copy-start(bf16[1152,2048]{1,0:T(8,128)(2,1)} %reshape.208) | copy-start | bytes 14155780
  431.1 6.8 %copy-start.9 = (bf16[1,2048,768]{2,1,0:T(8,128)(2,1)S(1)}, bf16[1,2048,768]{2,1,0:T(8,128)(2,1)}, u32[]{:S(2)}) copy-start(bf16[1,2048,768]{2,1,0:T(8,128)(2,1)} %param.26) | copy-start | bytes 9437188
  454.8 4.0 copy-start.5
  454.8 121.2 %all-to-all-start.5 = ((bf16[32,36,2048]{2,1,0:T(8,128)(2,1)}), bf16[32,36,2048]{2,1,0:T(8,128)(2,1)}, u32[]{:S(2)}, u32[]{:S(2)}) async-start(bf16[32,36,2048]{2,1,0:T(8,128)(2,1)} %reshape.209), calls=%async_computation.5 | async-start | bytes 10485760 | tf_op jit(solution)/shard_map/all_to_all | solution.py:151
  595.1 6.6 %copy-start.2 = (f32[128,2048]{1,0:T(8,128)S(1)}, f32[128,2048]{1,0:T(8,128)}, u32[]{:S(2)}) copy-start(f32[128,2048]{1,0:T(8,128)} %copy-done.1) | copy-start | bytes 3145732
Sparse Core Ops, SparseCore 0:
  31.6 34.2 all-gather.3
  67.7 35.3 all-gather.5
where the time goes:
time: 612 us; the launch traced here: 609 us
  blocking collectives  205 us (33%)
  waiting for transfers between devices  123 us (20%)
  local copies, waits for them, and re-layouts  104 us (17%)
  matrix products  95.3 us (16%)
  other arithmetic  56.4 us (9%)
  between operations  13.7 us (2%)
  starting transfers between devices  12.5 us (2%)
    all_to_all x1, blocking collectives, shards(): lax.all_to_all(outbox.reshape(experts_all, capacity, model_width), ('blk'...  121 us
    all_to_all x1, waiting for transfers between devices, shards(): lax.all_to_all(expert_answer.reshape(sources, item_count, model_width), (...  117 us
    all_gather x1, blocking collectives, shards(): lax.all_gather(segment_ids, ('blk', 'uly'), axis=0, tiled=True)  43.8 us
    dot_general x8, matrix products, key_tile(): jnp.einsum('qhk,khd->qhd', exp_scores.astype(jnp.bfloat16), value_tile_ro...  40.5 us
    dot_general x8, matrix products, key_tile(): jnp.einsum('qhd,khd->qhk', query_three, key_tile_rows, preferred_element_...  33.5 us
    reduce_sum x8, other arithmetic, key_tile(): weight_sum = weight_sum * rescale + jnp.sum(exp_scores, axis=2)  26.2 us
    all_to_all x1, blocking collectives, shards(): lax.all_to_all(key_wide, 'uly', split_axis=1, concat_axis=0, tiled=True)  21.6 us
    dynamic_slice x16, local copies, waits for them, and re-layouts, tile_step(): lax.dynamic_slice_in_dim(value_piece, tile_start, tile_rows, 0)  20.9 us
  transfers between devices with their start and end apart: 5, of which 2 were waited for; matrix products, arithmetic and copies ran while one was open for 4% of the time, Pallas kernels for 0%

commit v1 on v0

v1 whole, which is shorter than its diff:
```python
import functools
import math

import jax
import jax.numpy as jnp
from jax import lax
from jax.experimental import pallas as pl
from jax.experimental.pallas import tpu as pltpu
from jax.sharding import PartitionSpec as P

HEAD_SIZE = 128
EXTRA_ROWS = 8
FLOOR = -1e20
HIDDEN = -1e30


def chip_ring(count):
    return list(range(0, 1)) + list(range(1, count, 2)) + list(range(2, count, 2))[::-1]


def attend_kernel(first, last, counts, info_ref, q_ref, seg_q_ref, pre_q_ref, seg_k_ref, *refs):
    kv_refs, refs = refs[: len(counts)], refs[len(counts) :]
    if not first:
        top_in, sum_in, acc_in, *refs = refs
    if last:
        out_ref, top_ref, sum_ref, acc_ref = refs
    else:
        top_ref, sum_ref, acc_ref = refs
    kv_count, _, columns = q_ref.shape
    rows = seg_q_ref.shape[1]
    tiles = sum(counts)
    scale = math.log2(math.e) / math.sqrt(HEAD_SIZE)
    width = 2 * rows if columns % (2 * rows) == 0 else rows
    if first:
        top_ref[...] = jnp.full_like(top_ref, FLOOR)
        sum_ref[...] = jnp.zeros_like(sum_ref)
        acc_ref[...] = jnp.zeros_like(acc_ref)
    else:
        top_ref[...] = top_in[...]
        sum_ref[...] = sum_in[...]
        acc_ref[...] = acc_in[...]
    query_pos = info_ref[2 * tiles] + lax.broadcasted_iota(jnp.int32, (rows, rows), 1)
    start = 0
    for kv_ref, count in zip(kv_refs, counts, strict=True):

        def tile_step(i, _, kv_ref=kv_ref, start=start):
            tile = start + i

            @pl.when(info_ref[tile] > 0)
            def _():
                key_pos = info_ref[tiles + tile] + lax.broadcasted_iota(
                    jnp.int32, (rows, rows), 0
                )
                key_seg = jnp.broadcast_to(seg_k_ref[tile], (rows, rows)).T
                visible = (key_pos <= query_pos) & (
                    (key_seg == seg_q_ref[...]) | (key_seg == pre_q_ref[...])
                )
                bias = jnp.where(visible, 0.0, HIDDEN)
                bias = jnp.concatenate([bias] * (width // rows), axis=1)
                for g in range(kv_count):
                    key_tile = kv_ref[i, :rows, g * HEAD_SIZE : (g + 1) * HEAD_SIZE]
                    value_tile = kv_ref[
                        i, :rows, (kv_count + g) * HEAD_SIZE : (kv_count + g + 1) * HEAD_SIZE
                    ]
                    for at in range(0, columns, width):
                        part = pl.ds(at, width)
                        scores = (
                            jnp.dot(
                                key_tile, q_ref[g, :, part], preferred_element_type=jnp.float32
                            )
                            * scale
                            + bias
                        )
                        old_top = top_ref[g, :, part]
                        new_top = jnp.maximum(old_top, jnp.max(scores, axis=0, keepdims=True))
                        weights = jnp.exp2(scores - new_top)
                        rescale = jnp.exp2(old_top - new_top)
                        top_ref[g, :, part] = new_top
                        sum_ref[g, :, part] = sum_ref[g, :, part] * rescale + jnp.sum(
                            weights, axis=0, keepdims=True
                        )
                        acc_ref[g, :, part] = acc_ref[g, :, part] * rescale + jnp.dot(
                            value_tile,
                            weights.astype(jnp.bfloat16),
                            preferred_element_type=jnp.float32,
                        )

            return 0

        lax.fori_loop(0, count, tile_step, 0)
        start += count
    if last:
        for g in range(kv_count):
            for h in range(columns // rows):
                part = pl.ds(h * rows, rows)
                result = acc_ref[g, :, part] / sum_ref[g, :, part]
                at = (g * (columns // rows) + h) * HEAD_SIZE
                out_ref[:, at : at + HEAD_SIZE] = result.T.astype(out_ref.dtype)


def attend(kv_list, info, q_side, seg_q, pre_q, seg_k, state, last):
    kv_count, head, columns = q_side.shape
    rows = seg_q.shape[1]
    counts = tuple(kv.shape[0] for kv in kv_list)
    first = state is None
    state_shapes = [
        jax.ShapeDtypeStruct((kv_count, 1, columns), jnp.float32),
        jax.ShapeDtypeStruct((kv_count, 1, columns), jnp.float32),
        jax.ShapeDtypeStruct((kv_count, head, columns), jnp.float32),
    ]
    if last:
        out_shape = jax.ShapeDtypeStruct((rows, kv_count * columns // rows * head), jnp.bfloat16)
        scratch = [pltpu.VMEM(s.shape, s.dtype) for s in state_shapes]
    else:
        out_shape, scratch = state_shapes, []
    vmem = pl.BlockSpec(memory_space=pltpu.VMEM)
    operands = [q_side, seg_q, pre_q, seg_k, *kv_list, *(() if first else state)]
    return pl.pallas_call(
        functools.partial(attend_kernel, first, last, counts),
        out_shape=out_shape,
        in_specs=[pl.BlockSpec(memory_space=pltpu.SMEM)] + [vmem] * len(operands),
        out_specs=vmem if last else [vmem] * 3,
        scratch_shapes=scratch,
        compiler_params=pltpu.CompilerParams(vmem_limit_bytes=40 * 1024 * 1024),
        cost_estimate=pl.CostEstimate(
            flops=4 * len(kv_list) * rows * columns * kv_count * head,
            bytes_accessed=4_000_000,
            transcendentals=rows * columns * kv_count,
        ),
        name="attend_last" if last else "attend_own",
    )(info, *operands)


def shards(
    hidden_in,
    queries,
    keys,
    values,
    segment_ids,
    prefix_ids,
    o_weight,
    post_gain,
    expert_ids,
    gates,
    w_gate,
    w_up,
    w_down,
):
    bf16, f32 = jnp.bfloat16, jnp.float32
    tok, model_width = hidden_in.shape
    n_blk, n_uly = lax.axis_size("blk"), lax.axis_size("uly")
    chips = n_uly // 2
    experts_all = n_blk * n_uly
    top_count = expert_ids.shape[1]
    heads_all = queries.shape[1] // HEAD_SIZE
    kv_count = keys.shape[1] // HEAD_SIZE
    group = heads_all // kv_count
    blk, uly = lax.axis_index("blk"), lax.axis_index("uly")
    core, chip = uly % 2, uly // 2
    me = blk * n_uly + uly

    order = chip_ring(chips)
    ring_pairs = [
        (2 * order[i] + c, 2 * order[(i + 1) % chips] + c) for i in range(chips) for c in range(2)
    ]
    swap_pairs = [(u, u ^ 1) for u in range(n_uly)]
    next_chip = functools.partial(lax.ppermute, axis_name="uly", perm=ring_pairs)
    other_core = functools.partial(lax.ppermute, axis_name="uly", perm=swap_pairs)

    def other_block(x, m):
        return lax.ppermute(x, "blk", [(b, b ^ m) for b in range(n_blk)])

    order_of = jnp.array(order, jnp.int32)
    place_of = jnp.array([order.index(z) for z in range(chips)], jnp.int32)
    place = place_of[chip]
    chip_at = [order_of[(place - k) % chips] for k in range(chips)]

    share = gates / jnp.sum(gates, axis=1, keepdims=True)
    share_t, ids_t = share.T, expert_ids.T
    share_hi = share_t.astype(bf16)
    share_lo = (share_t - share_hi.astype(f32)).astype(bf16)
    kv_width = 2 * kv_count * HEAD_SIZE
    small = jnp.concatenate(
        [
            ids_t.astype(bf16).reshape(-1),
            share_hi.reshape(-1),
            share_lo.reshape(-1),
            segment_ids.astype(bf16),
        ]
    )
    small = jnp.pad(small, (0, EXTRA_ROWS * kv_width - small.shape[0]))
    values_t = values.reshape(tok, kv_count, HEAD_SIZE).transpose(2, 1, 0)
    kv_own = jnp.concatenate([keys, values_t.reshape(HEAD_SIZE, kv_count * tok)], axis=1)
    message = jnp.concatenate([kv_own, small.reshape(EXTRA_ROWS, kv_width)], axis=0)

    steps = [message]
    for _ in range(chips - 1):
        steps.append(next_chip(steps[-1]))
    kv_mine = jnp.stack(steps)
    kv_near = other_core(kv_mine)
    kv_far = [other_block(kv_mine, m) for m in range(1, n_blk)]
    kv_far_near = [other_core(kv) for kv in kv_far]

    def smalls(kv):
        return kv[:, tok:, :].reshape(kv.shape[0], -1)

    small_mine, small_near = smalls(kv_mine), smalls(kv_near)
    seg_at = 3 * top_count * tok

    seg_q = segment_ids
    table = jnp.arange(prefix_ids.shape[0], dtype=jnp.int32)
    pre_q = jnp.sum(jnp.where(seg_q[:, None] == table[None, :], prefix_ids[None, :], 0), axis=1)
    q_side = (
        queries.reshape(tok, kv_count, group, HEAD_SIZE)
        .transpose(1, 3, 2, 0)
        .reshape(kv_count, HEAD_SIZE, group * tok)
    )

    def tile_info(segs, devices):
        segs = segs.astype(jnp.int32)
        low, high = segs[:, 0], segs[:, -1]
        own = (low <= seg_q[-1]) & (high >= seg_q[0])
        shared = jnp.any(
            (pre_q[None, :] >= low[:, None]) & (pre_q[None, :] <= high[:, None]), axis=1
        )
        needed = (devices <= me) & (own | shared)
        return jnp.concatenate([needed.astype(jnp.int32), devices * tok, me[None] * tok])

    seg_row = seg_q.astype(f32)[None, :]
    pre_row = pre_q.astype(f32)[None, :]

    def device_list(sources):
        return jnp.stack(
            [b * n_uly + 2 * chip_at[k] + c for b, c in sources for k in range(chips)]
        ).astype(jnp.int32)

    segs_own = jnp.concatenate([small_mine[:, seg_at:][:, :tok], small_near[:, seg_at:][:, :tok]])
    state = attend(
        [kv_mine, kv_near],
        tile_info(segs_own, device_list([(blk, core), (blk, 1 - core)])),
        q_side,
        seg_row,
        pre_row,
        segs_own.astype(f32)[:, None, :],
        None,
        False,
    )
    segs_far = jnp.concatenate(
        [smalls(kv)[:, seg_at:][:, :tok] for kv in kv_far + kv_far_near]
    )
    far_sources = [(blk ^ m, core) for m in range(1, n_blk)] + [
        (blk ^ m, 1 - core) for m in range(1, n_blk)
    ]
    attended = attend(
        kv_far + kv_far_near,
        tile_info(segs_far, device_list(far_sources)),
        q_side,
        seg_row,
        pre_row,
        segs_far.astype(f32)[:, None, :],
        state,
        True,
    )

    mixed = hidden_in.astype(f32) + jnp.dot(attended, o_weight, preferred_element_type=f32)
    normed = (
        mixed * lax.rsqrt(jnp.mean(mixed * mixed, axis=1, keepdims=True) + 1e-06) * post_gain
    ).astype(bf16)

    capacity = max(2, 9 * tok * top_count // (8 * experts_all))
    count = top_count * tok
    expert_of = jnp.stack([(blk ^ m) * n_uly + uly for m in range(n_blk)]).astype(f32)

    def slots(small_rows):
        ids = small_rows[:, :count].reshape(chips, 1, top_count, tok).astype(f32)
        hi = small_rows[:, count : 2 * count].reshape(chips, 1, top_count, tok).astype(f32)
        lo = small_rows[:, 2 * count : 3 * count].reshape(chips, 1, top_count, tok).astype(f32)
        named = ids == expert_of[None, :, None, None]
        hit = jnp.any(named, axis=2)
        hi = jnp.sum(jnp.where(named, hi, 0.0), axis=2)
        lo = jnp.sum(jnp.where(named, lo, 0.0), axis=2)
        before = jnp.triu(jnp.ones((tok, tok), bf16), 1)
        rank = jnp.dot(
            hit.astype(bf16).reshape(chips * n_blk, tok), before, preferred_element_type=f32
        ).reshape(chips, n_blk, tok)
        return jnp.where(hit, rank, -1e6), hi, lo

    rank_a, hi_a, lo_a = slots(small_mine)
    rank_b, hi_b, lo_b = slots(small_near)
    rank = jnp.concatenate([rank_a, rank_b + capacity], axis=2).astype(jnp.int32)
    share_hi = jnp.concatenate([hi_a, hi_b], axis=2)
    share_lo = jnp.concatenate([lo_a, lo_b], axis=2)
    pair_rows = 2 * capacity
    slot_axis = jnp.arange(pair_rows, dtype=jnp.int32)
    chosen = rank[:, :, None, :] == slot_axis[None, None, :, None]

    rows_now = normed
    chunk_rows = []
    for k in range(chips):
        chunk_rows.append(rows_now)
        if k < chips - 1:
            rows_now = next_chip(rows_now)
    answers = []
    for k in range(chips):
        pair = jnp.concatenate([chunk_rows[k], other_core(chunk_rows[k])], axis=0)
        inbox = []
        for m in range(n_blk):
            picked = jnp.dot(
                chosen[k, m].astype(bf16), pair, preferred_element_type=f32
            ).astype(bf16)
            inbox.append(other_block(picked, m) if m else picked)
        rows = jnp.concatenate(inbox, axis=0)
        gate_proj = jnp.dot(rows, w_gate[0], preferred_element_type=f32)
        up_proj = jnp.dot(rows, w_up[0], preferred_element_type=f32)
        hidden_act = (jax.nn.silu(gate_proj) * up_proj).astype(bf16)
        answer = jnp.dot(hidden_act, w_down[0], preferred_element_type=f32).astype(bf16)
        answers.append(answer)

    partial = [None] * chips
    for k in [*range(1, chips), 0]:
        parts = [answers[k][m * pair_rows : (m + 1) * pair_rows] for m in range(n_blk)]
        back = jnp.concatenate([other_block(p, m) if m else p for m, p in enumerate(parts)], axis=0)
        spread = jnp.concatenate(
            [
                jnp.where(chosen[k], share[k][:, None, :], 0.0)
                .astype(bf16)
                .reshape(n_blk * pair_rows, 2 * tok)
                for share in (share_hi, share_lo)
            ],
            axis=0,
        )
        sums = lax.dot_general(
            spread,
            jnp.concatenate([back, back], axis=0),
            (((0,), (0,)), ((), ())),
            preferred_element_type=f32,
        )
        partial[k] = sums[:tok] + other_core(sums[tok:].astype(bf16)).astype(f32)
    total = None
    for k in range(1, chips):
        now = partial[k] if total is None else total.astype(f32) + partial[k]
        total = next_chip(now.astype(bf16))
    routed = partial[0] if total is None else partial[0] + total.astype(f32)
    return (mixed + routed).astype(bf16)


def solution(mesh):
    rows = P(("blk", "uly"), None)
    in_specs = (
        rows,
        rows,
        rows,
        rows,
        P(("blk", "uly")),
        P(),
        P(),
        P(),
        rows,
        rows,
        P(("blk", "uly"), None, None),
        P(("blk", "uly"), None, None),
        P(("blk", "uly"), None, None),
    )
    return jax.shard_map(shards, mesh=mesh, in_specs=in_specs, out_specs=rows, check_vma=False)
```

time: 612 us -> 279 us (0.46)
  blocking collectives: 205 us -> 0 us
  matrix products: 95.3 us -> 47.2 us
  local copies, waits for them, and re-layouts: 104 us -> 57.4 us
  starting transfers between devices: 12.5 us -> 54.3 us
  other arithmetic: 56.4 us -> 18.5 us
  waiting for transfers between devices: 123 us -> 91.1 us
  between operations: 13.7 us -> 7.44 us
    all_to_all x3 -> x0, blocking collectives: 161 us -> none  [the longest x1 121 us: shards(): lax.all_to_all(outbox.reshape(experts_all, capacity, model_width), ('blk'...]
    all_to_all x3 -> x0, waiting for transfers between devices: 123 us -> none  [the longest x1 117 us: shards(): lax.all_to_all(expert_answer.reshape(sources, item_count, model_width), (...]
    ppermute x0 -> x48, waiting for transfers between devices: none -> 91.1 us  [the longest x27 69.2 us: other_block(): return lax.ppermute(x, 'blk', [(b, b ^ m) for b in range(n_blk)])]
    ppermute x0 -> x48, starting transfers between devices: none -> 54.3 us  [the longest x27 38.2 us: other_block(): return lax.ppermute(x, 'blk', [(b, b ^ m) for b in range(n_blk)])]
    dot_general x20 -> x31, matrix products: 95.3 us -> 47.2 us  [the longest x4 23.4 us: shards(): jnp.dot(hidden_act, w_down[0], preferred_element_type=f32).astype(bf16)]
    all_gather x1 -> x0, blocking collectives: 43.8 us -> none  [shards(): lax.all_gather(segment_ids, ('blk', 'uly'), axis=0, tiled=True)]
    dynamic_slice x33 -> x2, local copies, waits for them, and re-layouts: 35.9 us -> 2.77 us  [the longest x1 1.47 us: shards(): chip_at = [order_of[(place - k) % chips] for k in range(chips)]]
    reduce_sum x11 -> x2, other arithmetic: 32.9 us -> 0.91 us  [the longest x1 0.76 us: shards(): jnp.sum(jnp.where(seg_q[:, None] == table[None, :], prefix_ids[None, :],...]
  transfers between devices with their start and end apart: 5 -> 48, of which waited for: 2 -> 20; matrix products, arithmetic and copies ran while one was open for 4% -> 31% of each run, Pallas kernels for 0% -> 0%
where the time goes in v1:
time: 279 us; the launch traced here: 278 us
  waiting for transfers between devices  91.1 us (33%)
  local copies, waits for them, and re-layouts  57.4 us (21%)
  starting transfers between devices  54.3 us (19%)
  matrix products  47.2 us (17%)
  other arithmetic  18.5 us (7%)
  between operations  7.44 us (3%)
    ppermute x27, waiting for transfers between devices, other_block(): return lax.ppermute(x, 'blk', [(b, b ^ m) for b in range(n_blk)])  69.2 us
    ppermute x27, starting transfers between devices, other_block(): return lax.ppermute(x, 'blk', [(b, b ^ m) for b in range(n_blk)])  38.2 us
    unnamed x166, local copies, waits for them, and re-layouts  35.7 us
    dot_general x4, matrix products, shards(): jnp.dot(hidden_act, w_down[0], preferred_element_type=f32).astype(bf16)  23.4 us
    ppermute x3, waiting for transfers between devices, shards(): total = next_chip(now.astype(bf16))  13.5 us
    dot_general x4, matrix products, shards(): up_proj = jnp.dot(rows, w_up[0], preferred_element_type=f32)  8.13 us
    ppermute x3, starting transfers between devices, shards(): steps.append(next_chip(steps[-1]))  7.36 us
    slice x4, local copies, waits for them, and re-layouts, shards(): answers[k][m * pair_rows:(m + 1) * pair_rows]  6.36 us
  transfers between devices with their start and end apart: 48, of which 20 were waited for; matrix products, arithmetic and copies ran while one was open for 31% of the time, Pallas kernels for 0%

profile of v1, /device:TPU:0, one launch (start us, length us, event | category | flops | bytes accessed | tf_op | source)
XLA Modules:
  0.0 278.5 jit_solution(14318687587506535914)
XLA Ops:
  6.4 3.0 %collective-permute-start = (bf16[136,512]{1,0:T(8,128)(2,1)}, bf16[136,512]{1,0:T(8,128)(2,1)S(1)}, u32[]{:S(2)}, u32[]{:S(2)}) collective-permute-start(bf16[136,512]{1,0:T(8,128)(2,1)} %get-tuple-element.44), channel_id=1, source_target_pairs={{0,2},{1,3},{2,6},{3,7},{6,4},{7,5},{4,0},{5,1},{8,10},{9,11},{10,... | collective-permute-start | bytes 417800 | tf_op jit(solution)/shard_map/ppermute | solution.py:198
  19.4 2.6 collective-permute-start.1
  22.1 3.5 %collective-permute-done.1 = bf16[136,512]{1,0:T(8,128)(2,1)} collective-permute-done((bf16[136,512]{1,0:T(8,128)(2,1)S(1)}, bf16[136,512]{1,0:T(8,128)(2,1)}, u32[]{:S(2)}, u32[]{:S(2)}) %collective-permute-start.1) | collective-permute-done | bytes 139296 | tf_op jit(solution)/shard_map/ppermute | solution.py:198
  39.2 14.3 %collective-permute-done.5.refs_2_ = bf16[4,136,512]{2,1,0:T(8,128)(2,1)S(1)} collective-permute-done((bf16[4,136,512]{2,1,0:T(8,128)(2,1)S(1)}, bf16[4,136,512]{2,1,0:T(8,128)(2,1)S(1)}, u32[]{:S(2)}, u32[]{:S(2)}) %collective-permute-start.5) | collective-permute-done | bytes 557088 | tf_op jit(solution)/shard_map/ppermute | solution.py:171
  53.5 10.2 %collective-permute-done.3.refs_0_ = bf16[4,136,512]{2,1,0:T(8,128)(2,1)S(1)} collective-permute-done((bf16[4,136,512]{2,1,0:T(8,128)(2,1)S(1)}, bf16[4,136,512]{2,1,0:T(8,128)(2,1)S(1)}, u32[]{:S(2)}, u32[]{:S(2)}) %collective-permute-start.3) | collective-permute-done | bytes 557088 | tf_op jit(solution)/shard_map/ppermute | solution.py:171
  83.3 4.8 %multiply_reduce_fusion = (f32[128]{0:T(128)S(1)}, f32[128,2048]{1,0:T(8,128)S(1)}) fusion(bf16[128,2048]{1,0:T(8,128)(2,1)S(1)} %attend_last.1, bf16[2048,2048]{1,0:T(8,128)(2,1)} %param.21, bf16[128,2048]{1,0:T(8,128)(2,1)S(1)} %copy-done.36), kind=kOutput, calls=%fused_computation.71 | convolution fusion | flops 1074790272 | bytes 10486272 | tf_op jit(solution)/shard_map/dot_general | solution.py:265
  94.5 4.7 %collective-permute-start.11 = (bf16[72,2048]{1,0:T(8,128)(2,1)S(1)}, bf16[72,2048]{1,0:T(8,128)(2,1)S(1)}, u32[]{:S(2)}, u32[]{:S(2)}) collective-permute-start(bf16[72,2048]{1,0:T(8,128)(2,1)S(1)} %convolution_convert_fusion.14), channel_id=1, source_target_pairs={{0,8},{8,0},{16,24},{24,16},{1,9},{9,1},{17,25},{25,17},{2,10},{10... | collective-permute-start | bytes 884744 | tf_op jit(solution)/shard_map/ppermute | solution.py:171
  99.5 3.4 %collective-permute-start.12 = (bf16[72,2048]{1,0:T(8,128)(2,1)S(1)}, bf16[72,2048]{1,0:T(8,128)(2,1)S(1)}, u32[]{:S(2)}, u32[]{:S(2)}) collective-permute-start(bf16[72,2048]{1,0:T(8,128)(2,1)S(1)} %convolution_convert_fusion.13), channel_id=1, source_target_pairs={{0,16},{8,24},{16,0},{24,8},{1,17},{9,25},{17,1},{25,9},{2,18},{10... | collective-permute-start | bytes 884744 | tf_op jit(solution)/shard_map/ppermute | solution.py:171
  103.3 4.3 %collective-permute-done.18 = bf16[128,2048]{1,0:T(8,128)(2,1)} collective-permute-done((bf16[128,2048]{1,0:T(8,128)(2,1)S(1)}, bf16[128,2048]{1,0:T(8,128)(2,1)}, u32[]{:S(2)}, u32[]{:S(2)}) %collective-permute-start.18) | collective-permute-done | bytes 524320 | tf_op jit(solution)/shard_map/ppermute | solution.py:302
  110.5 5.4 %collective-permute-done.12 = bf16[72,2048]{1,0:T(8,128)(2,1)S(1)} collective-permute-done((bf16[72,2048]{1,0:T(8,128)(2,1)S(1)}, bf16[72,2048]{1,0:T(8,128)(2,1)S(1)}, u32[]{:S(2)}, u32[]{:S(2)}) %collective-permute-start.12) | collective-permute-done | bytes 294944 | tf_op jit(solution)/shard_map/ppermute | solution.py:171
  119.3 5.9 %fusion.24 = bf16[288,2048]{1,0:T(8,128)(2,1)} fusion(bf16[1,768,2048]{2,1,0:T(8,128)(2,1)S(1)} %copy-done, f32[288,768]{1,0:T(8,128)} %fusion.14, bf16[1,2048,768]{2,1,0:T(8,128)(2,1)} %param.25, bf16[72,2048]{1,0:T(8,128)(2,1)} %copy-done.56, bf16[72,2048]{1,0:T(8,128)(2,1)} %copy-done.55, bf16[72,2048]{1,0:T(8,128)(2,1)} %copy-done.54, ...), kind=kOutput, calls=%fused_computation.24 | convolution fusion | flops 1818574848 | bytes 9535488 | tf_op jit(solution)/shard_map/dot_general | solution.py:316
  140.0 3.6 %collective-permute-done.15 = bf16[72,2048]{1,0:T(8,128)(2,1)S(1)} collective-permute-done((bf16[72,2048]{1,0:T(8,128)(2,1)S(1)}, bf16[72,2048]{1,0:T(8,128)(2,1)S(1)}, u32[]{:S(2)}, u32[]{:S(2)}) %collective-permute-start.15) | collective-permute-done | bytes 294944 | tf_op jit(solution)/shard_map/ppermute | solution.py:171
  150.0 6.1 %collective-permute-done.21 = bf16[72,2048]{1,0:T(8,128)(2,1)S(1)} collective-permute-done((bf16[72,2048]{1,0:T(8,128)(2,1)S(1)}, bf16[72,2048]{1,0:T(8,128)(2,1)S(1)}, u32[]{:S(2)}, u32[]{:S(2)}) %collective-permute-start.21) | collective-permute-done | bytes 294944 | tf_op jit(solution)/shard_map/ppermute | solution.py:171
  159.5 5.9 %fusion.27 = bf16[288,2048]{1,0:T(8,128)(2,1)} fusion(bf16[1,768,2048]{2,1,0:T(8,128)(2,1)S(1)} %copy-done, f32[288,768]{1,0:T(8,128)} %fusion.12, bf16[1,2048,768]{2,1,0:T(8,128)(2,1)} %param.25, bf16[72,2048]{1,0:T(8,128)(2,1)} %copy-done.53, bf16[72,2048]{1,0:T(8,128)(2,1)} %copy-done.52, bf16[72,2048]{1,0:T(8,128)(2,1)} %copy-done.49, ...), kind=kOutput, calls=%fused_computation.25 | convolution fusion | flops 1818574848 | bytes 9535488 | tf_op jit(solution)/shard_map/dot_general | solution.py:316
  178.3 4.2 %collective-permute-done.24 = bf16[72,2048]{1,0:T(8,128)(2,1)S(1)} collective-permute-done((bf16[72,2048]{1,0:T(8,128)(2,1)S(1)}, bf16[72,2048]{1,0:T(8,128)(2,1)S(1)}, u32[]{:S(2)}, u32[]{:S(2)}) %collective-permute-start.24) | collective-permute-done | bytes 294944 | tf_op jit(solution)/shard_map/ppermute | solution.py:171
  189.5 3.8 %collective-permute-done.31 = bf16[72,2048]{1,0:T(8,128)(2,1)S(1)} collective-permute-done((bf16[72,2048]{1,0:T(8,128)(2,1)S(1)}, bf16[72,2048]{1,0:T(8,128)(2,1)S(1)}, u32[]{:S(2)}, u32[]{:S(2)}) %collective-permute-start.31) | collective-permute-done | bytes 294944 | tf_op jit(solution)/shard_map/ppermute | solution.py:171
  198.0 5.9 %fusion.30 = bf16[288,2048]{1,0:T(8,128)(2,1)} fusion(bf16[1,768,2048]{2,1,0:T(8,128)(2,1)S(1)} %copy-done, f32[288,768]{1,0:T(8,128)} %fusion.10, bf16[1,2048,768]{2,1,0:T(8,128)(2,1)} %param.25, bf16[72,2048]{1,0:T(8,128)(2,1)} %copy-done.50, bf16[72,2048]{1,0:T(8,128)(2,1)} %copy-done.48, bf16[72,2048]{1,0:T(8,128)(2,1)} %copy-done.47, ...), kind=kOutput, calls=%fused_computation.26 | convolution fusion | flops 1818574848 | bytes 9535488 | tf_op jit(solution)/shard_map/dot_general | solution.py:316
  217.7 5.1 %collective-permute-done.34 = bf16[72,2048]{1,0:T(8,128)(2,1)S(1)} collective-permute-done((bf16[72,2048]{1,0:T(8,128)(2,1)S(1)}, bf16[72,2048]{1,0:T(8,128)(2,1)S(1)}, u32[]{:S(2)}, u32[]{:S(2)}) %collective-permute-start.34) | collective-permute-done | bytes 294944 | tf_op jit(solution)/shard_map/ppermute | solution.py:171
  228.3 3.3 %collective-permute-done.41 = bf16[72,2048]{1,0:T(8,128)(2,1)S(1)} collective-permute-done((bf16[72,2048]{1,0:T(8,128)(2,1)S(1)}, bf16[72,2048]{1,0:T(8,128)(2,1)S(1)}, u32[]{:S(2)}, u32[]{:S(2)}) %collective-permute-start.41) | collective-permute-done | bytes 294944 | tf_op jit(solution)/shard_map/ppermute | solution.py:171
  234.4 5.8 %fusion.33 = bf16[288,2048]{1,0:T(8,128)(2,1)} fusion(bf16[1,768,2048]{2,1,0:T(8,128)(2,1)S(1)} %copy-done, f32[288,768]{1,0:T(8,128)} %fusion.8, bf16[1,2048,768]{2,1,0:T(8,128)(2,1)} %param.25, bf16[72,2048]{1,0:T(8,128)(2,1)} %copy-done.51, bf16[72,2048]{1,0:T(8,128)(2,1)S(1)} %collective-permute-done.41, bf16[72,2048]{1,0:T(8,128)(2,1)} %copy-done.46, ...), kind=kOutput, calls=%fused_computation.27 | convolution fusion | flops 1818574848 | bytes 9535488 | tf_op jit(solution)/shard_map/dot_general | solution.py:316
  247.9 3.8 %collective-permute-done.43 = bf16[72,2048]{1,0:T(8,128)(2,1)S(1)} collective-permute-done((bf16[72,2048]{1,0:T(8,128)(2,1)S(1)}, bf16[72,2048]{1,0:T(8,128)(2,1)S(1)}, u32[]{:S(2)}, u32[]{:S(2)}) %collective-permute-start.43) | collective-permute-done | bytes 294944 | tf_op jit(solution)/shard_map/ppermute | solution.py:171
  251.7 4.3 %collective-permute-done.44 = bf16[72,2048]{1,0:T(8,128)(2,1)S(1)} collective-permute-done((bf16[72,2048]{1,0:T(8,128)(2,1)S(1)}, bf16[72,2048]{1,0:T(8,128)(2,1)S(1)}, u32[]{:S(2)}, u32[]{:S(2)}) %collective-permute-start.44) | collective-permute-done | bytes 294944 | tf_op jit(solution)/shard_map/ppermute | solution.py:171
  259.1 2.7 fusion.65
  263.9 13.5 %collective-permute-done.47 = bf16[128,2048]{1,0:T(8,128)(2,1)S(1)} collective-permute-done((bf16[128,2048]{1,0:T(8,128)(2,1)S(1)}, bf16[128,2048]{1,0:T(8,128)(2,1)S(1)}, u32[]{:S(2)}, u32[]{:S(2)}) %collective-permute-start.47) | collective-permute-done | bytes 524320 | tf_op jit(solution)/shard_map/ppermute | solution.py:342
  (351 shorter events, 140.8 us)
Async XLA Ops:
  35.5 28.5 %collective-permute-start.4 = (bf16[4,136,512]{2,1,0:T(8,128)(2,1)S(1)}, bf16[4,136,512]{2,1,0:T(8,128)(2,1)S(1)}, u32[]{:S(2)}, u32[]{:S(2)}) collective-permute-start(bf16[4,136,512]{2,1,0:T(8,128)(2,1)S(1)} %pad_maximum_fusion.5.refs_0_), channel_id=1, source_target_pairs={{0,16},{8,24},{16,0},{24,8},{1,17},{9,25},{17,1},{25,9},{2,18},{10... | collective-permute-start | bytes 1671176 | tf_op jit(solution)/shard_map/ppermute | solution.py:171
  37.1 16.4 %collective-permute-start.5 = (bf16[4,136,512]{2,1,0:T(8,128)(2,1)S(1)}, bf16[4,136,512]{2,1,0:T(8,128)(2,1)S(1)}, u32[]{:S(2)}, u32[]{:S(2)}) collective-permute-start(bf16[4,136,512]{2,1,0:T(8,128)(2,1)S(1)} %pad_maximum_fusion.5.refs_0_), channel_id=1, source_target_pairs={{0,24},{8,16},{16,8},{24,0},{1,25},{9,17},{17,9},{25,1},{2,26},{10... | collective-permute-start | bytes 1671176 | tf_op jit(solution)/shard_map/ppermute | solution.py:171
  38.5 25.2 %collective-permute-start.3 = (bf16[4,136,512]{2,1,0:T(8,128)(2,1)S(1)}, bf16[4,136,512]{2,1,0:T(8,128)(2,1)S(1)}, u32[]{:S(2)}, u32[]{:S(2)}) collective-permute-start(bf16[4,136,512]{2,1,0:T(8,128)(2,1)S(1)} %pad_maximum_fusion.5.refs_0_), channel_id=1, source_target_pairs={{0,8},{8,0},{16,24},{24,16},{1,9},{9,1},{17,25},{25,17},{2,10},{10... | collective-permute-start | bytes 1671176 | tf_op jit(solution)/shard_map/ppermute | solution.py:171
  94.5 16.0 %collective-permute-start.11 = (bf16[72,2048]{1,0:T(8,128)(2,1)S(1)}, bf16[72,2048]{1,0:T(8,128)(2,1)S(1)}, u32[]{:S(2)}, u32[]{:S(2)}) collective-permute-start(bf16[72,2048]{1,0:T(8,128)(2,1)S(1)} %convolution_convert_fusion.14), channel_id=1, source_target_pairs={{0,8},{8,0},{16,24},{24,16},{1,9},{9,1},{17,25},{25,17},{2,10},{10... | collective-permute-start | bytes 884744 | tf_op jit(solution)/shard_map/ppermute | solution.py:171
  99.5 16.4 %collective-permute-start.12 = (bf16[72,2048]{1,0:T(8,128)(2,1)S(1)}, bf16[72,2048]{1,0:T(8,128)(2,1)S(1)}, u32[]{:S(2)}, u32[]{:S(2)}) collective-permute-start(bf16[72,2048]{1,0:T(8,128)(2,1)S(1)} %convolution_convert_fusion.13), channel_id=1, source_target_pairs={{0,16},{8,24},{16,0},{24,8},{1,17},{9,25},{17,1},{25,9},{2,18},{10... | collective-permute-start | bytes 884744 | tf_op jit(solution)/shard_map/ppermute | solution.py:171
  107.6 23.2 %collective-permute-start.19 = (bf16[128,2048]{1,0:T(8,128)(2,1)}, bf16[128,2048]{1,0:T(8,128)(2,1)}, u32[]{:S(2)}, u32[]{:S(2)}) collective-permute-start(bf16[128,2048]{1,0:T(8,128)(2,1)} %collective-permute-done.18), channel_id=1, source_target_pairs={{0,1},{1,0},{2,3},{3,2},{4,5},{5,4},{6,7},{7,6},{8,9},{9,8},{10,11... | collective-permute-start | bytes 1572872 | tf_op jit(solution)/shard_map/ppermute | solution.py:305
  107.6 26.2 %collective-permute-start.28 = (bf16[128,2048]{1,0:T(8,128)(2,1)}, bf16[128,2048]{1,0:T(8,128)(2,1)}, u32[]{:S(2)}, u32[]{:S(2)}) collective-permute-start(bf16[128,2048]{1,0:T(8,128)(2,1)} %collective-permute-done.18), channel_id=1, source_target_pairs={{0,2},{1,3},{2,6},{3,7},{6,4},{7,5},{4,0},{5,1},{8,10},{9,11},{10,... | collective-permute-start | bytes 1572872 | tf_op jit(solution)/shard_map/ppermute | solution.py:302
  127.7 16.0 %collective-permute-start.15 = (bf16[72,2048]{1,0:T(8,128)(2,1)S(1)}, bf16[72,2048]{1,0:T(8,128)(2,1)S(1)}, u32[]{:S(2)}, u32[]{:S(2)}) collective-permute-start(bf16[72,2048]{1,0:T(8,128)(2,1)S(1)} %get-tuple-element.37), channel_id=1, source_target_pairs={{0,16},{8,24},{16,0},{24,8},{1,17},{9,25},{17,1},{25,9},{2,18},{10... | collective-permute-start | bytes 884744 | tf_op jit(solution)/shard_map/ppermute | solution.py:171
  133.2 16.8 %collective-permute-start.20 = (bf16[72,2048]{1,0:T(8,128)(2,1)S(1)}, bf16[72,2048]{1,0:T(8,128)(2,1)S(1)}, u32[]{:S(2)}, u32[]{:S(2)}) collective-permute-start(bf16[72,2048]{1,0:T(8,128)(2,1)S(1)} %convolution_convert_fusion.10), channel_id=1, source_target_pairs={{0,8},{8,0},{16,24},{24,16},{1,9},{9,1},{17,25},{25,17},{2,10},{10... | collective-permute-start | bytes 884744 | tf_op jit(solution)/shard_map/ppermute | solution.py:171
  133.9 22.2 %collective-permute-start.21 = (bf16[72,2048]{1,0:T(8,128)(2,1)S(1)}, bf16[72,2048]{1,0:T(8,128)(2,1)S(1)}, u32[]{:S(2)}, u32[]{:S(2)}) collective-permute-start(bf16[72,2048]{1,0:T(8,128)(2,1)S(1)} %convolution_convert_fusion.9), channel_id=1, source_target_pairs={{0,16},{8,24},{16,0},{24,8},{1,17},{9,25},{17,1},{25,9},{2,18},{10... | collective-permute-start | bytes 884744 | tf_op jit(solution)/shard_map/ppermute | solution.py:171
  137.8 18.3 %collective-permute-start.22 = (bf16[72,2048]{1,0:T(8,128)(2,1)S(1)}, bf16[72,2048]{1,0:T(8,128)(2,1)S(1)}, u32[]{:S(2)}, u32[]{:S(2)}) collective-permute-start(bf16[72,2048]{1,0:T(8,128)(2,1)S(1)} %convolution_convert_fusion.8), channel_id=1, source_target_pairs={{0,24},{8,16},{16,8},{24,0},{1,25},{9,17},{17,9},{25,1},{2,26},{10... | collective-permute-start | bytes 884744 | tf_op jit(solution)/shard_map/ppermute | solution.py:171
  143.7 26.7 %collective-permute-start.29 = (bf16[128,2048]{1,0:T(8,128)(2,1)}, bf16[128,2048]{1,0:T(8,128)(2,1)}, u32[]{:S(2)}, u32[]{:S(2)}) collective-permute-start(bf16[128,2048]{1,0:T(8,128)(2,1)} %collective-permute-done.28), channel_id=1, source_target_pairs={{0,1},{1,0},{2,3},{3,2},{4,5},{5,4},{6,7},{7,6},{8,9},{9,8},{10,11... | collective-permute-start | bytes 1572872 | tf_op jit(solution)/shard_map/ppermute | solution.py:305
  144.8 28.8 %collective-permute-start.38 = (bf16[128,2048]{1,0:T(8,128)(2,1)}, bf16[128,2048]{1,0:T(8,128)(2,1)}, u32[]{:S(2)}, u32[]{:S(2)}) collective-permute-start(bf16[128,2048]{1,0:T(8,128)(2,1)} %collective-permute-done.28), channel_id=1, source_target_pairs={{0,2},{1,3},{2,6},{3,7},{6,4},{7,5},{4,0},{5,1},{8,10},{9,11},{10,... | collective-permute-start | bytes 1572872 | tf_op jit(solution)/shard_map/ppermute | solution.py:302
  172.7 16.8 %collective-permute-start.30 = (bf16[72,2048]{1,0:T(8,128)(2,1)S(1)}, bf16[72,2048]{1,0:T(8,128)(2,1)S(1)}, u32[]{:S(2)}, u32[]{:S(2)}) collective-permute-start(bf16[72,2048]{1,0:T(8,128)(2,1)S(1)} %convolution_convert_fusion.6), channel_id=1, source_target_pairs={{0,8},{8,0},{16,24},{24,16},{1,9},{9,1},{17,25},{25,17},{2,10},{10... | collective-permute-start | bytes 884744 | tf_op jit(solution)/shard_map/ppermute | solution.py:171
  173.6 19.7 %collective-permute-start.31 = (bf16[72,2048]{1,0:T(8,128)(2,1)S(1)}, bf16[72,2048]{1,0:T(8,128)(2,1)S(1)}, u32[]{:S(2)}, u32[]{:S(2)}) collective-permute-start(bf16[72,2048]{1,0:T(8,128)(2,1)S(1)} %convolution_convert_fusion.5), channel_id=1, source_target_pairs={{0,16},{8,24},{16,0},{24,8},{1,17},{9,25},{17,1},{25,9},{2,18},{10... | collective-permute-start | bytes 884744 | tf_op jit(solution)/shard_map/ppermute | solution.py:171
  176.8 18.4 %collective-permute-start.32 = (bf16[72,2048]{1,0:T(8,128)(2,1)S(1)}, bf16[72,2048]{1,0:T(8,128)(2,1)S(1)}, u32[]{:S(2)}, u32[]{:S(2)}) collective-permute-start(bf16[72,2048]{1,0:T(8,128)(2,1)S(1)} %convolution_convert_fusion.4), channel_id=1, source_target_pairs={{0,24},{8,16},{16,8},{24,0},{1,25},{9,17},{17,9},{25,1},{2,26},{10... | collective-permute-start | bytes 884744 | tf_op jit(solution)/shard_map/ppermute | solution.py:171
  182.5 26.3 %collective-permute-start.39 = (bf16[128,2048]{1,0:T(8,128)(2,1)}, bf16[128,2048]{1,0:T(8,128)(2,1)}, u32[]{:S(2)}, u32[]{:S(2)}) collective-permute-start(bf16[128,2048]{1,0:T(8,128)(2,1)} %collective-permute-done.38), channel_id=1, source_target_pairs={{0,1},{1,0},{2,3},{3,2},{4,5},{5,4},{6,7},{7,6},{8,9},{9,8},{10,11... | collective-permute-start | bytes 1572872 | tf_op jit(solution)/shard_map/ppermute | solution.py:305
  188.7 23.7 %collective-permute-start.26 = (bf16[128,2048]{1,0:T(8,128)(2,1)}, bf16[128,2048]{1,0:T(8,128)(2,1)}, u32[]{:S(2)}, u32[]{:S(2)}) collective-permute-start(bf16[128,2048]{1,0:T(8,128)(2,1)} %slice.566), channel_id=1, source_target_pairs={{0,1},{1,0},{2,3},{3,2},{4,5},{5,4},{6,7},{7,6},{8,9},{9,8},{10,11... | collective-permute-start | bytes 1572872 | tf_op jit(solution)/shard_map/ppermute | solution.py:338
  206.5 16.3 %collective-permute-start.34 = (bf16[72,2048]{1,0:T(8,128)(2,1)S(1)}, bf16[72,2048]{1,0:T(8,128)(2,1)S(1)}, u32[]{:S(2)}, u32[]{:S(2)}) collective-permute-start(bf16[72,2048]{1,0:T(8,128)(2,1)S(1)} %get-tuple-element.29), channel_id=1, source_target_pairs={{0,16},{8,24},{16,0},{24,8},{1,17},{9,25},{17,1},{25,9},{2,18},{10... | collective-permute-start | bytes 884744 | tf_op jit(solution)/shard_map/ppermute | solution.py:171
  208.3 15.7 %collective-permute-start.35 = (bf16[72,2048]{1,0:T(8,128)(2,1)S(1)}, bf16[72,2048]{1,0:T(8,128)(2,1)S(1)}, u32[]{:S(2)}, u32[]{:S(2)}) collective-permute-start(bf16[72,2048]{1,0:T(8,128)(2,1)S(1)} %get-tuple-element.27), channel_id=1, source_target_pairs={{0,24},{8,16},{16,8},{24,0},{1,25},{9,17},{17,9},{25,1},{2,26},{10... | collective-permute-start | bytes 884744 | tf_op jit(solution)/shard_map/ppermute | solution.py:171
  210.5 17.8 %collective-permute-start.40 = (bf16[72,2048]{1,0:T(8,128)(2,1)S(1)}, bf16[72,2048]{1,0:T(8,128)(2,1)S(1)}, u32[]{:S(2)}, u32[]{:S(2)}) collective-permute-start(bf16[72,2048]{1,0:T(8,128)(2,1)S(1)} %convolution_convert_fusion.2), channel_id=1, source_target_pairs={{0,8},{8,0},{16,24},{24,16},{1,9},{9,1},{17,25},{25,17},{2,10},{10... | collective-permute-start | bytes 884744 | tf_op jit(solution)/shard_map/ppermute | solution.py:171
  212.4 19.2 %collective-permute-start.41 = (bf16[72,2048]{1,0:T(8,128)(2,1)S(1)}, bf16[72,2048]{1,0:T(8,128)(2,1)S(1)}, u32[]{:S(2)}, u32[]{:S(2)}) collective-permute-start(bf16[72,2048]{1,0:T(8,128)(2,1)S(1)} %convolution_convert_fusion.1), channel_id=1, source_target_pairs={{0,16},{8,24},{16,0},{24,8},{1,17},{9,25},{17,1},{25,9},{2,18},{10... | collective-permute-start | bytes 884744 | tf_op jit(solution)/shard_map/ppermute | solution.py:171
  222.8 22.5 %collective-permute-start.27 = (bf16[128,2048]{1,0:T(8,128)(2,1)}, bf16[128,2048]{1,0:T(8,128)(2,1)}, u32[]{:S(2)}, u32[]{:S(2)}) collective-permute-start(bf16[128,2048]{1,0:T(8,128)(2,1)} %fusion.41), channel_id=1, source_target_pairs={{0,2},{1,3},{2,6},{3,7},{6,4},{7,5},{4,0},{5,1},{8,10},{9,11},{10,... | collective-permute-start | bytes 1572872 | tf_op jit(solution)/shard_map/ppermute | solution.py:342
  228.3 17.0 %collective-permute-start.36 = (bf16[128,2048]{1,0:T(8,128)(2,1)}, bf16[128,2048]{1,0:T(8,128)(2,1)}, u32[]{:S(2)}, u32[]{:S(2)}) collective-permute-start(bf16[128,2048]{1,0:T(8,128)(2,1)} %slice.565), channel_id=1, source_target_pairs={{0,1},{1,0},{2,3},{3,2},{4,5},{5,4},{6,7},{7,6},{8,9},{9,8},{10,11... | collective-permute-start | bytes 1572872 | tf_op jit(solution)/shard_map/ppermute | solution.py:338
  (82 other events, 748.0 us)

commit v2 on v0

v2 whole, which is shorter than its diff:
```python
import functools
import math

import jax
import jax.numpy as jnp
from jax import lax
from jax.experimental import pallas as pl
from jax.experimental.pallas import tpu as pltpu
from jax.sharding import PartitionSpec as P

HEAD_SIZE = 128
FLOOR = -1e20
HIDDEN = -1e30
BF16, F32 = jnp.bfloat16, jnp.float32


def chip_ring(count):
    return list(range(0, 1)) + list(range(1, count, 2)) + list(range(2, count, 2))[::-1]


def call(kernel, name, out_shape, operands, scalars=(), scratch=(), unused=(), cost=None):
    vmem = pl.BlockSpec(memory_space=pltpu.VMEM)
    several = isinstance(out_shape, (list, tuple))
    flops, moved, exps = cost or (0, 0, 0)
    return pl.pallas_call(
        kernel,
        out_shape=out_shape,
        in_specs=[pl.BlockSpec(memory_space=pltpu.SMEM)] * len(scalars)
        + [vmem] * len(operands)
        + [pl.BlockSpec(memory_space=pl.ANY)] * len(unused),
        out_specs=[vmem] * len(out_shape) if several else vmem,
        scratch_shapes=list(scratch),
        compiler_params=pltpu.CompilerParams(vmem_limit_bytes=48 * 1024 * 1024),
        cost_estimate=pl.CostEstimate(flops=flops, bytes_accessed=moved, transcendentals=exps),
        name=name,
    )(*scalars, *operands, *unused)


def message_kernel(core_ref, key_ref, value_ref, ids_ref, gates_ref, seg_ref, keep, give, small):
    first = core_ref[0] == 0
    k0, k1 = (key_ref[:, i * HEAD_SIZE : (i + 1) * HEAD_SIZE] for i in range(2))
    v0, v1 = (
        value_ref[:, i * HEAD_SIZE : (i + 1) * HEAD_SIZE].astype(F32).T.astype(BF16)
        for i in range(2)
    )
    keep[:, :HEAD_SIZE] = jnp.where(first, k0, k1)
    keep[:, HEAD_SIZE:] = jnp.where(first, v0, v1)
    give[:, :HEAD_SIZE] = jnp.where(first, k1, k0)
    give[:, HEAD_SIZE:] = jnp.where(first, v1, v0)
    share = gates_ref[...] / jnp.sum(gates_ref[...], axis=0, keepdims=True)
    share_hi = share.astype(BF16).astype(F32)
    segs = jnp.broadcast_to(seg_ref[...].astype(F32), share.shape)
    small[...] = jnp.concatenate(
        [ids_ref[...].astype(F32), share_hi, share - share_hi, segs], axis=0
    ).astype(BF16)


def turn_kernel(core_ref, query_ref, keep, give):
    first = core_ref[0] == 0
    half = keep.shape[1]
    tok = query_ref.shape[0]
    for h in range(half // tok):
        a, b = (
            query_ref[:, g * (half // tok) * HEAD_SIZE + h * HEAD_SIZE :][:, :HEAD_SIZE]
            .astype(F32)
            .T.astype(BF16)
            for g in range(2)
        )
        keep[:, h * tok : (h + 1) * tok] = jnp.where(first, a, b)
        give[:, h * tok : (h + 1) * tok] = jnp.where(first, b, a)


def attend_kernel(pieces, first, last, info_ref, q_own, q_near, seg_q_ref, pre_q_ref, *refs):
    seg_k_ref, refs = refs[0], refs[1:]
    kv_refs, refs = refs[:pieces], refs[pieces:]
    if not first:
        top_in, sum_in, acc_in, *refs = refs
    if last:
        own_ref, near_ref, top_ref, sum_ref, acc_ref, q_ref = refs
    else:
        top_ref, sum_ref, acc_ref, q_ref = refs
    columns, rows = q_own.shape[1], seg_q_ref.shape[2]
    tiles = 2 * pieces
    scale = math.log2(math.e) / math.sqrt(HEAD_SIZE)
    width = 2 * rows
    q_ref[0] = q_own[...]
    q_ref[1] = q_near[...]
    if first:
        top_ref[...] = jnp.full_like(top_ref, FLOOR)
        sum_ref[...] = jnp.zeros_like(sum_ref)
        acc_ref[...] = jnp.zeros_like(acc_ref)
    else:
        top_ref[...] = top_in[...]
        sum_ref[...] = sum_in[...]
        acc_ref[...] = acc_in[...]
    for piece, kv_ref in enumerate(kv_refs):

        def step(i, _, piece=piece, kv_ref=kv_ref):
            j, g = i // 2, i % 2
            tile = 2 * piece + j

            @pl.when(info_ref[g * tiles + tile] > 0)
            def _():
                square = (rows, rows)
                key_pos = info_ref[2 * tiles + tile] + lax.broadcasted_iota(jnp.int32, square, 0)
                query_pos = info_ref[3 * tiles + g] + lax.broadcasted_iota(jnp.int32, square, 1)
                key_seg = jnp.broadcast_to(seg_k_ref[tile], square).T
                visible = (key_pos <= query_pos) & (
                    (key_seg == seg_q_ref[g]) | (key_seg == pre_q_ref[g])
                )
                bias = jnp.where(visible, 0.0, HIDDEN)
                bias = jnp.concatenate([bias] * (width // rows), axis=1)
                key_tile = kv_ref[j, :, :HEAD_SIZE]
                value_tile = kv_ref[j, :, HEAD_SIZE:]
                for at in range(0, columns, width):
                    part = pl.ds(at, width)
                    scores = (
                        jnp.dot(key_tile, q_ref[g, :, part], preferred_element_type=F32) * scale
                        + bias
                    )
                    old_top = top_ref[g, :, part]
                    new_top = jnp.maximum(old_top, jnp.max(scores, axis=0, keepdims=True))
                    weights = jnp.exp2(scores - new_top)
                    rescale = jnp.exp2(old_top - new_top)
                    top_ref[g, :, part] = new_top
                    sum_ref[g, :, part] = sum_ref[g, :, part] * rescale + jnp.sum(
                        weights, axis=0, keepdims=True
                    )
                    acc_ref[g, :, part] = acc_ref[g, :, part] * rescale + jnp.dot(
                        value_tile, weights.astype(BF16), preferred_element_type=F32
                    )

            return 0

        lax.fori_loop(0, 4, step, 0)
    if last:
        for g, out_ref in enumerate((own_ref, near_ref)):
            for h in range(columns // rows):
                part = pl.ds(h * rows, rows)
                result = acc_ref[g, :, part] / sum_ref[g, :, part]
                out_ref[:, h * HEAD_SIZE : (h + 1) * HEAD_SIZE] = result.T.astype(BF16)


def attend(kv_list, info, q_own, q_near, seg_q, pre_q, seg_k, state, last):
    head, columns = q_own.shape
    rows = seg_q.shape[2]
    first = state is None
    state_shapes = [
        jax.ShapeDtypeStruct((2, 1, columns), F32),
        jax.ShapeDtypeStruct((2, 1, columns), F32),
        jax.ShapeDtypeStruct((2, head, columns), F32),
    ]
    scratch = [pltpu.VMEM((2, head, columns), BF16)]
    if last:
        out_shape = [jax.ShapeDtypeStruct((rows, columns // rows * head), BF16)] * 2
        scratch = [pltpu.VMEM(s.shape, s.dtype) for s in state_shapes] + scratch
    else:
        out_shape = state_shapes
    return call(
        functools.partial(attend_kernel, len(kv_list), first, last),
        "attend_last" if last else "attend_own",
        out_shape,
        [q_own, q_near, seg_q, pre_q, seg_k, *kv_list, *(() if first else state)],
        scalars=[info],
        scratch=scratch,
        cost=(2_000_000_000, 4_000_000, 1_000_000),
    )


def project_kernel(core_ref, own_ref, got_ref, weight_ref, hidden_ref, gain_ref, mixed_ref, out_ref):
    core = core_ref[0]
    half = own_ref.shape[1]
    width = hidden_ref.shape[1]
    block = math.gcd(width, 512)
    own_at = pl.multiple_of(core * half, half)
    got_at = pl.multiple_of((1 - core) * half, half)

    def step(i, total):
        part = pl.ds(pl.multiple_of(i * block, block), block)
        now = (
            hidden_ref[:, part].astype(F32)
            + jnp.dot(
                own_ref[...], weight_ref[pl.ds(own_at, half), part], preferred_element_type=F32
            )
            + jnp.dot(
                got_ref[...], weight_ref[pl.ds(got_at, half), part], preferred_element_type=F32
            )
        )
        mixed_ref[:, part] = now
        return total + jnp.sum(now * now, axis=1, keepdims=True)

    total = lax.fori_loop(0, width // block, step, jnp.zeros((own_ref.shape[0], 1), F32))
    factor = lax.rsqrt(total / width + 1e-06)
    out_ref[...] = (mixed_ref[...] * factor * gain_ref[...]).astype(BF16)


def pick_kernel(n_blk, own_ref, near_ref, rank_ref, *outs):
    tok, width = own_ref.shape
    slots = outs[0].shape[0]
    block = math.gcd(width, 512)
    slot = lax.broadcasted_iota(jnp.int32, (slots, 2 * tok), 0)
    chosen = jnp.concatenate(
        [jnp.where(rank_ref[m] == slot, 1.0, 0.0) for m in range(n_blk)], axis=0
    ).astype(BF16)

    def step(i, _):
        part = pl.ds(pl.multiple_of(i * block, block), block)
        pair = jnp.concatenate([own_ref[:, part], near_ref[:, part]], axis=0)
        rows = jnp.dot(chosen, pair, preferred_element_type=F32)
        for m in range(n_blk):
            outs[m][:, part] = rows[m * slots : (m + 1) * slots].astype(BF16)
        return 0

    lax.fori_loop(0, width // block, step, 0)


def expert_kernel(n_blk, *refs):
    ins, (gate_ref, up_ref, down_ref), refs = refs[:n_blk], refs[n_blk : n_blk + 3], refs[n_blk + 3 :]
    outs, (rows_ref, act_ref) = refs[-n_blk - 2 : -2], refs[-2:]
    slots, width = ins[0].shape
    inner = gate_ref.shape[1]
    rows_ref[...] = jnp.concatenate([r[...].astype(F32) for r in ins], axis=0).astype(BF16)
    block = math.gcd(inner, 256)

    def hidden(i, _):
        part = pl.ds(pl.multiple_of(i * block, block), block)
        gate = jnp.dot(rows_ref[...], gate_ref[:, part], preferred_element_type=F32)
        up = jnp.dot(rows_ref[...], up_ref[:, part], preferred_element_type=F32)
        act_ref[:, part] = (gate / (1.0 + jnp.exp(-gate)) * up).astype(BF16)
        return 0

    lax.fori_loop(0, inner // block, hidden, 0)
    wide = math.gcd(width, 512)

    def answer(i, _):
        part = pl.ds(pl.multiple_of(i * wide, wide), wide)
        rows = jnp.dot(act_ref[...], down_ref[:, part], preferred_element_type=F32)
        for m in range(n_blk):
            outs[m][:, part] = rows[m * slots : (m + 1) * slots].astype(BF16)
        return 0

    lax.fori_loop(0, width // wide, answer, 0)


def spread_kernel(n_blk, *refs):
    backs, (place_ref, own_ref, near_ref) = refs[:n_blk], refs[n_blk : n_blk + 3]
    slots, width = backs[0].shape
    tok = own_ref.shape[0]
    place = place_ref[...]
    lane = lax.broadcasted_iota(jnp.int32, (2 * tok, n_blk * slots), 1).astype(F32)
    weight_hi = jnp.zeros(lane.shape, F32)
    weight_lo = jnp.zeros(lane.shape, F32)
    for m in range(n_blk):
        hit = lane == place[:, m : m + 1]
        weight_hi = weight_hi + jnp.where(hit, place[:, n_blk + m : n_blk + m + 1], 0.0)
        weight_lo = weight_lo + jnp.where(hit, place[:, 2 * n_blk + m : 2 * n_blk + m + 1], 0.0)
    weight_hi, weight_lo = weight_hi.astype(BF16), weight_lo.astype(BF16)
    block = math.gcd(width, 512)

    def step(i, _):
        part = pl.ds(pl.multiple_of(i * block, block), block)
        rows = jnp.concatenate([r[:, part].astype(F32) for r in backs], axis=0).astype(BF16)
        sums = jnp.dot(weight_hi, rows, preferred_element_type=F32) + jnp.dot(
            weight_lo, rows, preferred_element_type=F32
        )
        own_ref[:, part] = sums[:tok]
        near_ref[:, part] = sums[tok:].astype(BF16)
        return 0

    lax.fori_loop(0, width // block, step, 0)


def shards(
    hidden_in,
    queries,
    keys,
    values,
    segment_ids,
    prefix_ids,
    o_weight,
    post_gain,
    expert_ids,
    gates,
    w_gate,
    w_up,
    w_down,
):
    tok, model_width = hidden_in.shape
    n_blk, n_uly = lax.axis_size("blk"), lax.axis_size("uly")
    chips = n_uly // 2
    experts_all = n_blk * n_uly
    top_count = expert_ids.shape[1]
    columns = queries.shape[1] // HEAD_SIZE // 2 * tok
    blk, uly = lax.axis_index("blk"), lax.axis_index("uly")
    core, chip = uly % 2, uly // 2
    me = blk * n_uly + uly
    core_here = core.astype(jnp.int32)[None]

    order = chip_ring(chips)
    ring_pairs = [
        (2 * order[i] + c, 2 * order[(i + 1) % chips] + c) for i in range(chips) for c in range(2)
    ]
    swap_pairs = [(u, u ^ 1) for u in range(n_uly)]
    next_chip = functools.partial(lax.ppermute, axis_name="uly", perm=ring_pairs)
    other_core = functools.partial(lax.ppermute, axis_name="uly", perm=swap_pairs)

    def other_block(x, m):
        return lax.ppermute(x, "blk", [(b, b ^ m) for b in range(n_blk)])

    def shape(*dims, dtype=BF16):
        return jax.ShapeDtypeStruct(dims, dtype)

    keep, give, small = call(
        message_kernel,
        "message",
        [shape(tok, 2 * HEAD_SIZE), shape(tok, 2 * HEAD_SIZE), shape(4 * top_count, tok)],
        [keys, values, expert_ids.T, gates.T, segment_ids[None, :]],
        scalars=[core_here],
    )
    small_chip = jnp.stack([small, other_core(small)])
    kv_chip = jnp.stack([keep, other_core(give)])
    small_steps, kv_steps = [small_chip], [kv_chip]
    for _ in range(chips - 1):
        small_steps.append(next_chip(small_steps[-1]))
        kv_steps.append(next_chip(kv_steps[-1]))
    kv_far = [other_block(kv, m) for kv in kv_steps for m in range(1, n_blk)]
    q_keep, q_give = call(
        turn_kernel, "turn", [shape(HEAD_SIZE, columns)] * 2, [queries], scalars=[core_here]
    )
    q_near = other_core(q_give)

    smalls = jnp.stack(small_steps)
    segs_own = smalls[:, :, 3 * top_count, :].reshape(2 * chips, tok)
    segs_far = [other_block(segs_own, m) for m in range(1, n_blk)]

    order_of = jnp.array(order, jnp.int32)
    place_of = jnp.array([order.index(z) for z in range(chips)], jnp.int32)
    chip_at = order_of[(place_of[chip] - jnp.arange(chips, dtype=jnp.int32)) % chips]
    core_at = jnp.stack([core, 1 - core]).astype(jnp.int32)
    device_at = (2 * chip_at[:, None] + core_at[None, :]).reshape(2 * chips)

    seg_q = segs_own[:2].astype(jnp.int32)
    table = jnp.arange(prefix_ids.shape[0], dtype=jnp.int32)
    pre_q = jnp.sum(
        jnp.where(seg_q[:, :, None] == table[None, None, :], prefix_ids[None, None, :], 0), axis=2
    )
    chip_start = (blk * n_uly + device_at[:2]) * tok

    def tile_info(segs, devices):
        segs = segs.astype(jnp.int32)
        low, high = segs[:, 0], segs[:, -1]
        needed = []
        for g in range(2):
            own = (low <= seg_q[g, -1]) & (high >= seg_q[g, 0])
            shared = jnp.any(
                (pre_q[g][None, :] >= low[:, None]) & (pre_q[g][None, :] <= high[:, None]), axis=1
            )
            needed.append((devices * tok <= chip_start[g]) & (own | shared))
        return jnp.concatenate([n.astype(jnp.int32) for n in needed] + [devices * tok, chip_start])

    seg_rows, pre_rows = seg_q.astype(F32)[:, None, :], pre_q.astype(F32)[:, None, :]
    state = attend(
        kv_steps,
        tile_info(segs_own, blk * n_uly + device_at),
        q_keep,
        q_near,
        seg_rows,
        pre_rows,
        segs_own.astype(F32)[:, None, :],
        None,
        False,
    )
    far_pieces = [(k, m) for k in range(chips) for m in range(1, n_blk)]
    far_segs = jnp.stack([s.reshape(chips, 2, tok) for s in segs_far], axis=1).reshape(-1, tok)
    far_blocks = jnp.stack([blk ^ m for m in range(1, n_blk)])
    far_devices = (
        far_blocks[None, :, None] * n_uly + device_at.reshape(chips, 1, 2)
    ).reshape(-1)
    attended, for_near = attend(
        kv_far,
        tile_info(far_segs, far_devices),
        q_keep,
        q_near,
        seg_rows,
        pre_rows,
        far_segs.astype(F32)[:, None, :],
        state,
        True,
    )
    mixed, normed = call(
        project_kernel,
        "project",
        [shape(tok, model_width, dtype=F32), shape(tok, model_width)],
        [attended, other_core(for_near), o_weight, hidden_in, post_gain[None, :]],
        scalars=[core_here],
        cost=(1_000_000_000, 9_000_000, 0),
    )

    capacity = max(2, 9 * tok * top_count // (8 * experts_all))
    slots = -(-2 * capacity // 8) * 8
    expert_of = jnp.stack([(blk ^ m) * n_uly + uly for m in range(n_blk)]).astype(BF16)
    kinds = smalls.reshape(chips, 2, 4, top_count, tok)
    named = kinds[:, :, 0, None] == expert_of[None, None, :, None, None]
    hit = jnp.any(named, axis=3)
    share_hi = jnp.sum(jnp.where(named, kinds[:, :, 1, None].astype(F32), 0.0), axis=3)
    share_lo = jnp.sum(jnp.where(named, kinds[:, :, 2, None].astype(F32), 0.0), axis=3)
    rank = jnp.dot(
        hit.astype(BF16).reshape(chips * 2 * n_blk, tok),
        jnp.triu(jnp.ones((tok, tok), BF16), 1),
        preferred_element_type=F32,
    ).reshape(chips, 2, n_blk, tok)
    rank = jnp.where(hit, rank + jnp.array([0.0, capacity], F32)[None, :, None, None], -1e6)

    def by_token(x):
        return x.transpose(0, 2, 1, 3).reshape(chips, n_blk, 2 * tok)

    rank, share_hi, share_lo = by_token(rank), by_token(share_hi), by_token(share_lo)
    rank_rows = rank.astype(jnp.int32)[:, :, None, :]
    first_slot = (jnp.arange(n_blk, dtype=jnp.int32) * slots).astype(F32)[None, :, None]
    place = jnp.concatenate(
        [jnp.where(rank >= 0.0, rank + first_slot, -1.0), share_hi, share_lo], axis=1
    ).transpose(0, 2, 1)

    picked = []
    rows_now = normed
    for k in range(chips):
        picked.append(
            call(
                functools.partial(pick_kernel, n_blk),
                "pick",
                [shape(slots, model_width)] * n_blk,
                [rows_now, other_core(rows_now), rank_rows[k]],
                cost=(300_000_000, 0, 0),
            )
        )
        if k < chips - 1:
            rows_now = next_chip(rows_now)
    answers = []
    for k in range(chips):
        inbox = [other_block(x, m) if m else x for m, x in enumerate(picked[k])]
        answers.append(
            call(
                functools.partial(expert_kernel, n_blk),
                "expert",
                [shape(slots, model_width)] * n_blk,
                [*inbox, w_gate[0], w_up[0], w_down[0]],
                scratch=[
                    pltpu.VMEM((n_blk * slots, model_width), BF16),
                    pltpu.VMEM((n_blk * slots, w_gate.shape[2]), BF16),
                ],
                unused=[picked[k + 1][0]] if k < chips - 1 else [],
                cost=(3_000_000_000, 0, 0),
            )
        )
    total = None
    for k in [*range(1, chips), 0]:
        back = [other_block(x, m) if m else x for m, x in enumerate(answers[k])]
        own, near = call(
            functools.partial(spread_kernel, n_blk),
            "spread",
            [shape(tok, model_width, dtype=F32), shape(tok, model_width)],
            [*back, place[k]],
            cost=(600_000_000, 0, 0),
        )
        partial = own + other_core(near).astype(F32)
        if total is not None:
            partial = partial + total.astype(F32)
        if k > 0:
            total = next_chip(partial.astype(BF16))
    return (mixed + partial).astype(BF16)


def solution(mesh):
    rows = P(("blk", "uly"), None)
    in_specs = (
        rows,
        rows,
        rows,
        rows,
        P(("blk", "uly")),
        P(),
        P(),
        P(),
        rows,
        rows,
        P(("blk", "uly"), None, None),
        P(("blk", "uly"), None, None),
        P(("blk", "uly"), None, None),
    )
    return jax.shard_map(shards, mesh=mesh, in_specs=in_specs, out_specs=rows, check_vma=False)
```

time: 612 us -> 282 us (0.46)
  blocking collectives: 205 us -> 0 us
  matrix products: 95.3 us -> 0.09 us
  local copies, waits for them, and re-layouts: 104 us -> 22.9 us
  Pallas kernels: 0 us -> 58.3 us
  starting transfers between devices: 12.5 us -> 64.2 us
  other arithmetic: 56.4 us -> 18 us
  between operations: 13.7 us -> 0.66 us
    all_to_all x3 -> x0, blocking collectives: 161 us -> none  [the longest x1 121 us: shards(): lax.all_to_all(outbox.reshape(experts_all, capacity, model_width), ('blk'...]
    all_to_all x3 -> x0, waiting for transfers between devices: 123 us -> none  [the longest x1 117 us: shards(): lax.all_to_all(expert_answer.reshape(sources, item_count, model_width), (...]
    ppermute x0 -> x63, waiting for transfers between devices: none -> 117 us  [the longest x39 64.6 us: other_block(): return lax.ppermute(x, 'blk', [(b, b ^ m) for b in range(n_blk)])]
    dot_general x20 -> x1, matrix products: 95.3 us -> 0.09 us  [shards(): jnp.dot(hit.astype(BF16).reshape(chips * 2 * n_blk, tok), jnp.triu(jnp.on...]
    ppermute x0 -> x63, starting transfers between devices: none -> 64.2 us  [the longest x39 50.1 us: other_block(): return lax.ppermute(x, 'blk', [(b, b ^ m) for b in range(n_blk)])]
    pallas_call x0 -> x17, Pallas kernels: none -> 58.3 us  [call(): pl.pallas_call(kernel, out_shape=out_shape, in_specs=[pl.BlockSpec(memory...]
    all_gather x1 -> x0, blocking collectives: 43.8 us -> none  [shards(): lax.all_gather(segment_ids, ('blk', 'uly'), axis=0, tiled=True)]
    dynamic_slice x33 -> x1, local copies, waits for them, and re-layouts: 35.9 us -> 1.32 us  [shards(): place_of[chip] - jnp.arange(chips, dtype=jnp.int32)]
  transfers between devices with their start and end apart: 5 -> 63, of which waited for: 2 -> 28; matrix products, arithmetic and copies ran while one was open for 4% -> 9% of each run, Pallas kernels for 0% -> 18%
where the time goes in v2:
time: 282 us
  waiting for transfers between devices  117 us (41%)
  starting transfers between devices  64.2 us (23%)
  Pallas kernels  58.3 us (21%)
  local copies, waits for them, and re-layouts  22.9 us (8%)
  other arithmetic  18 us (6%)
    ppermute x39, waiting for transfers between devices, other_block(): return lax.ppermute(x, 'blk', [(b, b ^ m) for b in range(n_blk)])  64.6 us
    pallas_call x17, Pallas kernels, call(): pl.pallas_call(kernel, out_shape=out_shape, in_specs=[pl.BlockSpec(memory...  58.3 us
    ppermute x39, starting transfers between devices, other_block(): return lax.ppermute(x, 'blk', [(b, b ^ m) for b in range(n_blk)])  50.1 us
    ppermute x3, waiting for transfers between devices, shards(): rows_now = next_chip(rows_now)  25.5 us
    unnamed x64, local copies, waits for them, and re-layouts  14.1 us
    ppermute x3, waiting for transfers between devices, shards(): total = next_chip(partial.astype(BF16))  13.6 us
    ppermute x3, waiting for transfers between devices, shards(): small_steps.append(next_chip(small_steps[-1]))  8.03 us
    convert_element_type x2, other arithmetic, tile_info(): n.astype(jnp.int32)  7.57 us
  transfers between devices with their start and end apart: 63, of which 28 were waited for; matrix products, arithmetic and copies ran while one was open for 9% of the time, Pallas kernels for 18%

profile of v2, /device:TPU:0, one launch (start us, length us, event | category | flops | bytes accessed | tf_op | source)
XLA Modules:
  0.0 281.7 jit_solution(13998861379740538765)
XLA Ops:
  17.5 3.3 %collective-permute-done.2 = bf16[2,32,128]{2,0,1:T(2,128)(2,1)S(1)} collective-permute-done((bf16[2,32,128]{2,0,1:T(2,128)(2,1)S(1)}, bf16[2,32,128]{2,0,1:T(2,128)(2,1)S(1)}, u32[]{:S(2)}, u32[]{:S(2)}) %collective-permute-start.2) | collective-permute-done | bytes 16416 | tf_op jit(solution)/shard_map/ppermute | solution.py:324
  29.4 3.8 %and_convert_fusion.1 = (s32[8]{0:T(128)S(1)}, s32[8]{0:T(128)S(1)}) fusion(pred[8]{0:T(512)(128)(4,1)S(1)} %get-tuple-element.113, s32[8]{0:T(128)S(1)} %mul.67, s32[]{:T(128)} %bitcast.25, s32[]{:T(128)} %bitcast.23, s32[]{:T(128)} %bitcast.7, s32[8,128]{0,1:T(8,128)S(1)} %convert_element_type.157, pred[8]{0:T(512)(128)(4,1)S(1)} %get-tuple-element.114, ...), kind=kLoop, calls=%fused_computation.61 | loop fusion | flops 112 | bytes 200 | tf_op jit(solution)/shard_map/convert_element_type | solution.py:359
  51.7 3.8 %and_convert_fusion.3 = (s32[24]{0:T(128)S(1)}, s32[24]{0:T(128)S(1)}) fusion(pred[24]{0:T(512)(128)(4,1)S(1)} %get-tuple-element.115, s32[24]{0:T(128)S(1)} %get-tuple-element.112, s32[24]{0:T(128)S(1)} %get-tuple-element.111, s32[24]{0:T(128)S(1)} %mul.62, s32[]{:T(128)} %bitcast.25, s32[]{:T(128)} %bitcast.23, s32[]{:T(128)} %bitcast.7, ...), kind=kLoop, calls=%fused_computation.63 | loop fusion | flops 336 | bytes 552 | tf_op jit(solution)/shard_map/convert_element_type | solution.py:359
  70.2 5.7 %project.1 = (f32[128,2048]{1,0:T(8,128)S(1)}, bf16[128,2048]{1,0:T(8,128)(2,1)S(1)}) custom-call(s32[1]{0:T(128)} %bitcast.core_ref, bf16[128,1024]{1,0:T(8,128)(2,1)S(1)} %get-tuple-element.65.own_ref, bf16[128,1024]{1,0:T(8,128)(2,1)S(1)} %collective-permute-done.24.got_ref, bf16[2048,2048]{1,0:T(8,128)(2,1)} %weight_ref.1, ...), custom_call_target="tpu_custom_call" | custom-call | flops 1000000000 | bytes 9000000 | tf_op jit(solution)/shard_map/project/pallas_call | solution.py:25
  77.8 13.0 %collective-permute-done.29.own_ref = bf16[128,2048]{1,0:T(8,128)(2,1)S(1)} collective-permute-done((bf16[128,2048]{1,0:T(8,128)(2,1)S(1)}, bf16[128,2048]{1,0:T(8,128)(2,1)S(1)}, u32[]{:S(2)}, u32[]{:S(2)}) %collective-permute-start.29) | collective-permute-done | bytes 524320 | tf_op jit(solution)/shard_map/ppermute | solution.py:437
  92.3 12.5 %collective-permute-done.35.own_ref = bf16[128,2048]{1,0:T(8,128)(2,1)S(1)} collective-permute-done((bf16[128,2048]{1,0:T(8,128)(2,1)S(1)}, bf16[128,2048]{1,0:T(8,128)(2,1)S(1)}, u32[]{:S(2)}, u32[]{:S(2)}) %collective-permute-start.35) | collective-permute-done | bytes 524320 | tf_op jit(solution)/shard_map/ppermute | solution.py:437
  119.5 7.1 %collective-permute-done.54.refs_2_ = bf16[72,2048]{1,0:T(8,128)(2,1)} collective-permute-done((bf16[72,2048]{1,0:T(8,128)(2,1)}, bf16[72,2048]{1,0:T(8,128)(2,1)}, u32[]{:S(2)}, u32[]{:S(2)}) %collective-permute-start.54) | collective-permute-done | bytes 294944 | tf_op jit(solution)/shard_map/ppermute | solution.py:308
  131.4 8.1 %expert.7 = (bf16[72,2048]{1,0:T(8,128)(2,1)S(1)}, bf16[72,2048]{1,0:T(8,128)(2,1)}, bf16[72,2048]{1,0:T(8,128)(2,1)}, bf16[72,2048]{1,0:T(8,128)(2,1)S(1)}) custom-call(bf16[72,2048]{1,0:T(8,128)(2,1)S(1)} %copy-done.18, bf16[72,2048]{1,0:T(8,128)(2,1)} %collective-permute-done.53.refs_1_, bf16[72,2048]{1,0:T(8,128)(2,1)} %collective-permute-done.54.refs_2_, ...), custom_call_target="tpu_custom_call" | custom-call | flops 3000000000 | tf_op jit(solution)/shard_map/expert/pallas_call | solution.py:25
  151.2 4.2 %collective-permute-start.48 = (bf16[72,2048]{1,0:T(8,128)(2,1)S(1)}, bf16[72,2048]{1,0:T(8,128)(2,1)S(1)}, u32[]{:S(2)}, u32[]{:S(2)}) collective-permute-start(bf16[72,2048]{1,0:T(8,128)(2,1)S(1)} %copy-done.12), channel_id=1, source_target_pairs={{0,24},{8,16},{16,8},{24,0},{1,25},{9,17},{17,9},{25,1},{2,26},{10... | collective-permute-start | bytes 884744 | tf_op jit(solution)/shard_map/ppermute | solution.py:308
  157.6 3.5 %spread.7 = (f32[128,2048]{1,0:T(8,128)S(1)}, bf16[128,2048]{1,0:T(8,128)(2,1)S(1)}) custom-call(bf16[72,2048]{1,0:T(8,128)(2,1)S(1)} %copy-done.23, bf16[72,2048]{1,0:T(8,128)(2,1)} %collective-permute-done.56.refs_1_, bf16[72,2048]{1,0:T(8,128)(2,1)} %collective-permute-done.57.refs_2_, bf16[72,2048]{1,0:T(8,128)(2,1)} %collective-permute-done.58.refs_3_, ...), custom_call_target="tpu_custom_call" | custom-call | flops 600000000 | tf_op jit(solution)/shard_map/spread/pallas_call | solution.py:25
  162.3 6.0 %collective-permute-done.48.refs_3_ = bf16[72,2048]{1,0:T(8,128)(2,1)S(1)} collective-permute-done((bf16[72,2048]{1,0:T(8,128)(2,1)S(1)}, bf16[72,2048]{1,0:T(8,128)(2,1)S(1)}, u32[]{:S(2)}, u32[]{:S(2)}) %collective-permute-start.48) | collective-permute-done | bytes 294944 | tf_op jit(solution)/shard_map/ppermute | solution.py:308
  169.3 7.0 %expert.6 = (bf16[72,2048]{1,0:T(8,128)(2,1)S(1)}, bf16[72,2048]{1,0:T(8,128)(2,1)S(1)}, bf16[72,2048]{1,0:T(8,128)(2,1)S(1)}, bf16[72,2048]{1,0:T(8,128)(2,1)S(1)}) custom-call(bf16[72,2048]{1,0:T(8,128)(2,1)S(1)} %copy-done.21, bf16[72,2048]{1,0:T(8,128)(2,1)S(1)} %collective-permute-done.46.refs_1_, bf16[72,2048]{1,0:T(8,128)(2,1)S(1)} %collective-permute-done.47.refs_2_, ...), custom_call_target="tpu_custom_call" | custom-call | flops 3000000000 | tf_op jit(solution)/shard_map/expert/pallas_call | solution.py:25
  180.6 5.6 %collective-permute-done.49.refs_1_ = bf16[72,2048]{1,0:T(8,128)(2,1)S(1)} collective-permute-done((bf16[72,2048]{1,0:T(8,128)(2,1)S(1)}, bf16[72,2048]{1,0:T(8,128)(2,1)S(1)}, u32[]{:S(2)}, u32[]{:S(2)}) %collective-permute-start.49) | collective-permute-done | bytes 294944 | tf_op jit(solution)/shard_map/ppermute | solution.py:308
  187.0 4.8 %collective-permute-done.50.refs_2_ = bf16[72,2048]{1,0:T(8,128)(2,1)S(1)} collective-permute-done((bf16[72,2048]{1,0:T(8,128)(2,1)S(1)}, bf16[72,2048]{1,0:T(8,128)(2,1)S(1)}, u32[]{:S(2)}, u32[]{:S(2)}) %collective-permute-start.50) | collective-permute-done | bytes 294944 | tf_op jit(solution)/shard_map/ppermute | solution.py:308
  198.9 5.8 %collective-permute-done.39.refs_2_ = bf16[72,2048]{1,0:T(8,128)(2,1)S(1)} collective-permute-done((bf16[72,2048]{1,0:T(8,128)(2,1)S(1)}, bf16[72,2048]{1,0:T(8,128)(2,1)S(1)}, u32[]{:S(2)}, u32[]{:S(2)}) %collective-permute-start.39) | collective-permute-done | bytes 294944 | tf_op jit(solution)/shard_map/ppermute | solution.py:308
  204.7 7.8 %expert.5 = (bf16[72,2048]{1,0:T(8,128)(2,1)S(1)}, bf16[72,2048]{1,0:T(8,128)(2,1)}, bf16[72,2048]{1,0:T(8,128)(2,1)}, bf16[72,2048]{1,0:T(8,128)(2,1)}) custom-call(bf16[72,2048]{1,0:T(8,128)(2,1)S(1)} %get-tuple-element.80.refs_0_.refs_7_, bf16[72,2048]{1,0:T(8,128)(2,1)S(1)} %collective-permute-done.38.refs_1_, ...), custom_call_target="tpu_custom_call" | custom-call | flops 3000000000 | tf_op jit(solution)/shard_map/expert/pallas_call | solution.py:25
  217.8 5.7 %collective-permute-done.41.refs_1_ = bf16[72,2048]{1,0:T(8,128)(2,1)} collective-permute-done((bf16[72,2048]{1,0:T(8,128)(2,1)}, bf16[72,2048]{1,0:T(8,128)(2,1)}, u32[]{:S(2)}, u32[]{:S(2)}) %collective-permute-start.41) | collective-permute-done | bytes 294944 | tf_op jit(solution)/shard_map/ppermute | solution.py:308
  224.4 5.9 %collective-permute-done.42.refs_2_ = bf16[72,2048]{1,0:T(8,128)(2,1)} collective-permute-done((bf16[72,2048]{1,0:T(8,128)(2,1)}, bf16[72,2048]{1,0:T(8,128)(2,1)}, u32[]{:S(2)}, u32[]{:S(2)}) %collective-permute-start.42) | collective-permute-done | bytes 294944 | tf_op jit(solution)/shard_map/ppermute | solution.py:308
  232.6 3.5 %spread.5 = (f32[128,2048]{1,0:T(8,128)S(1)}, bf16[128,2048]{1,0:T(8,128)(2,1)S(1)}) custom-call(bf16[72,2048]{1,0:T(8,128)(2,1)S(1)} %copy-done.25, bf16[72,2048]{1,0:T(8,128)(2,1)} %collective-permute-done.41.refs_1_, bf16[72,2048]{1,0:T(8,128)(2,1)} %collective-permute-done.42.refs_2_, bf16[72,2048]{1,0:T(8,128)(2,1)} %collective-permute-done.43.refs_3_, ...), custom_call_target="tpu_custom_call" | custom-call | flops 600000000 | tf_op jit(solution)/shard_map/spread/pallas_call | solution.py:25
  237.7 4.7 %collective-permute-done.27.refs_2_ = bf16[72,2048]{1,0:T(8,128)(2,1)S(1)} collective-permute-done((bf16[72,2048]{1,0:T(8,128)(2,1)S(1)}, bf16[72,2048]{1,0:T(8,128)(2,1)S(1)}, u32[]{:S(2)}, u32[]{:S(2)}) %collective-permute-start.27) | collective-permute-done | bytes 294944 | tf_op jit(solution)/shard_map/ppermute | solution.py:308
  242.4 7.0 %expert.4 = (bf16[72,2048]{1,0:T(8,128)(2,1)S(1)}, bf16[72,2048]{1,0:T(8,128)(2,1)S(1)}, bf16[72,2048]{1,0:T(8,128)(2,1)S(1)}, bf16[72,2048]{1,0:T(8,128)(2,1)S(1)}) custom-call(bf16[72,2048]{1,0:T(8,128)(2,1)S(1)} %get-tuple-element.69.refs_0_, bf16[72,2048]{1,0:T(8,128)(2,1)S(1)} %collective-permute-done.26.refs_1_, ...), custom_call_target="tpu_custom_call" | custom-call | flops 3000000000 | tf_op jit(solution)/shard_map/expert/pallas_call | solution.py:25
  252.9 4.8 %collective-permute-done.31.refs_1_ = bf16[72,2048]{1,0:T(8,128)(2,1)S(1)} collective-permute-done((bf16[72,2048]{1,0:T(8,128)(2,1)S(1)}, bf16[72,2048]{1,0:T(8,128)(2,1)S(1)}, u32[]{:S(2)}, u32[]{:S(2)}) %collective-permute-start.31) | collective-permute-done | bytes 294944 | tf_op jit(solution)/shard_map/ppermute | solution.py:308
  257.7 5.0 %collective-permute-done.32.refs_2_ = bf16[72,2048]{1,0:T(8,128)(2,1)S(1)} collective-permute-done((bf16[72,2048]{1,0:T(8,128)(2,1)S(1)}, bf16[72,2048]{1,0:T(8,128)(2,1)S(1)}, u32[]{:S(2)}, u32[]{:S(2)}) %collective-permute-start.32) | collective-permute-done | bytes 294944 | tf_op jit(solution)/shard_map/ppermute | solution.py:308
  267.0 13.6 %collective-permute-done.62 = bf16[128,2048]{1,0:T(8,128)(2,1)S(1)} collective-permute-done((bf16[128,2048]{1,0:T(8,128)(2,1)S(1)}, bf16[128,2048]{1,0:T(8,128)(2,1)S(1)}, u32[]{:S(2)}, u32[]{:S(2)}) %collective-permute-start.62) | collective-permute-done | bytes 524320 | tf_op jit(solution)/shard_map/ppermute | solution.py:469
  (248 shorter events, 128.9 us)
Async XLA Ops:
  5.6 43.0 %collective-permute-start.7 = (bf16[128,1024]{1,0:T(8,128)(2,1)S(1)}, bf16[128,1024]{1,0:T(8,128)(2,1)S(1)}, u32[]{:S(2)}, u32[]{:S(2)}) collective-permute-start(bf16[128,1024]{1,0:T(8,128)(2,1)S(1)} %get-tuple-element.59), channel_id=1, source_target_pairs={{0,1},{1,0},{2,3},{3,2},{4,5},{5,4},{6,7},{7,6},{8,9},{9,8},{10,11... | collective-permute-start | bytes 786440 | tf_op jit(solution)/shard_map/ppermute | solution.py:330
  5.7 27.5 %collective-permute-start.8 = (bf16[128,256]{1,0:T(8,128)(2,1)S(1)}, bf16[128,256]{1,0:T(8,128)(2,1)S(1)}, u32[]{:S(2)}, u32[]{:S(2)}) collective-permute-start(bf16[128,256]{1,0:T(8,128)(2,1)S(1)} %get-tuple-element.61), channel_id=1, source_target_pairs={{0,1},{1,0},{2,3},{3,2},{4,5},{5,4},{6,7},{7,6},{8,9},{9,8},{10,11... | collective-permute-start | bytes 196616 | tf_op jit(solution)/shard_map/ppermute | solution.py:321
  75.9 14.9 %collective-permute-start.29 = (bf16[128,2048]{1,0:T(8,128)(2,1)S(1)}, bf16[128,2048]{1,0:T(8,128)(2,1)S(1)}, u32[]{:S(2)}, u32[]{:S(2)}) collective-permute-start(bf16[128,2048]{1,0:T(8,128)(2,1)S(1)} %get-tuple-element.68.own_ref), channel_id=1, source_target_pairs={{0,2},{1,3},{2,6},{3,7},{6,4},{7,5},{4,0},{5,1},{8,10},{9,11},{10,... | collective-permute-start | bytes 1572872 | tf_op jit(solution)/shard_map/ppermute | solution.py:437
  90.8 14.0 %collective-permute-start.35 = (bf16[128,2048]{1,0:T(8,128)(2,1)S(1)}, bf16[128,2048]{1,0:T(8,128)(2,1)S(1)}, u32[]{:S(2)}, u32[]{:S(2)}) collective-permute-start(bf16[128,2048]{1,0:T(8,128)(2,1)S(1)} %collective-permute-done.29.own_ref), channel_id=1, source_target_pairs={{0,2},{1,3},{2,6},{3,7},{6,4},{7,5},{4,0},{5,1},{8,10},{9,11},{10,... | collective-permute-start | bytes 1572872 | tf_op jit(solution)/shard_map/ppermute | solution.py:437
  91.0 14.6 %collective-permute-start.30 = (bf16[128,2048]{1,0:T(8,128)(2,1)S(1)}, bf16[128,2048]{1,0:T(8,128)(2,1)}, u32[]{:S(2)}, u32[]{:S(2)}) collective-permute-start(bf16[128,2048]{1,0:T(8,128)(2,1)S(1)} %collective-permute-done.29.own_ref), channel_id=1, source_target_pairs={{0,1},{1,0},{2,3},{3,2},{4,5},{5,4},{6,7},{7,6},{8,9},{9,8},{10,11... | collective-permute-start | bytes 1572872 | tf_op jit(solution)/shard_map/ppermute | solution.py:432
  111.2 15.4 %collective-permute-start.54 = (bf16[72,2048]{1,0:T(8,128)(2,1)}, bf16[72,2048]{1,0:T(8,128)(2,1)}, u32[]{:S(2)}, u32[]{:S(2)}) collective-permute-start(bf16[72,2048]{1,0:T(8,128)(2,1)} %get-tuple-element.101), channel_id=1, source_target_pairs={{0,16},{8,24},{16,0},{24,8},{1,17},{9,25},{17,1},{25,9},{2,18},{10... | collective-permute-start | bytes 884744 | tf_op jit(solution)/shard_map/ppermute | solution.py:308
  113.1 15.5 %collective-permute-start.55 = (bf16[72,2048]{1,0:T(8,128)(2,1)}, bf16[72,2048]{1,0:T(8,128)(2,1)}, u32[]{:S(2)}, u32[]{:S(2)}) collective-permute-start(bf16[72,2048]{1,0:T(8,128)(2,1)} %get-tuple-element.102), channel_id=1, source_target_pairs={{0,24},{8,16},{16,8},{24,0},{1,25},{9,17},{17,9},{25,1},{2,26},{10... | collective-permute-start | bytes 884744 | tf_op jit(solution)/shard_map/ppermute | solution.py:308
  114.6 28.2 %collective-permute-start.36 = (bf16[128,2048]{1,0:T(8,128)(2,1)S(1)}, bf16[128,2048]{1,0:T(8,128)(2,1)S(1)}, u32[]{:S(2)}, u32[]{:S(2)}) collective-permute-start(bf16[128,2048]{1,0:T(8,128)(2,1)S(1)} %collective-permute-done.35.own_ref), channel_id=1, source_target_pairs={{0,2},{1,3},{2,6},{3,7},{6,4},{7,5},{4,0},{5,1},{8,10},{9,11},{10,... | collective-permute-start | bytes 1572872 | tf_op jit(solution)/shard_map/ppermute | solution.py:437
  142.8 18.3 %collective-permute-start.37 = (bf16[128,2048]{1,0:T(8,128)(2,1)S(1)}, bf16[128,2048]{1,0:T(8,128)(2,1)S(1)}, u32[]{:S(2)}, u32[]{:S(2)}) collective-permute-start(bf16[128,2048]{1,0:T(8,128)(2,1)S(1)} %collective-permute-done.36.own_ref), channel_id=1, source_target_pairs={{0,1},{1,0},{2,3},{3,2},{4,5},{5,4},{6,7},{7,6},{8,9},{9,8},{10,11... | collective-permute-start | bytes 1572872 | tf_op jit(solution)/shard_map/ppermute | solution.py:432
  151.2 17.1 %collective-permute-start.48 = (bf16[72,2048]{1,0:T(8,128)(2,1)S(1)}, bf16[72,2048]{1,0:T(8,128)(2,1)S(1)}, u32[]{:S(2)}, u32[]{:S(2)}) collective-permute-start(bf16[72,2048]{1,0:T(8,128)(2,1)S(1)} %copy-done.12), channel_id=1, source_target_pairs={{0,24},{8,16},{16,8},{24,0},{1,25},{9,17},{17,9},{25,1},{2,26},{10... | collective-permute-start | bytes 884744 | tf_op jit(solution)/shard_map/ppermute | solution.py:308
  161.0 18.8 %collective-permute-start.59 = (bf16[128,2048]{1,0:T(8,128)(2,1)S(1)}, bf16[128,2048]{1,0:T(8,128)(2,1)S(1)}, u32[]{:S(2)}, u32[]{:S(2)}) collective-permute-start(bf16[128,2048]{1,0:T(8,128)(2,1)S(1)} %get-tuple-element.108), channel_id=1, source_target_pairs={{0,1},{1,0},{2,3},{3,2},{4,5},{5,4},{6,7},{7,6},{8,9},{9,8},{10,11... | collective-permute-start | bytes 1572872 | tf_op jit(solution)/shard_map/ppermute | solution.py:465
  177.1 14.7 %collective-permute-start.50 = (bf16[72,2048]{1,0:T(8,128)(2,1)S(1)}, bf16[72,2048]{1,0:T(8,128)(2,1)S(1)}, u32[]{:S(2)}, u32[]{:S(2)}) collective-permute-start(bf16[72,2048]{1,0:T(8,128)(2,1)S(1)} %get-tuple-element.96), channel_id=1, source_target_pairs={{0,16},{8,24},{16,0},{24,8},{1,17},{9,25},{17,1},{25,9},{2,18},{10... | collective-permute-start | bytes 884744 | tf_op jit(solution)/shard_map/ppermute | solution.py:308
  178.0 37.3 %collective-permute-start.25 = (bf16[128,2048]{1,0:T(8,128)(2,1)S(1)}, bf16[128,2048]{1,0:T(8,128)(2,1)S(1)}, u32[]{:S(2)}, u32[]{:S(2)}) collective-permute-start(bf16[128,2048]{1,0:T(8,128)(2,1)S(1)} %get-tuple-element.68.own_ref), channel_id=1, source_target_pairs={{0,1},{1,0},{2,3},{3,2},{4,5},{5,4},{6,7},{7,6},{8,9},{9,8},{10,11... | collective-permute-start | bytes 1572872 | tf_op jit(solution)/shard_map/ppermute | solution.py:432
  178.0 16.6 %collective-permute-start.51 = (bf16[72,2048]{1,0:T(8,128)(2,1)S(1)}, bf16[72,2048]{1,0:T(8,128)(2,1)S(1)}, u32[]{:S(2)}, u32[]{:S(2)}) collective-permute-start(bf16[72,2048]{1,0:T(8,128)(2,1)S(1)} %get-tuple-element.97), channel_id=1, source_target_pairs={{0,24},{8,16},{16,8},{24,0},{1,25},{9,17},{17,9},{25,1},{2,26},{10... | collective-permute-start | bytes 884744 | tf_op jit(solution)/shard_map/ppermute | solution.py:308
  179.8 19.1 %collective-permute-start.38 = (bf16[72,2048]{1,0:T(8,128)(2,1)S(1)}, bf16[72,2048]{1,0:T(8,128)(2,1)S(1)}, u32[]{:S(2)}, u32[]{:S(2)}) collective-permute-start(bf16[72,2048]{1,0:T(8,128)(2,1)S(1)} %get-tuple-element.81), channel_id=1, source_target_pairs={{0,8},{8,0},{16,24},{24,16},{1,9},{9,1},{17,25},{25,17},{2,10},{10... | collective-permute-start | bytes 884744 | tf_op jit(solution)/shard_map/ppermute | solution.py:308
  186.2 18.5 %collective-permute-start.39 = (bf16[72,2048]{1,0:T(8,128)(2,1)S(1)}, bf16[72,2048]{1,0:T(8,128)(2,1)S(1)}, u32[]{:S(2)}, u32[]{:S(2)}) collective-permute-start(bf16[72,2048]{1,0:T(8,128)(2,1)S(1)} %get-tuple-element.82), channel_id=1, source_target_pairs={{0,16},{8,24},{16,0},{24,8},{1,17},{9,25},{17,1},{25,9},{2,18},{10... | collective-permute-start | bytes 884744 | tf_op jit(solution)/shard_map/ppermute | solution.py:308
  194.7 41.4 %collective-permute-start.60 = (bf16[128,2048]{1,0:T(8,128)(2,1)}, bf16[128,2048]{1,0:T(8,128)(2,1)}, u32[]{:S(2)}, u32[]{:S(2)}) collective-permute-start(bf16[128,2048]{1,0:T(8,128)(2,1)} %add_convert_fusion.3), channel_id=1, source_target_pairs={{0,2},{1,3},{2,6},{3,7},{6,4},{7,5},{4,0},{5,1},{8,10},{9,11},{10,... | collective-permute-start | bytes 1572872 | tf_op jit(solution)/shard_map/ppermute | solution.py:469
  198.9 37.3 %collective-permute-start.52 = (bf16[128,2048]{1,0:T(8,128)(2,1)}, bf16[128,2048]{1,0:T(8,128)(2,1)}, u32[]{:S(2)}, u32[]{:S(2)}) collective-permute-start(bf16[128,2048]{1,0:T(8,128)(2,1)} %get-tuple-element.99), channel_id=1, source_target_pairs={{0,1},{1,0},{2,3},{3,2},{4,5},{5,4},{6,7},{7,6},{8,9},{9,8},{10,11... | collective-permute-start | bytes 1572872 | tf_op jit(solution)/shard_map/ppermute | solution.py:465
  214.2 16.1 %collective-permute-start.42 = (bf16[72,2048]{1,0:T(8,128)(2,1)}, bf16[72,2048]{1,0:T(8,128)(2,1)}, u32[]{:S(2)}, u32[]{:S(2)}) collective-permute-start(bf16[72,2048]{1,0:T(8,128)(2,1)} %get-tuple-element.86), channel_id=1, source_target_pairs={{0,16},{8,24},{16,0},{24,8},{1,17},{9,25},{17,1},{25,9},{2,18},{10... | collective-permute-start | bytes 884744 | tf_op jit(solution)/shard_map/ppermute | solution.py:308
  215.3 15.0 %collective-permute-start.43 = (bf16[72,2048]{1,0:T(8,128)(2,1)}, bf16[72,2048]{1,0:T(8,128)(2,1)}, u32[]{:S(2)}, u32[]{:S(2)}) collective-permute-start(bf16[72,2048]{1,0:T(8,128)(2,1)} %get-tuple-element.87), channel_id=1, source_target_pairs={{0,24},{8,16},{16,8},{24,0},{1,25},{9,17},{17,9},{25,1},{2,26},{10... | collective-permute-start | bytes 884744 | tf_op jit(solution)/shard_map/ppermute | solution.py:308
  223.5 14.2 %collective-permute-start.26 = (bf16[72,2048]{1,0:T(8,128)(2,1)S(1)}, bf16[72,2048]{1,0:T(8,128)(2,1)S(1)}, u32[]{:S(2)}, u32[]{:S(2)}) collective-permute-start(bf16[72,2048]{1,0:T(8,128)(2,1)S(1)} %get-tuple-element.70), channel_id=1, source_target_pairs={{0,8},{8,0},{16,24},{24,16},{1,9},{9,1},{17,25},{25,17},{2,10},{10... | collective-permute-start | bytes 884744 | tf_op jit(solution)/shard_map/ppermute | solution.py:308
  236.1 29.0 %collective-permute-start.44 = (bf16[128,2048]{1,0:T(8,128)(2,1)S(1)}, bf16[128,2048]{1,0:T(8,128)(2,1)S(1)}, u32[]{:S(2)}, u32[]{:S(2)}) collective-permute-start(bf16[128,2048]{1,0:T(8,128)(2,1)S(1)} %get-tuple-element.89), channel_id=1, source_target_pairs={{0,1},{1,0},{2,3},{3,2},{4,5},{5,4},{6,7},{7,6},{8,9},{9,8},{10,11... | collective-permute-start | bytes 1572872 | tf_op jit(solution)/shard_map/ppermute | solution.py:465
  237.6 27.5 %collective-permute-start.61 = (bf16[128,2048]{1,0:T(8,128)(2,1)S(1)}, bf16[128,2048]{1,0:T(8,128)(2,1)S(1)}, u32[]{:S(2)}, u32[]{:S(2)}) collective-permute-start(bf16[128,2048]{1,0:T(8,128)(2,1)S(1)} %add_convert_fusion.2), channel_id=1, source_target_pairs={{0,2},{1,3},{2,6},{3,7},{6,4},{7,5},{4,0},{5,1},{8,10},{9,11},{10,... | collective-permute-start | bytes 1572872 | tf_op jit(solution)/shard_map/ppermute | solution.py:469
  265.4 15.3 %collective-permute-start.62 = (bf16[128,2048]{1,0:T(8,128)(2,1)S(1)}, bf16[128,2048]{1,0:T(8,128)(2,1)S(1)}, u32[]{:S(2)}, u32[]{:S(2)}) collective-permute-start(bf16[128,2048]{1,0:T(8,128)(2,1)S(1)} %add_convert_fusion.1), channel_id=1, source_target_pairs={{0,2},{1,3},{2,6},{3,7},{6,4},{7,5},{4,0},{5,1},{8,10},{9,11},{10,... | collective-permute-start | bytes 1572872 | tf_op jit(solution)/shard_map/ppermute | solution.py:469
  (71 other events, 571.2 us)

commit v3 on v2

v3 whole, which is shorter than its diff:
```python
import functools
import math

import jax
import jax.numpy as jnp
from jax import lax
from jax.experimental import pallas as pl
from jax.experimental.pallas import tpu as pltpu
from jax.sharding import PartitionSpec as P

HEAD_SIZE = 128
FLOOR = -1e20
HIDDEN = -1e30
BF16, F32 = jnp.bfloat16, jnp.float32


def chip_ring(count):
    return list(range(0, 1)) + list(range(1, count, 2)) + list(range(2, count, 2))[::-1]


def call(kernel, name, out_shape, operands, scalars=(), scratch=(), unused=(), vmem_mib=8):
    vmem = pl.BlockSpec(memory_space=pltpu.VMEM)
    several = isinstance(out_shape, (list, tuple))
    return pl.pallas_call(
        kernel,
        out_shape=out_shape,
        in_specs=[pl.BlockSpec(memory_space=pltpu.SMEM)] * len(scalars)
        + [vmem] * len(operands)
        + [pl.BlockSpec(memory_space=pl.ANY)] * len(unused),
        out_specs=[vmem] * len(out_shape) if several else vmem,
        scratch_shapes=list(scratch),
        compiler_params=pltpu.CompilerParams(vmem_limit_bytes=vmem_mib * 1024 * 1024),
        cost_estimate=pl.CostEstimate(flops=1000, bytes_accessed=1000, transcendentals=0),
        name=name,
    )(*scalars, *operands, *unused)


def message_kernel(core_ref, key_ref, value_ref, ids_ref, gates_ref, seg_ref, keep, give, small):
    first = core_ref[0] == 0
    k0, k1 = (key_ref[:, i * HEAD_SIZE : (i + 1) * HEAD_SIZE] for i in range(2))
    v0, v1 = (
        value_ref[:, i * HEAD_SIZE : (i + 1) * HEAD_SIZE].astype(F32).T.astype(BF16)
        for i in range(2)
    )
    keep[:, :HEAD_SIZE] = jnp.where(first, k0, k1)
    keep[:, HEAD_SIZE:] = jnp.where(first, v0, v1)
    give[:, :HEAD_SIZE] = jnp.where(first, k1, k0)
    give[:, HEAD_SIZE:] = jnp.where(first, v1, v0)
    share = gates_ref[...] / jnp.sum(gates_ref[...], axis=0, keepdims=True)
    share_hi = share.astype(BF16).astype(F32)
    segs = jnp.broadcast_to(seg_ref[...].astype(F32), share.shape)
    small[...] = jnp.concatenate(
        [ids_ref[...].astype(F32), share_hi, share - share_hi, segs], axis=0
    ).astype(BF16)


def turn_kernel(core_ref, query_ref, keep, give):
    first = core_ref[0] == 0
    half = keep.shape[1]
    tok = query_ref.shape[0]
    for h in range(half // tok):
        a, b = (
            query_ref[:, g * (half // tok) * HEAD_SIZE + h * HEAD_SIZE :][:, :HEAD_SIZE]
            .astype(F32)
            .T.astype(BF16)
            for g in range(2)
        )
        keep[:, h * tok : (h + 1) * tok] = jnp.where(first, a, b)
        give[:, h * tok : (h + 1) * tok] = jnp.where(first, b, a)


def attend_kernel(
    pieces, order, n_blk, first, last, where_ref, prefix_ref, segs_ref, q_own, q_near, pre_ref, *refs
):
    seg_ref, refs = refs[0], refs[1:]
    kv_refs, refs = refs[: len(pieces)], refs[len(pieces) :]
    if not first:
        top_in, sum_in, acc_in, *refs = refs
    if last:
        own_ref, near_ref, top_ref, sum_ref, acc_ref, q_ref = refs
    else:
        top_ref, sum_ref, acc_ref, q_ref = refs
    columns, rows = q_own.shape[1], pre_ref.shape[2]
    chips = len(order)
    scale = math.log2(math.e) / math.sqrt(HEAD_SIZE)
    width = 2 * rows
    q_ref[0] = q_own[...]
    q_ref[1] = q_near[...]
    if first:
        top_ref[...] = jnp.full_like(top_ref, FLOOR)
        sum_ref[...] = jnp.zeros_like(sum_ref)
        acc_ref[...] = jnp.zeros_like(acc_ref)
    else:
        top_ref[...] = top_in[...]
        sum_ref[...] = sum_in[...]
        acc_ref[...] = acc_in[...]
    blk, core, chip = where_ref[0], where_ref[1] % 2, where_ref[1] // 2
    place = sum(jnp.where(chip == z, i, 0) for i, z in enumerate(order))

    def start_of(k, m, j):
        at = lax.rem(place - k + chips, chips)
        chip_there = sum(jnp.where(at == i, z, 0) for i, z in enumerate(order))
        core_there = core + j - 2 * core * j
        return ((blk ^ m) * (2 * chips) + 2 * chip_there + core_there) * rows

    for kv_ref, (k, m) in zip(kv_refs, pieces, strict=True):

        def step(i, _, kv_ref=kv_ref, k=k, m=m):
            j, g = i // 2, i % 2
            tile = (k * n_blk + m) * 2 + j
            key_start, query_start = start_of(k, m, j), start_of(0, 0, g)
            low, high = segs_ref[tile, 0], segs_ref[tile, rows - 1]
            query_low, query_high = segs_ref[g, 0], segs_ref[g, rows - 1]

            def shared(s, found):
                prefix = prefix_ref[s]
                return found | ((prefix >= low) & (prefix <= high)).astype(jnp.int32)

            own = ((low <= query_high) & (high >= query_low)).astype(jnp.int32)
            seen = lax.fori_loop(query_low, query_high + 1, shared, own)

            @pl.when((seen > 0) & (key_start <= query_start))
            def _():
                square = (rows, rows)
                key_pos = key_start + lax.broadcasted_iota(jnp.int32, square, 0)
                query_pos = query_start + lax.broadcasted_iota(jnp.int32, square, 1)
                key_seg = jnp.broadcast_to(seg_ref[tile], square).T
                visible = (key_pos <= query_pos) & (
                    (key_seg == seg_ref[g]) | (key_seg == pre_ref[g])
                )
                bias = jnp.where(visible, 0.0, HIDDEN)
                bias = jnp.concatenate([bias] * (width // rows), axis=1)
                key_tile = kv_ref[j, :, :HEAD_SIZE]
                value_tile = kv_ref[j, :, HEAD_SIZE:]
                for at in range(0, columns, width):
                    part = pl.ds(at, width)
                    scores = (
                        jnp.dot(key_tile, q_ref[g, :, part], preferred_element_type=F32) * scale
                        + bias
                    )
                    old_top = top_ref[g, :, part]
                    new_top = jnp.maximum(old_top, jnp.max(scores, axis=0, keepdims=True))
                    weights = jnp.exp2(scores - new_top)
                    rescale = jnp.exp2(old_top - new_top)
                    top_ref[g, :, part] = new_top
                    sum_ref[g, :, part] = sum_ref[g, :, part] * rescale + jnp.sum(
                        weights, axis=0, keepdims=True
                    )
                    acc_ref[g, :, part] = acc_ref[g, :, part] * rescale + jnp.dot(
                        value_tile, weights.astype(BF16), preferred_element_type=F32
                    )

            return 0

        lax.fori_loop(0, 4, step, 0)
    if last:
        for g, out_ref in enumerate((own_ref, near_ref)):
            for h in range(columns // rows):
                part = pl.ds(h * rows, rows)
                result = acc_ref[g, :, part] / sum_ref[g, :, part]
                out_ref[:, h * HEAD_SIZE : (h + 1) * HEAD_SIZE] = result.T.astype(BF16)


def attend(kv_list, pieces, order, n_blk, scalars, q_own, q_near, pre_rows, seg_rows, state, last):
    head, columns = q_own.shape
    rows = pre_rows.shape[2]
    first = state is None
    state_shapes = [
        jax.ShapeDtypeStruct((2, 1, columns), F32),
        jax.ShapeDtypeStruct((2, 1, columns), F32),
        jax.ShapeDtypeStruct((2, head, columns), F32),
    ]
    scratch = [pltpu.VMEM((2, head, columns), BF16)]
    if last:
        out_shape = [jax.ShapeDtypeStruct((rows, columns // rows * head), BF16)] * 2
        scratch = [pltpu.VMEM(s.shape, s.dtype) for s in state_shapes] + scratch
    else:
        out_shape = state_shapes
    return call(
        functools.partial(attend_kernel, pieces, order, n_blk, first, last),
        "attend_last" if last else "attend_own",
        out_shape,
        [q_own, q_near, pre_rows, seg_rows, *kv_list, *(() if first else state)],
        scalars=scalars,
        scratch=scratch,
        vmem_mib=9 + len(kv_list) // 4,
    )


def project_kernel(core_ref, own_ref, got_ref, weight_ref, hidden_ref, gain_ref, mixed_ref, out_ref):
    core = core_ref[0]
    half = own_ref.shape[1]
    width = hidden_ref.shape[1]
    block = math.gcd(width, 512)
    own_at = pl.multiple_of(core * half, half)
    got_at = pl.multiple_of((1 - core) * half, half)

    def step(i, total):
        part = pl.ds(pl.multiple_of(i * block, block), block)
        now = (
            hidden_ref[:, part].astype(F32)
            + jnp.dot(
                own_ref[...], weight_ref[pl.ds(own_at, half), part], preferred_element_type=F32
            )
            + jnp.dot(
                got_ref[...], weight_ref[pl.ds(got_at, half), part], preferred_element_type=F32
            )
        )
        mixed_ref[:, part] = now
        return total + jnp.sum(now * now, axis=1, keepdims=True)

    total = lax.fori_loop(0, width // block, step, jnp.zeros((own_ref.shape[0], 1), F32))
    factor = lax.rsqrt(total / width + 1e-06)
    out_ref[...] = (mixed_ref[...] * factor * gain_ref[...]).astype(BF16)


def fetch_kernel(count, *refs):
    sources, targets, sems = refs[:count], refs[-count - 1 : -1], refs[-1]
    copies = [
        pltpu.make_async_copy(source, target, sems.at[i])
        for i, (source, target) in enumerate(zip(sources, targets, strict=True))
    ]
    for copy in copies:
        copy.start()
    for copy in copies:
        copy.wait()


def fetch(arrays, after):
    count = len(arrays)
    hbm = pl.BlockSpec(memory_space=pltpu.HBM)
    return pl.pallas_call(
        functools.partial(fetch_kernel, count),
        out_shape=[jax.ShapeDtypeStruct(x.shape, x.dtype) for x in arrays],
        in_specs=[hbm] * (count + len(after)),
        out_specs=[pl.BlockSpec(memory_space=pltpu.VMEM)] * count,
        scratch_shapes=[pltpu.SemaphoreType.DMA((count,))],
        compiler_params=pltpu.CompilerParams(vmem_limit_bytes=24 * 1024 * 1024),
        cost_estimate=pl.CostEstimate(flops=1000, bytes_accessed=1000, transcendentals=0),
        name="fetch",
    )(*arrays, *after)


def slots_kernel(top_count, capacity, pack, n_blk, n_uly, where_ref, *refs):
    chips = (len(refs) - 2) // 3
    smalls, ranks, places = refs[:chips], refs[chips : 2 * chips], refs[2 * chips : -2]
    unpack_ref, repack_ref = refs[-2:]
    tok = smalls[0].shape[2]
    targets = 2 * n_blk
    blk, uly = where_ref[0], where_ref[1]
    earlier = lax.broadcasted_iota(jnp.int32, (tok, tok), 0)
    before = jnp.where(earlier < lax.broadcasted_iota(jnp.int32, (tok, tok), 1), 1.0, 0.0)
    before = before.astype(BF16)
    for small_ref, rank_ref, place_ref in zip(smalls, ranks, places, strict=True):
        ids, hi, lo = (
            small_ref[0, i * top_count : (i + 1) * top_count, :].astype(F32) for i in range(3)
        )
        rows = [[], [], []]
        for target in range(targets):
            m, j = target // 2, target % 2
            named = ids == ((blk ^ m) * n_uly + (uly ^ j)).astype(F32)
            for at, x in enumerate((jnp.ones_like(ids), hi, lo)):
                rows[at].append(jnp.sum(jnp.where(named, x, 0.0), axis=0, keepdims=True))
        hit, hi, lo = (jnp.concatenate(r, axis=0) for r in rows)
        rank = jnp.dot(hit.astype(BF16), before, preferred_element_type=F32)
        rank = jnp.where(hit > 0.0, rank, -1e6)
        for target in range(targets):
            rank_ref[target] = rank[target : target + 1].astype(jnp.int32)
        first = lax.broadcasted_iota(jnp.int32, rank.shape, 0).astype(F32) * (capacity * pack)
        place = jnp.concatenate([rank + first, hi, lo], axis=0)
        spare = jnp.zeros((place_ref.shape[1] - place.shape[0], tok), F32)
        place_ref[...] = jnp.concatenate([place, spare], axis=0).T
    rows_all = targets * capacity
    for part in range(pack):
        for ref, row_axis in ((unpack_ref, 0), (repack_ref, 1)):
            dims = ref.shape[1:] if row_axis == 0 else (ref.shape[0], rows_all)
            row = lax.broadcasted_iota(jnp.int32, dims, row_axis)
            spot = lax.broadcasted_iota(jnp.int32, dims, 1 - row_axis)
            target = sum(jnp.where(row >= t * capacity, 1, 0) for t in range(1, targets))
            same = spot == row + target * (capacity * (pack - 1)) + part * capacity
            same = jnp.where(same, 1.0, 0.0).astype(BF16)
            if row_axis == 0:
                ref[part] = same
            else:
                ref[:, part * rows_all : (part + 1) * rows_all] = same


def pick_kernel(capacity, pack, x_ref, rank_ref, *refs):
    targets, tok = rank_ref.shape[0], x_ref.shape[0]
    outs = refs[-(targets // 2) :]
    _, slots, width = outs[0].shape
    slot = lax.broadcasted_iota(jnp.int32, (slots, tok), 0)
    chosen = jnp.concatenate(
        [
            jnp.concatenate(
                [jnp.where(rank_ref[t] + q * capacity == slot, 1.0, 0.0) for q in range(pack)], axis=1
            )
            for t in range(targets)
        ],
        axis=0,
    ).astype(BF16)
    block = math.gcd(width, 512)
    for at in range(0, width, block):
        parts = jnp.concatenate(
            [x_ref[:, q * width + at : q * width + at + block] for q in range(pack)], axis=0
        )
        rows = jnp.dot(chosen, parts, preferred_element_type=F32)
        for t in range(targets):
            outs[t // 2][t % 2, :, at : at + block] = rows[t * slots : (t + 1) * slots].astype(BF16)


def second_kernel(*refs):
    for i, ref in enumerate(refs[:-1]):
        refs[-1][i] = ref[1]


def join_kernel(n_blk, *refs):
    for m, out_ref in enumerate(refs[-n_blk:]):
        out_ref[0] = refs[m][...]
        out_ref[1] = refs[n_blk][m]


def expert_kernel(n_blk, pack, *refs):
    ins, other_ref, refs = refs[:n_blk], refs[n_blk], refs[n_blk + 1 :]
    gate_ref, up_ref, down_ref, unpack_ref, repack_ref = refs[:5]
    outs, other_out = refs[-n_blk - 5 : -5], refs[-5]
    mail_ref, rows_ref, act_ref, answer_ref = refs[-4:]
    mails = [r[0].astype(F32) for r in ins] + [other_ref[m].astype(F32) for m in range(n_blk)]
    _, slots, part_width = other_ref.shape
    rows_all = rows_ref.shape[0]
    mail_ref[...] = jnp.concatenate(mails, axis=0).astype(BF16)
    block = math.gcd(part_width, 512)
    for q in range(pack):
        for at in range(0, part_width, block):
            rows_ref[:, q * part_width + at : q * part_width + at + block] = jnp.dot(
                unpack_ref[q], mail_ref[:, at : at + block], preferred_element_type=F32
            ).astype(BF16)
    inner, width = down_ref.shape
    block = math.gcd(inner, 256)

    def hidden(i, _):
        part = pl.ds(pl.multiple_of(i * block, block), block)
        gate = jnp.dot(rows_ref[...], gate_ref[:, part], preferred_element_type=F32)
        up = jnp.dot(rows_ref[...], up_ref[:, part], preferred_element_type=F32)
        act_ref[:, part] = (gate / (1.0 + jnp.exp(-gate)) * up).astype(BF16)
        return 0

    lax.fori_loop(0, inner // block, hidden, 0)
    wide = math.gcd(part_width, 512)
    for q in range(pack):

        def answer(i, _, q=q):
            at = i * wide
            to = pl.ds(pl.multiple_of(at, wide), wide)
            part = pl.ds(pl.multiple_of(q * part_width + at, wide), wide)
            answer_ref[q * rows_all : (q + 1) * rows_all, to] = jnp.dot(
                act_ref[...], down_ref[:, part], preferred_element_type=F32
            ).astype(BF16)
            return 0

        lax.fori_loop(0, part_width // wide, answer, 0)
    for at in range(0, part_width, wide):
        mail = jnp.dot(
            repack_ref[...], answer_ref[:, at : at + wide], preferred_element_type=F32
        )
        for t in range(2 * n_blk):
            rows = mail[t * slots : (t + 1) * slots].astype(BF16)
            if t < n_blk:
                outs[t][:, at : at + wide] = rows
            else:
                other_out[t - n_blk, :, at : at + wide] = rows


def spread_kernel(targets, capacity, pack, added, *refs):
    n_blk = targets // 2
    backs, place_ref, adds = refs[:n_blk], refs[n_blk], refs[n_blk + 1 : n_blk + 1 + added]
    out_ref, mail_ref = refs[-2:]
    _, slots, part_width = backs[0].shape
    tok = out_ref.shape[0]
    mails = [r[j].astype(F32) for r in backs for j in range(2)]
    mail_ref[...] = jnp.concatenate(mails, axis=0).astype(BF16)
    place = place_ref[...]
    lane = lax.broadcasted_iota(jnp.int32, (tok, targets * slots), 1).astype(F32)
    for q in range(pack):
        weight_hi = jnp.zeros(lane.shape, F32)
        weight_lo = jnp.zeros(lane.shape, F32)
        for t in range(targets):
            hit = lane == place[:, t : t + 1] + q * capacity
            weight_hi = jnp.where(hit, place[:, targets + t : targets + t + 1], weight_hi)
            weight_lo = jnp.where(hit, place[:, 2 * targets + t : 2 * targets + t + 1], weight_lo)
        weight = jnp.concatenate([weight_hi, weight_lo], axis=0).astype(BF16)
        block = math.gcd(part_width, 512)
        for at in range(0, part_width, block):
            both = jnp.dot(weight, mail_ref[:, at : at + block], preferred_element_type=F32)
            to = slice(q * part_width + at, q * part_width + at + block)
            total = both[:tok] + both[tok:]
            for ref in adds:
                total = total + ref[:, to].astype(F32)
            out_ref[:, to] = total.astype(BF16)


def shards(
    hidden_in,
    queries,
    keys,
    values,
    segment_ids,
    prefix_ids,
    o_weight,
    post_gain,
    expert_ids,
    gates,
    w_gate,
    w_up,
    w_down,
):
    tok, model_width = hidden_in.shape
    n_blk, n_uly = lax.axis_size("blk"), lax.axis_size("uly")
    chips = n_uly // 2
    experts_all = n_blk * n_uly
    top_count = expert_ids.shape[1]
    columns = queries.shape[1] // HEAD_SIZE // 2 * tok
    blk, uly = lax.axis_index("blk"), lax.axis_index("uly")
    core, chip = uly % 2, uly // 2
    me = blk * n_uly + uly
    core_here = core.astype(jnp.int32)[None]

    order = chip_ring(chips)
    ring_pairs = [
        (2 * order[i] + c, 2 * order[(i + 1) % chips] + c) for i in range(chips) for c in range(2)
    ]
    swap_pairs = [(u, u ^ 1) for u in range(n_uly)]
    next_chip = functools.partial(lax.ppermute, axis_name="uly", perm=ring_pairs)
    other_core = functools.partial(lax.ppermute, axis_name="uly", perm=swap_pairs)

    def other_block(x, m):
        return lax.ppermute(x, "blk", [(b, b ^ m) for b in range(n_blk)])

    def shape(*dims, dtype=BF16):
        return jax.ShapeDtypeStruct(dims, dtype)

    keep, give, small = call(
        message_kernel,
        "message",
        [shape(tok, 2 * HEAD_SIZE), shape(tok, 2 * HEAD_SIZE), shape(4 * top_count, tok)],
        [keys, values, expert_ids.T, gates.T, segment_ids[None, :]],
        scalars=[core_here],
    )
    kv_chip = jnp.stack([keep, other_core(give)])
    kv_chip, small = lax.optimization_barrier((kv_chip, small))
    small_chip = jnp.stack([small, other_core(small)])
    seg_at = 3 * top_count
    segs_chip = small_chip[:, seg_at : seg_at + 1]
    small_steps, kv_steps, kv_far = [], [kv_chip], []
    for k in range(chips):
        kv_far += [other_block(kv_steps[k], m) for m in range(1, n_blk)]
        if k < chips - 1:
            kv_next = next_chip(kv_steps[k])
            if k > 0:
                small_steps.append(next_chip(small_steps[-1]))
                sent = n_blk - 1
                kv_next, small_steps[-1], *kv_far[-2 * sent : -sent] = lax.optimization_barrier(
                    (kv_next, small_steps[-1], *kv_far[-2 * sent : -sent])
                )
            else:
                segs_plane = [other_block(small_chip[:, seg_at:], m)[:, :1] for m in range(1, n_blk)]
                kv_next, *segs_plane = lax.optimization_barrier((kv_next, *segs_plane))
                small_chip = jnp.concatenate([small_chip[:, :seg_at], segs_chip, *segs_plane], axis=1)
                small_chip = jnp.pad(small_chip, ((0, 0), (0, -small_chip.shape[1] % 16), (0, 0)))
                small_steps.append(small_chip)
            kv_steps.append(kv_next)
        else:
            small_steps.append(next_chip(small_steps[-1]))
    q_keep, q_give = call(
        turn_kernel, "turn", [shape(HEAD_SIZE, columns)] * 2, [queries], scalars=[core_here]
    )
    q_near = other_core(q_give)

    capacity = max(2, 9 * tok * top_count // (8 * experts_all))
    pack = 8 // math.gcd(capacity, 8)
    slots, part_width = capacity * pack, model_width // pack
    targets = 2 * n_blk
    rows_all = targets * capacity
    where = jnp.stack([blk, uly]).astype(jnp.int32)
    slot_tables = call(
        functools.partial(slots_kernel, top_count, capacity, pack, n_blk, n_uly),
        "slots",
        [shape(targets, 1, tok, dtype=jnp.int32)] * chips
        + [shape(tok, 128, dtype=F32)] * chips
        + [shape(pack, rows_all, targets * slots), shape(targets * slots, pack * rows_all)],
        small_steps,
        scalars=[where],
    )
    ranks, place, unpack, repack = (
        slot_tables[:chips],
        slot_tables[chips : 2 * chips],
        slot_tables[-2],
        slot_tables[-1],
    )
    o_here, gate_here, up_here, down_here = fetch(
        [o_weight, w_gate[0], w_up[0], w_down[0]], [kv_steps[-2]]
    )

    smalls = jnp.stack(small_steps)
    segs = smalls[:, :, seg_at : seg_at + n_blk].transpose(0, 2, 1, 3).reshape(-1, tok)
    seg_rows = segs.astype(F32)[:, None, :]
    segs = segs.astype(jnp.int32)
    table = jnp.arange(prefix_ids.shape[0], dtype=jnp.int32)
    pre_q = jnp.sum(
        jnp.where(segs[:2, :, None] == table[None, None, :], prefix_ids[None, None, :], 0), axis=2
    )
    pre_rows = pre_q.astype(F32)[:, None, :]
    scalars = [where, prefix_ids, segs]
    early = [seg_rows, o_here, gate_here, up_here, down_here, unpack, repack, *ranks, *place]
    seg_rows, o_here, gate_here, up_here, down_here, unpack, repack, *early = (
        lax.optimization_barrier(early)
    )
    ranks, place = early[:chips], early[chips:]
    state = attend(
        kv_steps,
        [(k, 0) for k in range(chips)],
        order,
        n_blk,
        scalars,
        q_keep,
        q_near,
        pre_rows,
        seg_rows,
        None,
        False,
    )
    attended, for_near = attend(
        kv_far,
        [(k, m) for k in range(chips) for m in range(1, n_blk)],
        order,
        n_blk,
        scalars,
        q_keep,
        q_near,
        pre_rows,
        seg_rows,
        state,
        True,
    )
    mixed, normed = call(
        project_kernel,
        "project",
        [shape(tok, model_width, dtype=F32), shape(tok, model_width)],
        [attended, other_core(for_near), o_here, hidden_in, post_gain[None, :]],
        scalars=[core_here],
        vmem_mib=10,
    )

    part = shape(slots, part_width)
    halves, stacked = shape(2, slots, part_width), shape(n_blk, slots, part_width)

    def pick(k, rows):
        kernel = functools.partial(pick_kernel, capacity, pack)
        return call(kernel, "pick", [halves] * n_blk, [rows, ranks[k]])

    def expert(inbox, swapped):
        *own, other = call(
            functools.partial(expert_kernel, n_blk, pack),
            "expert",
            [part] * n_blk + [stacked],
            [*inbox, swapped, gate_here, up_here, down_here, unpack, repack],
            scratch=[
                pltpu.VMEM((targets * slots, part_width), BF16),
                pltpu.VMEM((rows_all, model_width), BF16),
                pltpu.VMEM((rows_all, w_gate.shape[2]), BF16),
                pltpu.VMEM((pack * rows_all, part_width), BF16),
            ],
            vmem_mib=12,
        )
        return own, other

    def spread(k, back, adds):
        return call(
            functools.partial(spread_kernel, targets, capacity, pack, len(adds)),
            "spread",
            shape(tok, model_width),
            [*back, place[k], *adds],
            scratch=[pltpu.VMEM((targets * slots, part_width), BF16)],
            vmem_mib=4 * pack,
        )

    def exchange(parts):
        return [other_block(x, m) if m else x for m, x in enumerate(parts)]

    way_back = [*range(1, chips), 0]
    rows, outbox = {0: normed}, {0: pick(0, normed)}
    arrived, own, other, got, back, total = {}, {}, {}, {}, {}, {}
    for now in range(2 * chips):
        new = {}
        if now + 1 < chips:
            new["rows", now + 1] = [next_chip(rows[now])]
        if now < chips:
            new["arrived", now] = exchange(outbox[now])
        if now >= chips:
            k = way_back[now - chips]
            joined = call(
                functools.partial(join_kernel, n_blk), "join", [halves] * n_blk, [*own[k], got[k]]
            )
            new["back", k] = exchange(joined)
        if now > chips:
            k = way_back[now - chips - 1]
            before = [total[way_back[now - chips - 2]]] if now > chips + 1 else []
            new["total", k] = [next_chip(spread(k, back[k], before))]
        if chips - 1 <= now < 2 * chips - 1:
            k = way_back[now - chips + 1]
            new["got", k] = [other_core(other[k])]
        if 1 <= now <= chips:
            k = now - 1
            seconds = call(second_kernel, "second", stacked, arrived[k])
            own_k, other_k = expert(arrived[k], other_core(seconds))
            new["own", k], new["other", k] = own_k, [other_k]
        if now + 1 < chips:
            new["outbox", now + 1] = pick(now + 1, new["rows", now + 1][0])
        flat = lax.optimization_barrier([x for group in new.values() for x in group])
        for (kind, k), group in new.items():
            group = [flat.pop(0) for _ in group]
            for name, table in (("arrived", arrived), ("own", own), ("back", back), ("outbox", outbox)):
                if kind == name:
                    table[k] = group
            for name, table in (("rows", rows), ("other", other), ("got", got), ("total", total)):
                if kind == name:
                    table[k] = group[0]
    before = [total[way_back[-2]]] if chips > 1 else []
    return spread(0, back[0], [*before, mixed])


def solution(mesh):
    rows = P(("blk", "uly"), None)
    in_specs = (
        rows,
        rows,
        rows,
        rows,
        P(("blk", "uly")),
        P(),
        P(),
        P(),
        rows,
        rows,
        P(("blk", "uly"), None, None),
        P(("blk", "uly"), None, None),
        P(("blk", "uly"), None, None),
    )
    return jax.shard_map(shards, mesh=mesh, in_specs=in_specs, out_specs=rows, check_vma=False)
```

time: 282 us -> 219 us (0.78)
  waiting for transfers between devices: 117 us -> 88.5 us
  other arithmetic: 18 us -> 0.24 us
  local copies, waits for them, and re-layouts: 22.9 us -> 10.5 us
  Pallas kernels: 58.3 us -> 47.6 us
  starting transfers between devices: 64.2 us -> 71.6 us
    ppermute x17, waiting for transfers between devices: 43.3 us -> 27.1 us  [the longest x3 27.1 us: shards(): new['rows', now + 1] = [next_chip(rows[now])]]
    pallas_call x17 -> x26, Pallas kernels: 58.3 us -> 44.2 us  [call(): pl.pallas_call(kernel, out_shape=out_shape, in_specs=[pl.BlockSpec(memory...]
    convert_element_type x14 -> x3, other arithmetic: 11.2 us -> 0.02 us  [the longest x1 0.01 us: shards(): seg_rows = segs.astype(F32)[:, None, :]]
    ppermute x39, waiting for transfers between devices: 64.6 us -> 56.1 us  [other_block(): return lax.ppermute(x, 'blk', [(b, b ^ m) for b in range(n_blk)])]
    ppermute x17, starting transfers between devices: 7.69 us -> 14.9 us  [the longest x3 6.51 us: shards(): kv_next = next_chip(kv_steps[k])]
    ppermute x3, waiting for transfers between devices: 8.03 us -> 1.65 us  [shards(): small_steps.append(next_chip(small_steps[-1]))]
    ppermute x39, starting transfers between devices: 50.1 us -> 55 us  [other_block(): return lax.ppermute(x, 'blk', [(b, b ^ m) for b in range(n_blk)])]
    ppermute x3, starting transfers between devices: 5.31 us -> 1.01 us  [shards(): small_steps.append(next_chip(small_steps[-1]))]
  transfers between devices with their start and end apart: 63 -> 63, of which waited for: 28 -> 23; matrix products, arithmetic and copies ran while one was open for 9% -> 0% of each run, Pallas kernels for 18% -> 17%
where the time goes in v3:
time: 219 us
  waiting for transfers between devices  88.5 us (40%)
  starting transfers between devices  71.6 us (33%)
  Pallas kernels  47.6 us (22%)
  local copies, waits for them, and re-layouts  10.5 us (5%)
    ppermute x39, waiting for transfers between devices, other_block(): return lax.ppermute(x, 'blk', [(b, b ^ m) for b in range(n_blk)])  56.1 us
    ppermute x39, starting transfers between devices, other_block(): return lax.ppermute(x, 'blk', [(b, b ^ m) for b in range(n_blk)])  55 us
    pallas_call x26, Pallas kernels, call(): pl.pallas_call(kernel, out_shape=out_shape, in_specs=[pl.BlockSpec(memory...  44.2 us
    ppermute x3, waiting for transfers between devices, shards(): new['rows', now + 1] = [next_chip(rows[now])]  27.1 us
    unnamed x24, local copies, waits for them, and re-layouts  10.4 us
    ppermute x3, starting transfers between devices, shards(): kv_next = next_chip(kv_steps[k])  6.51 us
  transfers between devices with their start and end apart: 63, of which 23 were waited for; matrix products, arithmetic and copies ran while one was open for 0% of the time, Pallas kernels for 17%

profile of v3, /device:TPU:0, one launch (start us, length us, event | category | flops | bytes accessed | tf_op | source)
XLA Modules:
  0.0 218.9 jit_solution(4692679122761917347)
XLA Ops:
  5.3 3.0 %collective-permute-start.2 = (bf16[2,128,256]{2,1,0:T(8,128)(2,1)S(1)}, bf16[2,128,256]{2,1,0:T(8,128)(2,1)S(1)}, u32[]{:S(2)}, u32[]{:S(2)}) collective-permute-start(bf16[2,128,256]{2,1,0:T(8,128)(2,1)S(1)} %pad_maximum_fusion.refs_1_), channel_id=1, source_target_pairs={{0,2},{1,3},{2,6},{3,7},{6,4},{7,5},{4,0},{5,1},{8,10},{9,11},{10,... | collective-permute-start | bytes 393224 | tf_op jit(solution)/shard_map/ppermute | solution.py:458
  29.1 2.8 %collective-permute-start.20 = (bf16[2,128,256]{2,1,0:T(8,128)(2,1)S(1)}, bf16[2,128,256]{2,1,0:T(8,128)(2,1)S(1)}, u32[]{:S(2)}, u32[]{:S(2)}) collective-permute-start(bf16[2,128,256]{2,1,0:T(8,128)(2,1)S(1)} %collective-permute-done.6.refs_4_.refs_3_), channel_id=1, source_target_pairs={{0,24},{8,16},{16,8},{24,0},{1,25},{9,17},{17,9},{25,1},{2,26},{10... | collective-permute-start | bytes 393224 | tf_op jit(solution)/shard_map/ppermute | solution.py:437
  41.9 3.4 %fetch.1 = (bf16[2048,2048]{1,0:T(8,128)(2,1)S(1)}, bf16[2048,768]{1,0:T(8,128)(2,1)S(1)}, bf16[2048,768]{1,0:T(8,128)(2,1)S(1)}, bf16[768,2048]{1,0:T(8,128)(2,1)S(1)}) custom-call(bf16[2048,2048]{1,0:T(8,128)(2,1)} %refs_0_.1, bf16[2048,768]{1,0:T(8,128)(2,1)S(1)} %bitcast.26, bf16[2048,768]{1,0:T(8,128)(2,1)S(1)} %bitcast.27, ...), custom_call_target="tpu_custom_call" | custom-call | flops 1000 | bytes 1000 | tf_op jit(solution)/shard_map/fetch/pallas_call | solution.py:232
  50.2 3.0 %attend_own.1 = (f32[2,1,1024]{2,1,0:T(1,128)S(1)}, f32[2,1,1024]{2,1,0:T(1,128)S(1)}, f32[2,128,1024]{2,1,0:T(8,128)S(1)}) custom-call(s32[2]{0:T(128)S(1)} %pad_add_fusion.where_ref, s32[64]{0:T(128)S(1)} %copy-done.8, s32[32,128]{1,0:T(8,128)S(1)} %bitcast.30, bf16[128,1024]{1,0:T(8,128)(2,1)S(1)} %get-tuple-element.199.q_own, ...), custom_call_target="tpu_custom_call" | custom-call | flops 1000 | bytes 1000 | tf_op jit(solution)/shard_map/attend_own/pallas_call | solution.py:24
  53.3 3.1 %attend_last.1 = (bf16[128,1024]{1,0:T(8,128)(2,1)S(1)}, bf16[128,1024]{1,0:T(8,128)(2,1)S(1)}) custom-call(s32[2]{0:T(128)S(1)} %pad_add_fusion.where_ref, s32[64]{0:T(128)S(1)} %copy-done.8, s32[32,128]{1,0:T(8,128)S(1)} %bitcast.31, bf16[128,1024]{1,0:T(8,128)(2,1)S(1)} %get-tuple-element.199.q_own, bf16[128,1024]{1,0:T(8,128)(2,1)S(1)} %collective-permute-done.17.q_near, ...), custom_call_target="tpu_custom_call" | custom-call | flops 1000 | bytes 1000 | tf_op jit(solution)/shard_map/attend_last/pallas_call | solution.py:24
  60.3 2.9 %collective-permute-start.25 = (bf16[128,2048]{1,0:T(8,128)(2,1)S(1)}, bf16[128,2048]{1,0:T(8,128)(2,1)S(1)}, u32[]{:S(2)}, u32[]{:S(2)}) collective-permute-start(bf16[128,2048]{1,0:T(8,128)(2,1)S(1)} %get-tuple-element.229.x_ref), channel_id=1, source_target_pairs={{0,2},{1,3},{2,6},{3,7},{6,4},{7,5},{4,0},{5,1},{8,10},{9,11},{10,... | collective-permute-start | bytes 1572872 | tf_op jit(solution)/shard_map/ppermute | solution.py:596
  63.9 6.6 %collective-permute-start.27 = (bf16[2,72,1024]{2,1,0:T(8,128)(2,1)S(1)}, bf16[2,72,1024]{2,1,0:T(8,128)(2,1)S(1)}, u32[]{:S(2)}, u32[]{:S(2)}) collective-permute-start(bf16[2,72,1024]{2,1,0:T(8,128)(2,1)S(1)} %get-tuple-element.233), channel_id=1, source_target_pairs={{0,16},{8,24},{16,0},{24,8},{1,17},{9,25},{17,1},{25,9},{2,18},{10... | collective-permute-start | bytes 884744 | tf_op jit(solution)/shard_map/ppermute | solution.py:437
  71.8 4.1 %collective-permute-done.25.x_ref = bf16[128,2048]{1,0:T(8,128)(2,1)S(1)} collective-permute-done((bf16[128,2048]{1,0:T(8,128)(2,1)S(1)}, bf16[128,2048]{1,0:T(8,128)(2,1)S(1)}, u32[]{:S(2)}, u32[]{:S(2)}) %collective-permute-start.25) | collective-permute-done | bytes 524320 | tf_op jit(solution)/shard_map/ppermute | solution.py:596
  76.4 6.7 %collective-permute-done.27.refs_2_ = bf16[2,72,1024]{2,1,0:T(8,128)(2,1)S(1)} collective-permute-done((bf16[2,72,1024]{2,1,0:T(8,128)(2,1)S(1)}, bf16[2,72,1024]{2,1,0:T(8,128)(2,1)S(1)}, u32[]{:S(2)}, u32[]{:S(2)}) %collective-permute-start.27) | collective-permute-done | bytes 294944 | tf_op jit(solution)/shard_map/ppermute | solution.py:437
  88.8 11.4 %collective-permute-done.29.x_ref = bf16[128,2048]{1,0:T(8,128)(2,1)S(1)} collective-permute-done((bf16[128,2048]{1,0:T(8,128)(2,1)S(1)}, bf16[128,2048]{1,0:T(8,128)(2,1)S(1)}, u32[]{:S(2)}, u32[]{:S(2)}) %collective-permute-start.29) | collective-permute-done | bytes 524320 | tf_op jit(solution)/shard_map/ppermute | solution.py:596
  100.7 6.2 %expert.4 = (bf16[72,1024]{1,0:T(8,128)(2,1)S(1)}, bf16[72,1024]{1,0:T(8,128)(2,1)S(1)}, bf16[72,1024]{1,0:T(8,128)(2,1)S(1)}, bf16[72,1024]{1,0:T(8,128)(2,1)S(1)}, bf16[4,72,1024]{2,1,0:T(8,128)(2,1)S(1)}) custom-call(bf16[2,72,1024]{2,1,0:T(8,128)(2,1)S(1)} %get-tuple-element.245.refs_0_, bf16[2,72,1024]{2,1,0:T(8,128)(2,1)S(1)} %collective-permute-done.26.refs_1_, ...), custom_call_target="tpu_custom_call" | custom-call | flops 1000 | bytes 1000 | tf_op jit(solution)/shard_map/expert/pallas_call | solution.py:24
  110.7 11.6 %collective-permute-done.34.x_ref = bf16[128,2048]{1,0:T(8,128)(2,1)S(1)} collective-permute-done((bf16[128,2048]{1,0:T(8,128)(2,1)S(1)}, bf16[128,2048]{1,0:T(8,128)(2,1)S(1)}, u32[]{:S(2)}, u32[]{:S(2)}) %collective-permute-start.34) | collective-permute-done | bytes 524320 | tf_op jit(solution)/shard_map/ppermute | solution.py:596
  122.8 6.2 %expert.5 = (bf16[72,1024]{1,0:T(8,128)(2,1)S(1)}, bf16[72,1024]{1,0:T(8,128)(2,1)S(1)}, bf16[72,1024]{1,0:T(8,128)(2,1)S(1)}, bf16[72,1024]{1,0:T(8,128)(2,1)S(1)}, bf16[4,72,1024]{2,1,0:T(8,128)(2,1)S(1)}) custom-call(bf16[2,72,1024]{2,1,0:T(8,128)(2,1)S(1)} %get-tuple-element.273.refs_0_, bf16[2,72,1024]{2,1,0:T(8,128)(2,1)S(1)} %collective-permute-done.30.refs_1_, ...), custom_call_target="tpu_custom_call" | custom-call | flops 1000 | bytes 1000 | tf_op jit(solution)/shard_map/expert/pallas_call | solution.py:24
  133.1 6.2 %expert.6 = (bf16[72,1024]{1,0:T(8,128)(2,1)S(1)}, bf16[72,1024]{1,0:T(8,128)(2,1)S(1)}, bf16[72,1024]{1,0:T(8,128)(2,1)S(1)}, bf16[72,1024]{1,0:T(8,128)(2,1)S(1)}, bf16[4,72,1024]{2,1,0:T(8,128)(2,1)S(1)}) custom-call(bf16[2,72,1024]{2,1,0:T(8,128)(2,1)S(1)} %get-tuple-element.296.refs_0_, bf16[2,72,1024]{2,1,0:T(8,128)(2,1)S(1)} %collective-permute-done.35.refs_1_, ...), custom_call_target="tpu_custom_call" | custom-call | flops 1000 | bytes 1000 | tf_op jit(solution)/shard_map/expert/pallas_call | solution.py:24
  139.5 5.7 %collective-permute-done.40.refs_2_ = bf16[2,72,1024]{2,1,0:T(8,128)(2,1)S(1)} collective-permute-done((bf16[2,72,1024]{2,1,0:T(8,128)(2,1)S(1)}, bf16[2,72,1024]{2,1,0:T(8,128)(2,1)S(1)}, u32[]{:S(2)}, u32[]{:S(2)}) %collective-permute-start.40) | collective-permute-done | bytes 294944 | tf_op jit(solution)/shard_map/ppermute | solution.py:437
  149.5 6.2 %expert.7 = (bf16[72,1024]{1,0:T(8,128)(2,1)S(1)}, bf16[72,1024]{1,0:T(8,128)(2,1)S(1)}, bf16[72,1024]{1,0:T(8,128)(2,1)S(1)}, bf16[72,1024]{1,0:T(8,128)(2,1)S(1)}, bf16[4,72,1024]{2,1,0:T(8,128)(2,1)S(1)}) custom-call(bf16[2,72,1024]{2,1,0:T(8,128)(2,1)S(1)} %get-tuple-element.311.refs_0_, bf16[2,72,1024]{2,1,0:T(8,128)(2,1)S(1)} %collective-permute-done.39.refs_1_, ...), custom_call_target="tpu_custom_call" | custom-call | flops 1000 | bytes 1000 | tf_op jit(solution)/shard_map/expert/pallas_call | solution.py:24
  155.9 4.8 %collective-permute-done.45.refs_2_ = bf16[2,72,1024]{2,1,0:T(8,128)(2,1)S(1)} collective-permute-done((bf16[2,72,1024]{2,1,0:T(8,128)(2,1)S(1)}, bf16[2,72,1024]{2,1,0:T(8,128)(2,1)S(1)}, u32[]{:S(2)}, u32[]{:S(2)}) %collective-permute-start.45) | collective-permute-done | bytes 294944 | tf_op jit(solution)/shard_map/ppermute | solution.py:437
  167.9 6.3 %collective-permute-done.49.refs_1_ = bf16[2,72,1024]{2,1,0:T(8,128)(2,1)S(1)} collective-permute-done((bf16[2,72,1024]{2,1,0:T(8,128)(2,1)S(1)}, bf16[2,72,1024]{2,1,0:T(8,128)(2,1)S(1)}, u32[]{:S(2)}, u32[]{:S(2)}) %collective-permute-start.49) | collective-permute-done | bytes 294944 | tf_op jit(solution)/shard_map/ppermute | solution.py:437
  174.2 6.2 %collective-permute-done.50.refs_2_ = bf16[2,72,1024]{2,1,0:T(8,128)(2,1)S(1)} collective-permute-done((bf16[2,72,1024]{2,1,0:T(8,128)(2,1)S(1)}, bf16[2,72,1024]{2,1,0:T(8,128)(2,1)S(1)}, u32[]{:S(2)}, u32[]{:S(2)}) %collective-permute-start.50) | collective-permute-done | bytes 294944 | tf_op jit(solution)/shard_map/ppermute | solution.py:437
  182.0 3.0 %collective-permute-start.57 = (bf16[128,2048]{1,0:T(8,128)(2,1)S(1)}, bf16[128,2048]{1,0:T(8,128)(2,1)S(1)}, u32[]{:S(2)}, u32[]{:S(2)}) collective-permute-start(bf16[128,2048]{1,0:T(8,128)(2,1)S(1)} %spread.5), channel_id=1, source_target_pairs={{0,2},{1,3},{2,6},{3,7},{6,4},{7,5},{4,0},{5,1},{8,10},{9,11},{10,... | collective-permute-start | bytes 1572872 | tf_op jit(solution)/shard_map/ppermute | solution.py:608
  188.7 6.5 %collective-permute-done.54.refs_1_ = bf16[2,72,1024]{2,1,0:T(8,128)(2,1)S(1)} collective-permute-done((bf16[2,72,1024]{2,1,0:T(8,128)(2,1)S(1)}, bf16[2,72,1024]{2,1,0:T(8,128)(2,1)S(1)}, u32[]{:S(2)}, u32[]{:S(2)}) %collective-permute-start.54) | collective-permute-done | bytes 294944 | tf_op jit(solution)/shard_map/ppermute | solution.py:437
  195.2 3.5 %collective-permute-done.55.refs_2_ = bf16[2,72,1024]{2,1,0:T(8,128)(2,1)S(1)} collective-permute-done((bf16[2,72,1024]{2,1,0:T(8,128)(2,1)S(1)}, bf16[2,72,1024]{2,1,0:T(8,128)(2,1)S(1)}, u32[]{:S(2)}, u32[]{:S(2)}) %collective-permute-start.55) | collective-permute-done | bytes 294944 | tf_op jit(solution)/shard_map/ppermute | solution.py:437
  206.4 6.5 %collective-permute-done.59.refs_1_ = bf16[2,72,1024]{2,1,0:T(8,128)(2,1)S(1)} collective-permute-done((bf16[2,72,1024]{2,1,0:T(8,128)(2,1)S(1)}, bf16[2,72,1024]{2,1,0:T(8,128)(2,1)S(1)}, u32[]{:S(2)}, u32[]{:S(2)}) %collective-permute-start.59) | collective-permute-done | bytes 294944 | tf_op jit(solution)/shard_map/ppermute | solution.py:437
  212.9 3.6 %collective-permute-done.60.refs_2_ = bf16[2,72,1024]{2,1,0:T(8,128)(2,1)S(1)} collective-permute-done((bf16[2,72,1024]{2,1,0:T(8,128)(2,1)S(1)}, bf16[2,72,1024]{2,1,0:T(8,128)(2,1)S(1)}, u32[]{:S(2)}, u32[]{:S(2)}) %collective-permute-start.60) | collective-permute-done | bytes 294944 | tf_op jit(solution)/shard_map/ppermute | solution.py:437
  (169 shorter events, 88.9 us)
Async XLA Ops:
  28.4 17.6 %collective-permute-start.17 = (bf16[128,1024]{1,0:T(8,128)(2,1)S(1)}, bf16[128,1024]{1,0:T(8,128)(2,1)S(1)}, u32[]{:S(2)}, u32[]{:S(2)}) collective-permute-start(bf16[128,1024]{1,0:T(8,128)(2,1)S(1)} %get-tuple-element.200), channel_id=1, source_target_pairs={{0,1},{1,0},{2,3},{3,2},{4,5},{5,4},{6,7},{7,6},{8,9},{9,8},{10,11... | collective-permute-start | bytes 786440 | tf_op jit(solution)/shard_map/ppermute | solution.py:477
  29.1 18.7 %collective-permute-start.20 = (bf16[2,128,256]{2,1,0:T(8,128)(2,1)S(1)}, bf16[2,128,256]{2,1,0:T(8,128)(2,1)S(1)}, u32[]{:S(2)}, u32[]{:S(2)}) collective-permute-start(bf16[2,128,256]{2,1,0:T(8,128)(2,1)S(1)} %collective-permute-done.6.refs_4_.refs_3_), channel_id=1, source_target_pairs={{0,24},{8,16},{16,8},{24,0},{1,25},{9,17},{17,9},{25,1},{2,26},{10... | collective-permute-start | bytes 393224 | tf_op jit(solution)/shard_map/ppermute | solution.py:437
  33.2 20.0 %collective-permute-start.19 = (bf16[2,128,256]{2,1,0:T(8,128)(2,1)S(1)}, bf16[2,128,256]{2,1,0:T(8,128)(2,1)S(1)}, u32[]{:S(2)}, u32[]{:S(2)}) collective-permute-start(bf16[2,128,256]{2,1,0:T(8,128)(2,1)S(1)} %collective-permute-done.6.refs_4_.refs_3_), channel_id=1, source_target_pairs={{0,16},{8,24},{16,0},{24,8},{1,17},{9,25},{17,1},{25,9},{2,18},{10... | collective-permute-start | bytes 393224 | tf_op jit(solution)/shard_map/ppermute | solution.py:437
  35.0 18.2 %collective-permute-start.18 = (bf16[2,128,256]{2,1,0:T(8,128)(2,1)S(1)}, bf16[2,128,256]{2,1,0:T(8,128)(2,1)S(1)}, u32[]{:S(2)}, u32[]{:S(2)}) collective-permute-start(bf16[2,128,256]{2,1,0:T(8,128)(2,1)S(1)} %collective-permute-done.6.refs_4_.refs_3_), channel_id=1, source_target_pairs={{0,8},{8,0},{16,24},{24,16},{1,9},{9,1},{17,25},{25,17},{2,10},{10... | collective-permute-start | bytes 393224 | tf_op jit(solution)/shard_map/ppermute | solution.py:437
  60.3 15.6 %collective-permute-start.25 = (bf16[128,2048]{1,0:T(8,128)(2,1)S(1)}, bf16[128,2048]{1,0:T(8,128)(2,1)S(1)}, u32[]{:S(2)}, u32[]{:S(2)}) collective-permute-start(bf16[128,2048]{1,0:T(8,128)(2,1)S(1)} %get-tuple-element.229.x_ref), channel_id=1, source_target_pairs={{0,2},{1,3},{2,6},{3,7},{6,4},{7,5},{4,0},{5,1},{8,10},{9,11},{10,... | collective-permute-start | bytes 1572872 | tf_op jit(solution)/shard_map/ppermute | solution.py:596
  63.9 19.2 %collective-permute-start.27 = (bf16[2,72,1024]{2,1,0:T(8,128)(2,1)S(1)}, bf16[2,72,1024]{2,1,0:T(8,128)(2,1)S(1)}, u32[]{:S(2)}, u32[]{:S(2)}) collective-permute-start(bf16[2,72,1024]{2,1,0:T(8,128)(2,1)S(1)} %get-tuple-element.233), channel_id=1, source_target_pairs={{0,16},{8,24},{16,0},{24,8},{1,17},{9,25},{17,1},{25,9},{2,18},{10... | collective-permute-start | bytes 884744 | tf_op jit(solution)/shard_map/ppermute | solution.py:437
  84.9 15.8 %collective-permute-start.33 = (bf16[4,72,1024]{2,1,0:T(8,128)(2,1)S(1)}, bf16[4,72,1024]{2,1,0:T(8,128)(2,1)S(1)}, u32[]{:S(2)}, u32[]{:S(2)}) collective-permute-start(bf16[4,72,1024]{2,1,0:T(8,128)(2,1)S(1)} %second.4), channel_id=1, source_target_pairs={{0,1},{1,0},{2,3},{3,2},{4,5},{5,4},{6,7},{7,6},{8,9},{9,8},{10,11... | collective-permute-start | bytes 1769480 | tf_op jit(solution)/shard_map/ppermute | solution.py:615
  85.0 15.2 %collective-permute-start.29 = (bf16[128,2048]{1,0:T(8,128)(2,1)S(1)}, bf16[128,2048]{1,0:T(8,128)(2,1)S(1)}, u32[]{:S(2)}, u32[]{:S(2)}) collective-permute-start(bf16[128,2048]{1,0:T(8,128)(2,1)S(1)} %collective-permute-done.25.x_ref), channel_id=1, source_target_pairs={{0,2},{1,3},{2,6},{3,7},{6,4},{7,5},{4,0},{5,1},{8,10},{9,11},{10,... | collective-permute-start | bytes 1572872 | tf_op jit(solution)/shard_map/ppermute | solution.py:596
  85.4 21.6 %collective-permute-start.30 = (bf16[2,72,1024]{2,1,0:T(8,128)(2,1)S(1)}, bf16[2,72,1024]{2,1,0:T(8,128)(2,1)S(1)}, u32[]{:S(2)}, u32[]{:S(2)}) collective-permute-start(bf16[2,72,1024]{2,1,0:T(8,128)(2,1)S(1)} %get-tuple-element.242), channel_id=1, source_target_pairs={{0,8},{8,0},{16,24},{24,16},{1,9},{9,1},{17,25},{25,17},{2,10},{10... | collective-permute-start | bytes 884744 | tf_op jit(solution)/shard_map/ppermute | solution.py:437
  86.5 20.5 %collective-permute-start.31 = (bf16[2,72,1024]{2,1,0:T(8,128)(2,1)S(1)}, bf16[2,72,1024]{2,1,0:T(8,128)(2,1)S(1)}, u32[]{:S(2)}, u32[]{:S(2)}) collective-permute-start(bf16[2,72,1024]{2,1,0:T(8,128)(2,1)S(1)} %get-tuple-element.243), channel_id=1, source_target_pairs={{0,16},{8,24},{16,0},{24,8},{1,17},{9,25},{17,1},{25,9},{2,18},{10... | collective-permute-start | bytes 884744 | tf_op jit(solution)/shard_map/ppermute | solution.py:437
  87.7 19.3 %collective-permute-start.32 = (bf16[2,72,1024]{2,1,0:T(8,128)(2,1)S(1)}, bf16[2,72,1024]{2,1,0:T(8,128)(2,1)S(1)}, u32[]{:S(2)}, u32[]{:S(2)}) collective-permute-start(bf16[2,72,1024]{2,1,0:T(8,128)(2,1)S(1)} %get-tuple-element.244), channel_id=1, source_target_pairs={{0,24},{8,16},{16,8},{24,0},{1,25},{9,17},{17,9},{25,1},{2,26},{10... | collective-permute-start | bytes 884744 | tf_op jit(solution)/shard_map/ppermute | solution.py:437
  107.0 15.8 %collective-permute-start.38 = (bf16[4,72,1024]{2,1,0:T(8,128)(2,1)S(1)}, bf16[4,72,1024]{2,1,0:T(8,128)(2,1)S(1)}, u32[]{:S(2)}, u32[]{:S(2)}) collective-permute-start(bf16[4,72,1024]{2,1,0:T(8,128)(2,1)S(1)} %second.5), channel_id=1, source_target_pairs={{0,1},{1,0},{2,3},{3,2},{4,5},{5,4},{6,7},{7,6},{8,9},{9,8},{10,11... | collective-permute-start | bytes 1769480 | tf_op jit(solution)/shard_map/ppermute | solution.py:615
  107.1 15.2 %collective-permute-start.34 = (bf16[128,2048]{1,0:T(8,128)(2,1)S(1)}, bf16[128,2048]{1,0:T(8,128)(2,1)S(1)}, u32[]{:S(2)}, u32[]{:S(2)}) collective-permute-start(bf16[128,2048]{1,0:T(8,128)(2,1)S(1)} %collective-permute-done.29.x_ref), channel_id=1, source_target_pairs={{0,2},{1,3},{2,6},{3,7},{6,4},{7,5},{4,0},{5,1},{8,10},{9,11},{10,... | collective-permute-start | bytes 1572872 | tf_op jit(solution)/shard_map/ppermute | solution.py:596
  107.1 21.8 %collective-permute-start.35 = (bf16[2,72,1024]{2,1,0:T(8,128)(2,1)S(1)}, bf16[2,72,1024]{2,1,0:T(8,128)(2,1)S(1)}, u32[]{:S(2)}, u32[]{:S(2)}) collective-permute-start(bf16[2,72,1024]{2,1,0:T(8,128)(2,1)S(1)} %get-tuple-element.270), channel_id=1, source_target_pairs={{0,8},{8,0},{16,24},{24,16},{1,9},{9,1},{17,25},{25,17},{2,10},{10... | collective-permute-start | bytes 884744 | tf_op jit(solution)/shard_map/ppermute | solution.py:437
  107.8 21.2 %collective-permute-start.36 = (bf16[2,72,1024]{2,1,0:T(8,128)(2,1)S(1)}, bf16[2,72,1024]{2,1,0:T(8,128)(2,1)S(1)}, u32[]{:S(2)}, u32[]{:S(2)}) collective-permute-start(bf16[2,72,1024]{2,1,0:T(8,128)(2,1)S(1)} %get-tuple-element.271), channel_id=1, source_target_pairs={{0,16},{8,24},{16,0},{24,8},{1,17},{9,25},{17,1},{25,9},{2,18},{10... | collective-permute-start | bytes 884744 | tf_op jit(solution)/shard_map/ppermute | solution.py:437
  109.5 19.5 %collective-permute-start.37 = (bf16[2,72,1024]{2,1,0:T(8,128)(2,1)S(1)}, bf16[2,72,1024]{2,1,0:T(8,128)(2,1)S(1)}, u32[]{:S(2)}, u32[]{:S(2)}) collective-permute-start(bf16[2,72,1024]{2,1,0:T(8,128)(2,1)S(1)} %get-tuple-element.272), channel_id=1, source_target_pairs={{0,24},{8,16},{16,8},{24,0},{1,25},{9,17},{17,9},{25,1},{2,26},{10... | collective-permute-start | bytes 884744 | tf_op jit(solution)/shard_map/ppermute | solution.py:437
  129.2 16.1 %collective-permute-start.42 = (bf16[4,72,1024]{2,1,0:T(8,128)(2,1)S(1)}, bf16[4,72,1024]{2,1,0:T(8,128)(2,1)S(1)}, u32[]{:S(2)}, u32[]{:S(2)}) collective-permute-start(bf16[4,72,1024]{2,1,0:T(8,128)(2,1)S(1)} %get-tuple-element.295), channel_id=1, source_target_pairs={{0,1},{1,0},{2,3},{3,2},{4,5},{5,4},{6,7},{7,6},{8,9},{9,8},{10,11... | collective-permute-start | bytes 1769480 | tf_op jit(solution)/shard_map/ppermute | solution.py:611
  130.2 15.0 %collective-permute-start.40 = (bf16[2,72,1024]{2,1,0:T(8,128)(2,1)S(1)}, bf16[2,72,1024]{2,1,0:T(8,128)(2,1)S(1)}, u32[]{:S(2)}, u32[]{:S(2)}) collective-permute-start(bf16[2,72,1024]{2,1,0:T(8,128)(2,1)S(1)} %get-tuple-element.293), channel_id=1, source_target_pairs={{0,16},{8,24},{16,0},{24,8},{1,17},{9,25},{17,1},{25,9},{2,18},{10... | collective-permute-start | bytes 884744 | tf_op jit(solution)/shard_map/ppermute | solution.py:437
  145.4 17.1 %collective-permute-start.47 = (bf16[4,72,1024]{2,1,0:T(8,128)(2,1)S(1)}, bf16[4,72,1024]{2,1,0:T(8,128)(2,1)S(1)}, u32[]{:S(2)}, u32[]{:S(2)}) collective-permute-start(bf16[4,72,1024]{2,1,0:T(8,128)(2,1)S(1)} %get-tuple-element.310), channel_id=1, source_target_pairs={{0,1},{1,0},{2,3},{3,2},{4,5},{5,4},{6,7},{7,6},{8,9},{9,8},{10,11... | collective-permute-start | bytes 1769480 | tf_op jit(solution)/shard_map/ppermute | solution.py:611
  162.5 17.9 %collective-permute-start.53 = (bf16[4,72,1024]{2,1,0:T(8,128)(2,1)S(1)}, bf16[4,72,1024]{2,1,0:T(8,128)(2,1)S(1)}, u32[]{:S(2)}, u32[]{:S(2)}) collective-permute-start(bf16[4,72,1024]{2,1,0:T(8,128)(2,1)S(1)} %get-tuple-element.338), channel_id=1, source_target_pairs={{0,1},{1,0},{2,3},{3,2},{4,5},{5,4},{6,7},{7,6},{8,9},{9,8},{10,11... | collective-permute-start | bytes 1769480 | tf_op jit(solution)/shard_map/ppermute | solution.py:611
  164.2 16.3 %collective-permute-start.52 = (bf16[128,2048]{1,0:T(8,128)(2,1)S(1)}, bf16[128,2048]{1,0:T(8,128)(2,1)S(1)}, u32[]{:S(2)}, u32[]{:S(2)}) collective-permute-start(bf16[128,2048]{1,0:T(8,128)(2,1)S(1)} %spread.4), channel_id=1, source_target_pairs={{0,2},{1,3},{2,6},{3,7},{6,4},{7,5},{4,0},{5,1},{8,10},{9,11},{10,... | collective-permute-start | bytes 1572872 | tf_op jit(solution)/shard_map/ppermute | solution.py:608
  165.0 15.5 %collective-permute-start.50 = (bf16[2,72,1024]{2,1,0:T(8,128)(2,1)S(1)}, bf16[2,72,1024]{2,1,0:T(8,128)(2,1)S(1)}, u32[]{:S(2)}, u32[]{:S(2)}) collective-permute-start(bf16[2,72,1024]{2,1,0:T(8,128)(2,1)S(1)} %get-tuple-element.331), channel_id=1, source_target_pairs={{0,16},{8,24},{16,0},{24,8},{1,17},{9,25},{17,1},{25,9},{2,18},{10... | collective-permute-start | bytes 884744 | tf_op jit(solution)/shard_map/ppermute | solution.py:437
  174.2 14.6 %collective-permute-start.58 = (bf16[4,72,1024]{2,1,0:T(8,128)(2,1)S(1)}, bf16[4,72,1024]{2,1,0:T(8,128)(2,1)S(1)}, u32[]{:S(2)}, u32[]{:S(2)}) collective-permute-start(bf16[4,72,1024]{2,1,0:T(8,128)(2,1)S(1)} %get-tuple-element.350), channel_id=1, source_target_pairs={{0,1},{1,0},{2,3},{3,2},{4,5},{5,4},{6,7},{7,6},{8,9},{9,8},{10,11... | collective-permute-start | bytes 1769480 | tf_op jit(solution)/shard_map/ppermute | solution.py:611
  182.0 18.4 %collective-permute-start.57 = (bf16[128,2048]{1,0:T(8,128)(2,1)S(1)}, bf16[128,2048]{1,0:T(8,128)(2,1)S(1)}, u32[]{:S(2)}, u32[]{:S(2)}) collective-permute-start(bf16[128,2048]{1,0:T(8,128)(2,1)S(1)} %spread.5), channel_id=1, source_target_pairs={{0,2},{1,3},{2,6},{3,7},{6,4},{7,5},{4,0},{5,1},{8,10},{9,11},{10,... | collective-permute-start | bytes 1572872 | tf_op jit(solution)/shard_map/ppermute | solution.py:608
  (51 other events, 384.1 us)

commit v4 on v3

v4 whole, which is shorter than its diff:
```python
import functools
import math

import jax
import jax.numpy as jnp
from jax import lax
from jax.experimental import pallas as pl
from jax.experimental.pallas import tpu as pltpu
from jax.sharding import PartitionSpec as P

HEAD_SIZE = 128
FLOOR = -1e20
HIDDEN = -1e30
BF16, F32 = jnp.bfloat16, jnp.float32


def chip_ring(count):
    return list(range(0, 1)) + list(range(1, count, 2)) + list(range(2, count, 2))[::-1]


def call(
    kernel, name, out_shape, operands, scalars=(), scratch=(), unused=(), vmem_mib=4, flops=1000
):
    vmem = pl.BlockSpec(memory_space=pltpu.VMEM)
    several = isinstance(out_shape, (list, tuple))
    return pl.pallas_call(
        kernel,
        out_shape=out_shape,
        in_specs=[pl.BlockSpec(memory_space=pltpu.SMEM)] * len(scalars)
        + [vmem] * len(operands)
        + [pl.BlockSpec(memory_space=pl.ANY)] * len(unused),
        out_specs=[vmem] * len(out_shape) if several else vmem,
        scratch_shapes=list(scratch),
        compiler_params=pltpu.CompilerParams(vmem_limit_bytes=vmem_mib * 1024 * 1024),
        cost_estimate=pl.CostEstimate(flops=flops, bytes_accessed=1000, transcendentals=0),
        name=name,
    )(*scalars, *operands, *unused)


def message_kernel(core_ref, key_ref, value_ref, ids_ref, gates_ref, seg_ref, keep, give):
    tok = key_ref.shape[0]
    first = core_ref[0] == 0
    k0, k1 = (key_ref[:, i * HEAD_SIZE : (i + 1) * HEAD_SIZE] for i in range(2))
    v0, v1 = (
        value_ref[:, i * HEAD_SIZE : (i + 1) * HEAD_SIZE].astype(F32).T.astype(BF16)
        for i in range(2)
    )
    share = gates_ref[...] / jnp.sum(gates_ref[...], axis=0, keepdims=True)
    share_hi = share.astype(BF16).astype(F32)
    segs = jnp.broadcast_to(seg_ref[...].astype(F32), share.shape)
    left = jnp.concatenate([ids_ref[...].astype(F32), share_hi], axis=0)
    right = jnp.concatenate([share - share_hi, segs], axis=0)
    small = jnp.concatenate([left, right], axis=1).astype(BF16)
    keep[:tok, :HEAD_SIZE] = jnp.where(first, k0, k1)
    keep[:tok, HEAD_SIZE:] = jnp.where(first, v0, v1)
    keep[tok:, :] = small
    give[:tok, :HEAD_SIZE] = jnp.where(first, k1, k0)
    give[:tok, HEAD_SIZE:] = jnp.where(first, v1, v0)
    give[tok:, :] = small


def small_part(ref, j, tok):
    rows = ref[j, tok:, :].astype(F32)
    half = rows.shape[0] // 2
    return rows[:half, :tok], rows[half:, :tok], rows[:half, tok:], rows[half : half + 1, tok:]


def pair_kernel(a_ref, b_ref, out_ref):
    if len(a_ref.shape) < len(out_ref.shape):
        out_ref[0] = a_ref[...]
        out_ref[1] = b_ref[...]
    else:
        out_ref[: a_ref.shape[0]] = a_ref[...]
        out_ref[a_ref.shape[0] :] = b_ref[...]


def turn_kernel(core_ref, query_ref, keep, give):
    first = core_ref[0] == 0
    half = keep.shape[1]
    tok = query_ref.shape[0]
    for h in range(half // tok):
        a, b = (
            query_ref[:, g * (half // tok) * HEAD_SIZE + h * HEAD_SIZE :][:, :HEAD_SIZE]
            .astype(F32)
            .T.astype(BF16)
            for g in range(2)
        )
        keep[:, h * tok : (h + 1) * tok] = jnp.where(first, a, b)
        give[:, h * tok : (h + 1) * tok] = jnp.where(first, b, a)


def attend_kernel(
    pieces, order, n_blk, first, last, where_ref, prefix_ref, q_own, q_near, home_ref, *refs
):
    kv_refs, refs = refs[: len(pieces)], refs[len(pieces) :]
    if not first:
        top_in, sum_in, acc_in, *refs = refs
    if last:
        own_ref, near_ref, top_ref, sum_ref, acc_ref, *refs = refs
    else:
        top_ref, sum_ref, acc_ref, *refs = refs
    seg_ref, pre_ref, table, segs_ref, sem, q_ref = refs
    columns, rows = q_own.shape[1], home_ref.shape[1] - 16
    each = kv_refs[0].shape[0]
    for tile in range(2 + each * len(pieces)):
        ref, at = (home_ref, tile) if tile < 2 else (kv_refs[(tile - 2) // each], (tile - 2) % each)
        seg_ref[tile] = small_part(ref, at, rows)[3]
        table[tile : tile + 1, :] = seg_ref[tile].astype(jnp.int32)
    copy = pltpu.make_async_copy(table, segs_ref, sem)
    copy.start()
    copy.wait()
    for g in range(2):

        def prefixes(s, row, g=g):
            return jnp.where(seg_ref[g] == s.astype(F32), prefix_ref[s].astype(F32), row)

        pre_ref[g] = lax.fori_loop(
            segs_ref[g, 0], segs_ref[g, rows - 1] + 1, prefixes, jnp.zeros((1, rows), F32)
        )
    chips = len(order)
    scale = math.log2(math.e) / math.sqrt(HEAD_SIZE)
    width = 2 * rows
    q_ref[0] = q_own[...]
    q_ref[1] = q_near[...]
    if first:
        top_ref[...] = jnp.full_like(top_ref, FLOOR)
        sum_ref[...] = jnp.zeros_like(sum_ref)
        acc_ref[...] = jnp.zeros_like(acc_ref)
    else:
        top_ref[...] = top_in[...]
        sum_ref[...] = sum_in[...]
        acc_ref[...] = acc_in[...]
    blk, core, chip = where_ref[0], where_ref[1] % 2, where_ref[1] // 2
    place = sum(jnp.where(chip == z, i, 0) for i, z in enumerate(order))

    def start_of(k, m, j):
        at = lax.rem(place - k + chips, chips)
        chip_there = sum(jnp.where(at == i, z, 0) for i, z in enumerate(order))
        core_there = core + j - 2 * core * j
        return ((blk ^ m) * (2 * chips) + 2 * chip_there + core_there) * rows

    for number, (kv_ref, (k, m)) in enumerate(zip(kv_refs, pieces, strict=True)):

        def step(i, _, number=number, kv_ref=kv_ref, k=k, m=m):
            at, g = i // 2, i % 2
            tile = 2 + each * number + at
            key_start, query_start = start_of(k + at // 2, m, at % 2), start_of(0, 0, g)
            low, high = segs_ref[tile, 0], segs_ref[tile, rows - 1]
            query_low, query_high = segs_ref[g, 0], segs_ref[g, rows - 1]

            def shared(s, found):
                prefix = prefix_ref[s]
                return found | ((prefix >= low) & (prefix <= high)).astype(jnp.int32)

            own = ((low <= query_high) & (high >= query_low)).astype(jnp.int32)
            seen = lax.fori_loop(query_low, query_high + 1, shared, own)

            @pl.when((seen > 0) & (key_start <= query_start))
            def _():
                square = (rows, rows)
                key_pos = key_start + lax.broadcasted_iota(jnp.int32, square, 0)
                query_pos = query_start + lax.broadcasted_iota(jnp.int32, square, 1)
                key_seg = jnp.broadcast_to(seg_ref[tile], square).T
                visible = (key_pos <= query_pos) & (
                    (key_seg == seg_ref[g]) | (key_seg == pre_ref[g])
                )
                bias = jnp.where(visible, 0.0, HIDDEN)
                bias = jnp.concatenate([bias] * (width // rows), axis=1)
                key_tile = kv_ref[at, :rows, :HEAD_SIZE]
                value_tile = kv_ref[at, :rows, HEAD_SIZE:]
                for column in range(0, columns, width):
                    part = pl.ds(column, width)
                    scores = (
                        jnp.dot(key_tile, q_ref[g, :, part], preferred_element_type=F32) * scale
                        + bias
                    )
                    old_top = top_ref[g, :, part]
                    new_top = jnp.maximum(old_top, jnp.max(scores, axis=0, keepdims=True))
                    weights = jnp.exp2(scores - new_top)
                    rescale = jnp.exp2(old_top - new_top)
                    top_ref[g, :, part] = new_top
                    sum_ref[g, :, part] = sum_ref[g, :, part] * rescale + jnp.sum(
                        weights, axis=0, keepdims=True
                    )
                    acc_ref[g, :, part] = acc_ref[g, :, part] * rescale + jnp.dot(
                        value_tile, weights.astype(BF16), preferred_element_type=F32
                    )

            return 0

        lax.fori_loop(0, 2 * each, step, 0)
    if last:
        for g, out_ref in enumerate((own_ref, near_ref)):
            for h in range(columns // rows):
                part = pl.ds(h * rows, rows)
                result = acc_ref[g, :, part] / sum_ref[g, :, part]
                out_ref[:, h * HEAD_SIZE : (h + 1) * HEAD_SIZE] = result.T.astype(BF16)


def attend(kv_list, pieces, order, n_blk, scalars, q_own, q_near, home, state, last):
    head, columns = q_own.shape
    rows = home.shape[1] - 16
    tiles = 2 + kv_list[0].shape[0] * len(kv_list)
    first = state is None
    state_shapes = [
        jax.ShapeDtypeStruct((2, 1, columns), F32),
        jax.ShapeDtypeStruct((2, 1, columns), F32),
        jax.ShapeDtypeStruct((2, head, columns), F32),
    ]
    scratch = [
        pltpu.VMEM((tiles, 1, rows), F32),
        pltpu.VMEM((2, 1, rows), F32),
        pltpu.VMEM((tiles, rows), jnp.int32),
        pltpu.SMEM((tiles, rows), jnp.int32),
        pltpu.SemaphoreType.DMA,
        pltpu.VMEM((2, head, columns), BF16),
    ]
    if last:
        out_shape = [jax.ShapeDtypeStruct((rows, columns // rows * head), BF16)] * 2
        scratch = [pltpu.VMEM(s.shape, s.dtype) for s in state_shapes] + scratch
    else:
        out_shape = state_shapes
    return call(
        functools.partial(attend_kernel, pieces, order, n_blk, first, last),
        "attend_last" if last else "attend_own",
        out_shape,
        [q_own, q_near, home, *kv_list, *(() if first else state)],
        scalars=scalars,
        scratch=scratch,
        vmem_mib=5 + len(kv_list) // 2,
        flops=8_000_000_000 if last else 1000,
    )


def project_kernel(
    core_ref, own_ref, got_ref, hidden_ref, gain_ref, weight_hbm, mixed_ref, out_ref, weight_ref, sems
):
    core = core_ref[0]
    half = own_ref.shape[1]
    width = hidden_ref.shape[1]
    blocks = sems.shape[0]
    block = width // blocks
    own_at = pl.multiple_of(core * half, half)
    got_at = pl.multiple_of((1 - core) * half, half)
    copies = [
        pltpu.make_async_copy(
            weight_hbm.at[:, pl.ds(i * block, block)], weight_ref.at[i], sems.at[i]
        )
        for i in range(blocks)
    ]
    for copy in copies:
        copy.start()
    total = jnp.zeros((own_ref.shape[0], 1), F32)
    for i, copy in enumerate(copies):
        part = pl.ds(i * block, block)
        copy.wait()
        now = (
            hidden_ref[:, part].astype(F32)
            + jnp.dot(
                own_ref[...], weight_ref[i, pl.ds(own_at, half), :], preferred_element_type=F32
            )
            + jnp.dot(
                got_ref[...], weight_ref[i, pl.ds(got_at, half), :], preferred_element_type=F32
            )
        )
        mixed_ref[:, part] = now
        total = total + jnp.sum(now * now, axis=1, keepdims=True)
    factor = lax.rsqrt(total / width + 1e-06)
    out_ref[...] = (mixed_ref[...] * factor * gain_ref[...]).astype(BF16)


def fetch_kernel(count, *refs):
    sources, targets, sems = refs[:count], refs[-count - 1 : -1], refs[-1]
    copies = [
        pltpu.make_async_copy(source, target, sems.at[i])
        for i, (source, target) in enumerate(zip(sources, targets, strict=True))
    ]
    for copy in copies:
        copy.start()
    for copy in copies:
        copy.wait()


def fetch(arrays, after):
    count = len(arrays)
    hbm = pl.BlockSpec(memory_space=pltpu.HBM)
    return pl.pallas_call(
        functools.partial(fetch_kernel, count),
        out_shape=[jax.ShapeDtypeStruct(x.shape, x.dtype) for x in arrays],
        in_specs=[hbm] * (count + len(after)),
        out_specs=[pl.BlockSpec(memory_space=pltpu.VMEM)] * count,
        scratch_shapes=[pltpu.SemaphoreType.DMA((count,))],
        compiler_params=pltpu.CompilerParams(vmem_limit_bytes=4 * 1024 * 1024),
        cost_estimate=pl.CostEstimate(flops=1000, bytes_accessed=1000, transcendentals=0),
        name="fetch",
    )(*arrays, *after)


def sort_rows(kv_ref, where_ref, top_count, n_blk, n_uly):
    tok = kv_ref.shape[1] - 16
    blk, uly = where_ref[0], where_ref[1]
    ids, hi, lo, _ = (x[:top_count] for x in small_part(kv_ref, 0, tok))
    rows = [[], [], []]
    for target in range(2 * n_blk):
        m, j = target // 2, target % 2
        named = ids == ((blk ^ m) * n_uly + (uly ^ j)).astype(F32)
        for at, x in enumerate((jnp.ones_like(ids), hi, lo)):
            rows[at].append(jnp.sum(jnp.where(named, x, 0.0), axis=0, keepdims=True))
    hit, hi, lo = (jnp.concatenate(r, axis=0) for r in rows)
    earlier = lax.broadcasted_iota(jnp.int32, (tok, tok), 0)
    before = jnp.where(earlier < lax.broadcasted_iota(jnp.int32, (tok, tok), 1), 1.0, 0.0)
    rank = jnp.dot(hit.astype(BF16), before.astype(BF16), preferred_element_type=F32)
    return jnp.where(hit > 0.0, rank, -1e6), hi, lo


def weights_kernel(top_count, capacity, pack, n_blk, n_uly, where_ref, *refs):
    chips = (len(refs) - 1) // 2
    targets, slots = 2 * n_blk, capacity * pack
    for kv_ref, weight_ref in zip(refs[:chips], refs[-chips:], strict=True):
        tok = kv_ref.shape[1] - 16
        rank, hi, lo = sort_rows(kv_ref, where_ref, top_count, n_blk, n_uly)
        first = lax.broadcasted_iota(jnp.int32, rank.shape, 0).astype(F32) * slots
        spare = jnp.zeros((tok - 3 * targets, tok), F32)
        place = jnp.concatenate([rank + first, hi, lo, spare], axis=0).T
        for q in range(pack):
            for at in range(0, targets * slots, 128):
                width = min(128, targets * slots - at)
                lane = at + lax.broadcasted_iota(jnp.int32, (tok, width), 1).astype(F32)
                weight_hi = jnp.zeros(lane.shape, F32)
                weight_lo = jnp.zeros(lane.shape, F32)
                for t in range(at // slots, min(targets, -(-(at + width) // slots))):
                    hit = lane == place[:, t : t + 1] + q * capacity
                    weight_hi = jnp.where(hit, place[:, targets + t : targets + t + 1], weight_hi)
                    weight_lo = jnp.where(
                        hit, place[:, 2 * targets + t : 2 * targets + t + 1], weight_lo
                    )
                weight_ref[q, :tok, at : at + width] = weight_hi.astype(BF16)
                weight_ref[q, tok:, at : at + width] = weight_lo.astype(BF16)


def slots_kernel(top_count, capacity, pack, n_blk, n_uly, where_ref, *refs):
    chips = (len(refs) - 2) // 2
    unpack_ref, repack_ref = refs[-2:]
    targets = 2 * n_blk
    for kv_ref, rank_ref in zip(refs[:chips], refs[chips:-2], strict=True):
        rank = sort_rows(kv_ref, where_ref, top_count, n_blk, n_uly)[0].astype(jnp.int32)
        for target in range(targets):
            rank_ref[target] = rank[target : target + 1]
    for part in range(pack):
        for ref, row_axis in ((unpack_ref, 0), (repack_ref, 1)):
            row = lax.broadcasted_iota(jnp.int32, ref.shape[1:], row_axis)
            spot = lax.broadcasted_iota(jnp.int32, ref.shape[1:], 1 - row_axis)
            target = sum(jnp.where(row >= t * capacity, 1, 0) for t in range(1, n_blk))
            same = spot == row + target * (capacity * (pack - 1)) + part * capacity
            ref[part] = jnp.where(same, 1.0, 0.0).astype(BF16)


def pick_kernel(capacity, pack, x_ref, rank_ref, *refs):
    targets, tok = rank_ref.shape[0], x_ref.shape[0]
    outs = refs[-(targets // 2) :]
    _, slots, width = outs[0].shape
    slot = lax.broadcasted_iota(jnp.int32, (slots, tok), 0)
    chosen = jnp.concatenate(
        [
            jnp.concatenate(
                [jnp.where(rank_ref[t] + q * capacity == slot, 1.0, 0.0) for q in range(pack)], axis=1
            )
            for t in range(targets)
        ],
        axis=0,
    ).astype(BF16)
    block = math.gcd(width, 512)
    for at in range(0, width, block):
        parts = jnp.concatenate(
            [x_ref[:, q * width + at : q * width + at + block] for q in range(pack)], axis=0
        )
        rows = jnp.dot(chosen, parts, preferred_element_type=F32)
        for t in range(targets):
            outs[t // 2][t % 2, :, at : at + block] = rows[t * slots : (t + 1) * slots].astype(BF16)


def expert_kernel(n_blk, pack, *refs):
    ins, experts, (unpack_ref, repack_ref), refs = (
        refs[:n_blk],
        (refs[n_blk : n_blk + 3], refs[n_blk + 3 : n_blk + 6]),
        refs[n_blk + 6 : n_blk + 8],
        refs[n_blk + 8 :],
    )
    outs, (mail_ref, rows_ref, act_ref, answer_ref) = refs[-n_blk - 4 : -4], refs[-4:]
    _, slots, part_width = ins[0].shape
    block = math.gcd(part_width, 512)
    for j, (gate_ref, up_ref, down_ref) in enumerate(experts):
        mail_ref[j] = jnp.concatenate([r[j].astype(F32) for r in ins], axis=0).astype(BF16)
        for q in range(pack):
            for at in range(0, part_width, block):
                rows_ref[j, :, q * part_width + at : q * part_width + at + block] = jnp.dot(
                    unpack_ref[q], mail_ref[j, :, at : at + block], preferred_element_type=F32
                ).astype(BF16)
        inner = down_ref.shape[1]
        inner_block = math.gcd(inner, 256)

        def hidden(i, _, j=j, gate_ref=gate_ref, up_ref=up_ref):
            part = pl.ds(pl.multiple_of(i * inner_block, inner_block), inner_block)
            gate = jnp.dot(rows_ref[j], gate_ref[0, :, part], preferred_element_type=F32)
            up = jnp.dot(rows_ref[j], up_ref[0, :, part], preferred_element_type=F32)
            act_ref[j, :, part] = (gate / (1.0 + jnp.exp(-gate)) * up).astype(BF16)
            return 0

        lax.fori_loop(0, inner // inner_block, hidden, 0)
        for q in range(pack):

            def answer(i, _, j=j, q=q, down_ref=down_ref):
                at = i * block
                to = pl.ds(pl.multiple_of(at, block), block)
                part = pl.ds(pl.multiple_of(q * part_width + at, block), block)
                answer_ref[j, q, :, to] = jnp.dot(
                    act_ref[j], down_ref[0, :, part], preferred_element_type=F32
                ).astype(BF16)
                return 0

            lax.fori_loop(0, part_width // block, answer, 0)
        for at in range(0, part_width, block):
            mail = sum(
                jnp.dot(
                    repack_ref[q],
                    answer_ref[j, q, :, at : at + block],
                    preferred_element_type=F32,
                )
                for q in range(pack)
            )
            for m in range(n_blk):
                outs[m][j, :, at : at + block] = mail[m * slots : (m + 1) * slots].astype(BF16)


def spread_kernel(n_blk, pack, added, *refs):
    backs, weight_ref, adds = refs[:n_blk], refs[n_blk], refs[n_blk + 1 : n_blk + 1 + added]
    out_ref, mail_ref = refs[-2:]
    _, slots, part_width = backs[0].shape
    tok = out_ref.shape[0]
    mails = [r[j].astype(F32) for r in backs for j in range(2)]
    mail_ref[...] = jnp.concatenate(mails, axis=0).astype(BF16)
    block = math.gcd(part_width, 512)
    for q in range(pack):
        for at in range(0, part_width, block):
            both = jnp.dot(weight_ref[q], mail_ref[:, at : at + block], preferred_element_type=F32)
            to = slice(q * part_width + at, q * part_width + at + block)
            total = both[:tok] + both[tok:]
            for ref in adds:
                total = total + ref[:, to].astype(F32)
            out_ref[:, to] = total.astype(BF16)


def shards(
    hidden_in,
    queries,
    keys,
    values,
    segment_ids,
    prefix_ids,
    o_weight,
    post_gain,
    expert_ids,
    gates,
    w_gate,
    w_up,
    w_down,
):
    tok, model_width = hidden_in.shape
    n_blk, n_uly = lax.axis_size("blk"), lax.axis_size("uly")
    chips = n_uly // 2
    experts_all = n_blk * n_uly
    top_count = expert_ids.shape[1]
    columns = queries.shape[1] // HEAD_SIZE // 2 * tok
    blk, uly = lax.axis_index("blk"), lax.axis_index("uly")
    core, chip = uly % 2, uly // 2
    me = blk * n_uly + uly
    core_here = core.astype(jnp.int32)[None]

    order = chip_ring(chips)
    ring_pairs = [
        (2 * order[i] + c, 2 * order[(i + 1) % chips] + c) for i in range(chips) for c in range(2)
    ]
    swap_pairs = [(u, u ^ 1) for u in range(n_uly)]
    next_chip = functools.partial(lax.ppermute, axis_name="uly", perm=ring_pairs)
    other_core = functools.partial(lax.ppermute, axis_name="uly", perm=swap_pairs)

    def other_block(x, m):
        return lax.ppermute(x, "blk", [(b, b ^ m) for b in range(n_blk)])

    def tied(*groups):
        flat = list(lax.optimization_barrier(tuple(x for group in groups for x in group)))
        return [[flat.pop(0) for _ in group] for group in groups]

    def shape(*dims, dtype=BF16):
        return jax.ShapeDtypeStruct(dims, dtype)

    keep, give = call(
        message_kernel,
        "message",
        [shape(tok + 16, 2 * HEAD_SIZE)] * 2,
        [keys, values, expert_ids.T, gates.T, segment_ids[None, :]],
        scalars=[core_here],
    )
    where = jnp.stack([blk, uly]).astype(jnp.int32)
    q_keep, q_give = call(
        turn_kernel, "turn", [shape(HEAD_SIZE, columns)] * 2, [queries], scalars=[core_here]
    )
    kv_steps = [
        call(pair_kernel, "pair", shape(2, tok + 16, 2 * HEAD_SIZE), [keep, other_core(give)])
    ]
    groups, kv_far = [], []
    for k in range(1, chips):
        kv_next = next_chip(kv_steps[-1])
        beside = [q_keep, other_core(q_give)] if k == 1 else []
        kv_next, *beside = lax.optimization_barrier((kv_next, *beside))
        if k == 1:
            q_keep, q_near = beside
        kv_steps.append(kv_next)
        if k % 2:
            groups.append(
                call(pair_kernel, "pair", shape(4, tok + 16, 2 * HEAD_SIZE), kv_steps[-2:])
            )
            kv_far.append([other_block(groups[-1], m) for m in range(1, n_blk)])
    capacity = max(2, 9 * tok * top_count // (8 * experts_all))
    pack = 8 // math.gcd(capacity, 8)
    slots, part_width = capacity * pack, model_width // pack
    targets = 2 * n_blk
    half_rows = n_blk * capacity
    *ranks, unpack, repack = call(
        functools.partial(slots_kernel, top_count, capacity, pack, n_blk, n_uly),
        "slots",
        [shape(targets, 1, tok, dtype=jnp.int32)] * chips
        + [shape(pack, half_rows, n_blk * slots), shape(pack, n_blk * slots, half_rows)],
        kv_steps,
        scalars=[where],
        vmem_mib=3 + pack * pack // 2,
    )
    scalars = [where, prefix_ids]
    pieces = [(k, 0) for k in range(0, chips, 2)]
    state = attend(
        groups, pieces, order, n_blk, scalars, q_keep, q_near, kv_steps[0], None, False
    )
    *ranks, unpack, repack, a, b, c, x, y, z = lax.optimization_barrier(
        [*ranks, unpack, repack, *state, w_gate, w_up, w_down]
    )
    (x, y, z), *kv_far = tied([x, y, z], *kv_far)
    mine, near = [x, y, z], [other_core(w) for w in (x, y, z)]
    pieces = [(k, m) for k in range(0, chips, 2) for m in range(1, n_blk)]
    attended, for_near = attend(
        [kv for group in kv_far for kv in group],
        pieces,
        order,
        n_blk,
        scalars,
        q_keep,
        q_near,
        kv_steps[0],
        [a, b, c],
        True,
    )
    blocks = max(1, model_width // 512)
    mixed, normed = call(
        project_kernel,
        "project",
        [shape(tok, model_width, dtype=F32), shape(tok, model_width)],
        [attended, other_core(for_near), hidden_in, post_gain[None, :]],
        scalars=[core_here],
        unused=[o_weight],
        scratch=[
            pltpu.VMEM((blocks, o_weight.shape[0], model_width // blocks), BF16),
            pltpu.SemaphoreType.DMA((blocks,)),
        ],
        vmem_mib=12,
        flops=4_000_000_000,
    )

    halves = shape(2, slots, part_width)

    def pick(k, rows):
        kernel = functools.partial(pick_kernel, capacity, pack)
        return call(kernel, "pick", [halves] * n_blk, [rows, ranks[k]])

    def expert(inbox):
        return call(
            functools.partial(expert_kernel, n_blk, pack),
            "expert",
            [halves] * n_blk,
            [*inbox, *experts, unpack, repack],
            scratch=[
                pltpu.VMEM((2, n_blk * slots, part_width), BF16),
                pltpu.VMEM((2, half_rows, model_width), BF16),
                pltpu.VMEM((2, half_rows, w_gate.shape[2]), BF16),
                pltpu.VMEM((2, pack, half_rows, part_width), BF16),
            ],
            vmem_mib=6 + pack,
        )

    def spread(k, back, adds):
        return call(
            functools.partial(spread_kernel, n_blk, pack, len(adds)),
            "spread",
            shape(tok, model_width),
            [*back, weights[k], *adds],
            scratch=[pltpu.VMEM((targets * slots, part_width), BF16)],
            vmem_mib=2 + pack,
        )

    def exchange(parts):
        return [other_block(x, m) if m else x for m, x in enumerate(parts)]

    way_back = [*range(1, chips), 0]
    normed, *experts = lax.optimization_barrier([normed, *mine, *near])
    rows = {0: normed}
    arrived, answers, back, total, weights = {}, {}, {}, {}, {}
    for now in range(2 * chips):
        new = {}
        if now + 1 < chips:
            new["rows", now + 1] = [next_chip(rows[now])]
        if now < chips:
            picked = pick(now, rows[now])
            new["arrived", now] = exchange(picked)
        if now >= chips:
            k = way_back[now - chips]
            new["back", k] = exchange(answers[k])
        if now > chips:
            k = way_back[now - chips - 1]
            before = [total[way_back[now - chips - 2]]] if now > chips + 1 else []
            new["total", k] = [next_chip(spread(k, back[k], before))]
        if chips - 1 <= now < 2 * chips - 1:
            k = way_back[now - chips + 1]
            new["answers", k] = expert(arrived[k])
        if chips <= now < 2 * chips:
            k = way_back[now - chips]
            new["weights", k] = [
                call(
                    functools.partial(weights_kernel, top_count, capacity, pack, n_blk, n_uly),
                    "weights",
                    shape(pack, 2 * tok, targets * slots),
                    [kv_steps[k]],
                    scalars=[where],
                    unused=[answers[k][0]],
                    vmem_mib=3 + pack * pack // 2,
                )
            ]
        flat = lax.optimization_barrier([x for group in new.values() for x in group])
        for (kind, k), group in new.items():
            group = [flat.pop(0) for _ in group]
            for name, table in (("arrived", arrived), ("answers", answers), ("back", back)):
                if kind == name:
                    table[k] = group
            for name, table in (("rows", rows), ("total", total), ("weights", weights)):
                if kind == name:
                    table[k] = group[0]
    before = [total[way_back[-2]]] if chips > 1 else []
    return spread(0, back[0], [*before, mixed])


def solution(mesh):
    rows = P(("blk", "uly"), None)
    in_specs = (
        rows,
        rows,
        rows,
        rows,
        P(("blk", "uly")),
        P(),
        P(),
        P(),
        rows,
        rows,
        P(("blk", "uly"), None, None),
        P(("blk", "uly"), None, None),
        P(("blk", "uly"), None, None),
    )
    return jax.shard_map(shards, mesh=mesh, in_specs=in_specs, out_specs=rows, check_vma=False)
```

time: 219 us -> 194 us (0.89)
  waiting for transfers between devices: 88.5 us -> 67.8 us
  starting transfers between devices: 71.6 us -> 53.6 us
  Pallas kernels: 47.6 us -> 57 us
  local copies, waits for them, and re-layouts: 10.5 us -> 14.2 us
    ppermute x3, waiting for transfers between devices: 27.1 us -> 0.01 us  [shards(): new['rows', now + 1] = [next_chip(rows[now])]]
    ppermute x39 -> x30, starting transfers between devices: 55 us -> 37.8 us  [other_block(): return lax.ppermute(x, 'blk', [(b, b ^ m) for b in range(n_blk)])]
    pallas_call x26 -> x25, Pallas kernels: 44.2 us -> 57 us  [call(): pl.pallas_call(kernel, out_shape=out_shape, in_specs=[pl.BlockSpec(memory...]
    ppermute x17 -> x8, waiting for transfers between devices: 3.75 us -> 13.9 us  [the longest x3 12.7 us: shards(): kv_next = next_chip(kv_steps[-1])]
    ppermute x39 -> x30, waiting for transfers between devices: 56.1 us -> 49.4 us  [other_block(): return lax.ppermute(x, 'blk', [(b, b ^ m) for b in range(n_blk)])]
    ppermute x17 -> x8, starting transfers between devices: 9.39 us -> 5.43 us  [the longest x3 4.27 us: shards(): kv_next = next_chip(kv_steps[-1])]
    unnamed x24 -> x56, local copies, waits for them, and re-layouts: 10.4 us -> 14.2 us
    pallas_call x1 -> x0, Pallas kernels: 3.43 us -> none  [fetch(): pl.pallas_call(functools.partial(fetch_kernel, count), out_shape=[jax.Sha...]
  transfers between devices with their start and end apart: 63 -> 45, of which waited for: 23 -> 18; matrix products, arithmetic and copies ran while one was open for 0% -> 0% of each run, Pallas kernels for 17% -> 27%
where the time goes in v4:
time: 194 us; the launch traced here: 193 us
  waiting for transfers between devices  67.8 us (35%)
  Pallas kernels  57 us (29%)
  starting transfers between devices  53.6 us (28%)
  local copies, waits for them, and re-layouts  14.2 us (7%)
    pallas_call x25, Pallas kernels, call(): pl.pallas_call(kernel, out_shape=out_shape, in_specs=[pl.BlockSpec(memory...  57 us
    ppermute x30, waiting for transfers between devices, other_block(): return lax.ppermute(x, 'blk', [(b, b ^ m) for b in range(n_blk)])  49.4 us
    ppermute x30, starting transfers between devices, other_block(): return lax.ppermute(x, 'blk', [(b, b ^ m) for b in range(n_blk)])  37.8 us
    unnamed x56, local copies, waits for them, and re-layouts  14.2 us
    ppermute x3, waiting for transfers between devices, shards(): kv_next = next_chip(kv_steps[-1])  12.7 us
    ppermute x3, starting transfers between devices, shards(): new['rows', now + 1] = [next_chip(rows[now])]  6.08 us
    ppermute x1, waiting for transfers between devices, shards(): other_core(for_near)  4.5 us
    ppermute x3, starting transfers between devices, shards(): kv_next = next_chip(kv_steps[-1])  4.27 us
  transfers between devices with their start and end apart: 45, of which 18 were waited for; matrix products, arithmetic and copies ran while one was open for 0% of the time, Pallas kernels for 27%

profile of v4, /device:TPU:0, one launch (start us, length us, event | category | flops | bytes accessed | tf_op | source)
XLA Modules:
  0.0 193.1 jit_solution(10746817031655823920)
XLA Ops:
  7.1 2.8 %collective-permute-start.1 = (bf16[2,144,256]{2,1,0:T(8,128)(2,1)S(1)}, bf16[2,144,256]{2,1,0:T(8,128)(2,1)S(1)}, u32[]{:S(2)}, u32[]{:S(2)}) collective-permute-start(bf16[2,144,256]{2,1,0:T(8,128)(2,1)S(1)} %pair.3.refs_0_.a_ref.home_ref), channel_id=1, source_target_pairs={{0,2},{1,3},{2,6},{3,7},{6,4},{7,5},{4,0},{5,1},{8,10},{9,11},{10,... | collective-permute-start | bytes 442376 | tf_op jit(solution)/shard_map/ppermute | solution.py:513
  9.9 5.4 %collective-permute-done.1.refs_1_.b_ref.refs_0_ = bf16[2,144,256]{2,1,0:T(8,128)(2,1)S(1)} collective-permute-done((bf16[2,144,256]{2,1,0:T(8,128)(2,1)S(1)}, bf16[2,144,256]{2,1,0:T(8,128)(2,1)S(1)}, u32[]{:S(2)}, u32[]{:S(2)}) %collective-permute-start.1) | collective-permute-done | bytes 147488 | tf_op jit(solution)/shard_map/ppermute | solution.py:513
  18.4 3.4 %collective-permute-done.3.refs_2_.a_ref.refs_0_ = bf16[2,144,256]{2,1,0:T(8,128)(2,1)S(1)} collective-permute-done((bf16[2,144,256]{2,1,0:T(8,128)(2,1)S(1)}, bf16[2,144,256]{2,1,0:T(8,128)(2,1)S(1)}, u32[]{:S(2)}, u32[]{:S(2)}) %collective-permute-start.3) | collective-permute-done | bytes 147488 | tf_op jit(solution)/shard_map/ppermute | solution.py:513
  23.9 3.9 %collective-permute-done.4.refs_3_.b_ref.refs_0_ = bf16[2,144,256]{2,1,0:T(8,128)(2,1)S(1)} collective-permute-done((bf16[2,144,256]{2,1,0:T(8,128)(2,1)S(1)}, bf16[2,144,256]{2,1,0:T(8,128)(2,1)S(1)}, u32[]{:S(2)}, u32[]{:S(2)}) %collective-permute-start.4) | collective-permute-done | bytes 147488 | tf_op jit(solution)/shard_map/ppermute | solution.py:513
  27.8 2.3 %collective-permute-start.7 = (bf16[4,144,256]{2,1,0:T(8,128)(2,1)}, bf16[4,144,256]{2,1,0:T(8,128)(2,1)}, u32[]{:S(2)}, u32[]{:S(2)}) collective-permute-start(bf16[4,144,256]{2,1,0:T(8,128)(2,1)} %pair.4.refs_0_), channel_id=1, source_target_pairs={{0,24},{8,16},{16,8},{24,0},{1,25},{9,17},{17,9},{25,1},{2,26},{10... | collective-permute-start | bytes 884744 | tf_op jit(solution)/shard_map/ppermute | solution.py:488
  40.9 4.4 %attend_own.1 = (f32[2,1,1024]{2,1,0:T(1,128)S(1)}, f32[2,1,1024]{2,1,0:T(1,128)S(1)}, f32[2,128,1024]{2,1,0:T(8,128)S(1)}) custom-call(s32[2]{0:T(128)S(1)} %pad_add_fusion.where_ref, s32[64]{0:T(128)S(1)} %copy-done.21, bf16[128,1024]{1,0:T(8,128)(2,1)S(1)} %copy-done.11, bf16[128,1024]{1,0:T(8,128)(2,1)S(1)} %copy-done.14, ...), custom_call_target="tpu_custom_call" | custom-call | flops 1000 | bytes 1000 | tf_op jit(solution)/shard_map/attend_own/pallas_call | solution.py:26
  45.4 2.6 %collective-permute-done.8.refs_3_ = bf16[4,144,256]{2,1,0:T(8,128)(2,1)} collective-permute-done((bf16[4,144,256]{2,1,0:T(8,128)(2,1)}, bf16[4,144,256]{2,1,0:T(8,128)(2,1)}, u32[]{:S(2)}, u32[]{:S(2)}) %collective-permute-start.8) | collective-permute-done | bytes 294944 | tf_op jit(solution)/shard_map/ppermute | solution.py:488
  52.9 5.9 %attend_last.1 = (bf16[128,1024]{1,0:T(8,128)(2,1)S(1)}, bf16[128,1024]{1,0:T(8,128)(2,1)S(1)}) custom-call(s32[2]{0:T(128)S(1)} %pad_add_fusion.where_ref, s32[64]{0:T(128)S(1)} %copy-done.22, bf16[128,1024]{1,0:T(8,128)(2,1)S(1)} %copy-done.12, bf16[128,1024]{1,0:T(8,128)(2,1)S(1)} %copy-done.15, bf16[2,144,256]{2,1,0:T(8,128)(2,1)S(1)} %pair.3.refs_0_.a_ref.home_ref, ...), custom_call_target="tpu_custom_call" | custom-call | flops 8000000000 | bytes 1000 | tf_op jit(solution)/shard_map/attend_last/pallas_call | solution.py:26
  59.4 4.5 %collective-permute-done.11.got_ref = bf16[128,1024]{1,0:T(8,128)(2,1)S(1)} collective-permute-done((bf16[128,1024]{1,0:T(8,128)(2,1)S(1)}, bf16[128,1024]{1,0:T(8,128)(2,1)S(1)}, u32[]{:S(2)}, u32[]{:S(2)}) %collective-permute-start.11) | collective-permute-done | bytes 262176 | tf_op jit(solution)/shard_map/ppermute | solution.py:566
  63.9 3.6 %project.1 = (f32[128,2048]{1,0:T(8,128)S(1)}, bf16[128,2048]{1,0:T(8,128)(2,1)S(1)}) custom-call(s32[1]{0:T(128)} %bitcast.core_ref, bf16[128,1024]{1,0:T(8,128)(2,1)S(1)} %get-tuple-element.171.own_ref, bf16[128,1024]{1,0:T(8,128)(2,1)S(1)} %collective-permute-done.11.got_ref, bf16[128,2048]{1,0:T(8,128)(2,1)S(1)} %copy-done.24, f32[1,2048]{1,0:T(1,128)S(1)} %bitcast.10, ...), custom_call_target="tpu_custom_call" | custom-call | flops 4000000000 | bytes 1000 | tf_op jit(solution)/shard_map/project/pallas_call | solution.py:26
  67.5 3.5 %collective-permute-start.15 = (bf16[128,2048]{1,0:T(8,128)(2,1)S(1)}, bf16[128,2048]{1,0:T(8,128)(2,1)S(1)}, u32[]{:S(2)}, u32[]{:S(2)}) collective-permute-start(bf16[128,2048]{1,0:T(8,128)(2,1)S(1)} %get-tuple-element.177.x_ref), channel_id=1, source_target_pairs={{0,2},{1,3},{2,6},{3,7},{6,4},{7,5},{4,0},{5,1},{8,10},{9,11},{10,... | collective-permute-start | bytes 1572872 | tf_op jit(solution)/shard_map/ppermute | solution.py:618
  75.1 6.4 %collective-permute-done.16.refs_1_ = bf16[2,72,1024]{2,1,0:T(8,128)(2,1)S(1)} collective-permute-done((bf16[2,72,1024]{2,1,0:T(8,128)(2,1)S(1)}, bf16[2,72,1024]{2,1,0:T(8,128)(2,1)S(1)}, u32[]{:S(2)}, u32[]{:S(2)}) %collective-permute-start.16) | collective-permute-done | bytes 294944 | tf_op jit(solution)/shard_map/ppermute | solution.py:488
  81.5 6.4 %collective-permute-done.17.refs_2_ = bf16[2,72,1024]{2,1,0:T(8,128)(2,1)S(1)} collective-permute-done((bf16[2,72,1024]{2,1,0:T(8,128)(2,1)S(1)}, bf16[2,72,1024]{2,1,0:T(8,128)(2,1)S(1)}, u32[]{:S(2)}, u32[]{:S(2)}) %collective-permute-start.17) | collective-permute-done | bytes 294944 | tf_op jit(solution)/shard_map/ppermute | solution.py:488
  92.2 6.5 %collective-permute-done.20.refs_1_ = bf16[2,72,1024]{2,1,0:T(8,128)(2,1)S(1)} collective-permute-done((bf16[2,72,1024]{2,1,0:T(8,128)(2,1)S(1)}, bf16[2,72,1024]{2,1,0:T(8,128)(2,1)S(1)}, u32[]{:S(2)}, u32[]{:S(2)}) %collective-permute-start.20) | collective-permute-done | bytes 294944 | tf_op jit(solution)/shard_map/ppermute | solution.py:488
  98.7 4.9 %collective-permute-done.21.refs_2_ = bf16[2,72,1024]{2,1,0:T(8,128)(2,1)S(1)} collective-permute-done((bf16[2,72,1024]{2,1,0:T(8,128)(2,1)S(1)}, bf16[2,72,1024]{2,1,0:T(8,128)(2,1)S(1)}, u32[]{:S(2)}, u32[]{:S(2)}) %collective-permute-start.21) | collective-permute-done | bytes 294944 | tf_op jit(solution)/shard_map/ppermute | solution.py:488
  109.9 5.7 %collective-permute-done.24.refs_1_ = bf16[2,72,1024]{2,1,0:T(8,128)(2,1)S(1)} collective-permute-done((bf16[2,72,1024]{2,1,0:T(8,128)(2,1)S(1)}, bf16[2,72,1024]{2,1,0:T(8,128)(2,1)S(1)}, u32[]{:S(2)}, u32[]{:S(2)}) %collective-permute-start.24) | collective-permute-done | bytes 294944 | tf_op jit(solution)/shard_map/ppermute | solution.py:488
  115.6 3.8 %collective-permute-done.25.refs_2_ = bf16[2,72,1024]{2,1,0:T(8,128)(2,1)S(1)} collective-permute-done((bf16[2,72,1024]{2,1,0:T(8,128)(2,1)S(1)}, bf16[2,72,1024]{2,1,0:T(8,128)(2,1)S(1)}, u32[]{:S(2)}, u32[]{:S(2)}) %collective-permute-start.25) | collective-permute-done | bytes 294944 | tf_op jit(solution)/shard_map/ppermute | solution.py:488
  123.7 7.1 %expert.4 = (bf16[2,72,1024]{2,1,0:T(8,128)(2,1)S(1)}, bf16[2,72,1024]{2,1,0:T(8,128)(2,1)S(1)}, bf16[2,72,1024]{2,1,0:T(8,128)(2,1)S(1)}, bf16[2,72,1024]{2,1,0:T(8,128)(2,1)S(1)}) custom-call(bf16[2,72,1024]{2,1,0:T(8,128)(2,1)S(1)} %get-tuple-element.201.refs_0_, bf16[2,72,1024]{2,1,0:T(8,128)(2,1)S(1)} %collective-permute-done.20.refs_1_, ...), custom_call_target="tpu_custom_call" | custom-call | flops 1000 | bytes 1000 | tf_op jit(solution)/shard_map/expert/pallas_call | solution.py:26
  130.8 3.3 %collective-permute-done.29.refs_3_ = bf16[2,72,1024]{2,1,0:T(8,128)(2,1)S(1)} collective-permute-done((bf16[2,72,1024]{2,1,0:T(8,128)(2,1)S(1)}, bf16[2,72,1024]{2,1,0:T(8,128)(2,1)S(1)}, u32[]{:S(2)}, u32[]{:S(2)}) %collective-permute-start.29) | collective-permute-done | bytes 294944 | tf_op jit(solution)/shard_map/ppermute | solution.py:488
  137.6 7.1 %expert.5 = (bf16[2,72,1024]{2,1,0:T(8,128)(2,1)S(1)}, bf16[2,72,1024]{2,1,0:T(8,128)(2,1)S(1)}, bf16[2,72,1024]{2,1,0:T(8,128)(2,1)S(1)}, bf16[2,72,1024]{2,1,0:T(8,128)(2,1)S(1)}) custom-call(bf16[2,72,1024]{2,1,0:T(8,128)(2,1)S(1)} %get-tuple-element.221.refs_0_, bf16[2,72,1024]{2,1,0:T(8,128)(2,1)S(1)} %collective-permute-done.24.refs_1_, ...), custom_call_target="tpu_custom_call" | custom-call | flops 1000 | bytes 1000 | tf_op jit(solution)/shard_map/expert/pallas_call | solution.py:26
  152.3 7.1 %expert.6 = (bf16[2,72,1024]{2,1,0:T(8,128)(2,1)S(1)}, bf16[2,72,1024]{2,1,0:T(8,128)(2,1)S(1)}, bf16[2,72,1024]{2,1,0:T(8,128)(2,1)S(1)}, bf16[2,72,1024]{2,1,0:T(8,128)(2,1)S(1)}) custom-call(bf16[2,72,1024]{2,1,0:T(8,128)(2,1)S(1)} %get-tuple-element.238.refs_0_, bf16[2,72,1024]{2,1,0:T(8,128)(2,1)S(1)} %collective-permute-done.27.refs_1_, ...), custom_call_target="tpu_custom_call" | custom-call | flops 1000 | bytes 1000 | tf_op jit(solution)/shard_map/expert/pallas_call | solution.py:26
  167.4 7.1 %expert.7 = (bf16[2,72,1024]{2,1,0:T(8,128)(2,1)S(1)}, bf16[2,72,1024]{2,1,0:T(8,128)(2,1)S(1)}, bf16[2,72,1024]{2,1,0:T(8,128)(2,1)S(1)}, bf16[2,72,1024]{2,1,0:T(8,128)(2,1)S(1)}) custom-call(bf16[2,72,1024]{2,1,0:T(8,128)(2,1)S(1)} %get-tuple-element.256.refs_0_, bf16[2,72,1024]{2,1,0:T(8,128)(2,1)S(1)} %collective-permute-done.16.refs_1_, ...), custom_call_target="tpu_custom_call" | custom-call | flops 1000 | bytes 1000 | tf_op jit(solution)/shard_map/expert/pallas_call | solution.py:26
  178.7 2.8 %collective-permute-start.41 = (bf16[2,72,1024]{2,1,0:T(8,128)(2,1)S(1)}, bf16[2,72,1024]{2,1,0:T(8,128)(2,1)S(1)}, u32[]{:S(2)}, u32[]{:S(2)}) collective-permute-start(bf16[2,72,1024]{2,1,0:T(8,128)(2,1)S(1)} %get-tuple-element.265), channel_id=1, source_target_pairs={{0,8},{8,0},{16,24},{24,16},{1,9},{9,1},{17,25},{25,17},{2,10},{10... | collective-permute-start | bytes 884744 | tf_op jit(solution)/shard_map/ppermute | solution.py:488
  186.2 5.2 %collective-permute-done.42.refs_2_ = bf16[2,72,1024]{2,1,0:T(8,128)(2,1)S(1)} collective-permute-done((bf16[2,72,1024]{2,1,0:T(8,128)(2,1)S(1)}, bf16[2,72,1024]{2,1,0:T(8,128)(2,1)S(1)}, u32[]{:S(2)}, u32[]{:S(2)}) %collective-permute-start.42) | collective-permute-done | bytes 294944 | tf_op jit(solution)/shard_map/ppermute | solution.py:488
  (148 shorter events, 77.1 us)
Async XLA Ops:
  1.4 13.8 %collective-permute-start.2 = (bf16[128,1024]{1,0:T(8,128)(2,1)S(1)}, bf16[128,1024]{1,0:T(8,128)(2,1)S(1)}, u32[]{:S(2)}, u32[]{:S(2)}) collective-permute-start(bf16[128,1024]{1,0:T(8,128)(2,1)S(1)} %get-tuple-element.146), channel_id=1, source_target_pairs={{0,1},{1,0},{2,3},{3,2},{4,5},{5,4},{6,7},{7,6},{8,9},{9,8},{10,11... | collective-permute-start | bytes 786440 | tf_op jit(solution)/shard_map/ppermute | solution.py:514
  16.9 16.6 %collective-permute-start.5 = (bf16[4,144,256]{2,1,0:T(8,128)(2,1)}, bf16[4,144,256]{2,1,0:T(8,128)(2,1)S(1)}, u32[]{:S(2)}, u32[]{:S(2)}) collective-permute-start(bf16[4,144,256]{2,1,0:T(8,128)(2,1)} %pair.4.refs_0_), channel_id=1, source_target_pairs={{0,8},{8,0},{16,24},{24,16},{1,9},{9,1},{17,25},{25,17},{2,10},{10... | collective-permute-start | bytes 884744 | tf_op jit(solution)/shard_map/ppermute | solution.py:488
  22.4 23.0 %collective-permute-start.6 = (bf16[4,144,256]{2,1,0:T(8,128)(2,1)}, bf16[4,144,256]{2,1,0:T(8,128)(2,1)}, u32[]{:S(2)}, u32[]{:S(2)}) collective-permute-start(bf16[4,144,256]{2,1,0:T(8,128)(2,1)} %pair.4.refs_0_), channel_id=1, source_target_pairs={{0,16},{8,24},{16,0},{24,8},{1,17},{9,25},{17,1},{25,9},{2,18},{10... | collective-permute-start | bytes 884744 | tf_op jit(solution)/shard_map/ppermute | solution.py:488
  27.8 17.5 %collective-permute-start.7 = (bf16[4,144,256]{2,1,0:T(8,128)(2,1)}, bf16[4,144,256]{2,1,0:T(8,128)(2,1)}, u32[]{:S(2)}, u32[]{:S(2)}) collective-permute-start(bf16[4,144,256]{2,1,0:T(8,128)(2,1)} %pair.4.refs_0_), channel_id=1, source_target_pairs={{0,24},{8,16},{16,8},{24,0},{1,25},{9,17},{17,9},{25,1},{2,26},{10... | collective-permute-start | bytes 884744 | tf_op jit(solution)/shard_map/ppermute | solution.py:488
  31.5 13.9 %collective-permute-start.10 = (bf16[4,144,256]{2,1,0:T(8,128)(2,1)}, bf16[4,144,256]{2,1,0:T(8,128)(2,1)}, u32[]{:S(2)}, u32[]{:S(2)}) collective-permute-start(bf16[4,144,256]{2,1,0:T(8,128)(2,1)} %pair.5.refs_1_), channel_id=1, source_target_pairs={{0,24},{8,16},{16,8},{24,0},{1,25},{9,17},{17,9},{25,1},{2,26},{10... | collective-permute-start | bytes 884744 | tf_op jit(solution)/shard_map/ppermute | solution.py:488
  32.1 15.9 %collective-permute-start.8 = (bf16[4,144,256]{2,1,0:T(8,128)(2,1)}, bf16[4,144,256]{2,1,0:T(8,128)(2,1)}, u32[]{:S(2)}, u32[]{:S(2)}) collective-permute-start(bf16[4,144,256]{2,1,0:T(8,128)(2,1)} %pair.5.refs_1_), channel_id=1, source_target_pairs={{0,8},{8,0},{16,24},{24,16},{1,9},{9,1},{17,25},{25,17},{2,10},{10... | collective-permute-start | bytes 884744 | tf_op jit(solution)/shard_map/ppermute | solution.py:488
  34.2 14.7 %collective-permute-start.9 = (bf16[4,144,256]{2,1,0:T(8,128)(2,1)}, bf16[4,144,256]{2,1,0:T(8,128)(2,1)}, u32[]{:S(2)}, u32[]{:S(2)}) collective-permute-start(bf16[4,144,256]{2,1,0:T(8,128)(2,1)} %pair.5.refs_1_), channel_id=1, source_target_pairs={{0,16},{8,24},{16,0},{24,8},{1,17},{9,25},{17,1},{25,9},{2,18},{10... | collective-permute-start | bytes 884744 | tf_op jit(solution)/shard_map/ppermute | solution.py:488
  48.8 18.7 %collective-permute-start.12 = (bf16[1,2048,768]{2,1,0:T(8,128)(2,1)S(1)}, bf16[1,2048,768]{2,1,0:T(8,128)(2,1)S(1)}, u32[]{:S(2)}, u32[]{:S(2)}) collective-permute-start(bf16[1,2048,768]{2,1,0:T(8,128)(2,1)S(1)} %copy-done), channel_id=1, source_target_pairs={{0,1},{1,0},{2,3},{3,2},{4,5},{5,4},{6,7},{7,6},{8,9},{9,8},{10,11... | collective-permute-start | bytes 9437192 | tf_op jit(solution)/shard_map/ppermute | solution.py:547
  48.9 18.7 %collective-permute-start.13 = (bf16[1,2048,768]{2,1,0:T(8,128)(2,1)}, bf16[1,2048,768]{2,1,0:T(8,128)(2,1)S(1)}, u32[]{:S(2)}, u32[]{:S(2)}) collective-permute-start(bf16[1,2048,768]{2,1,0:T(8,128)(2,1)} %refs_5_.3), channel_id=1, source_target_pairs={{0,1},{1,0},{2,3},{3,2},{4,5},{5,4},{6,7},{7,6},{8,9},{9,8},{10,11... | collective-permute-start | bytes 9437192 | tf_op jit(solution)/shard_map/ppermute | solution.py:547
  49.4 18.2 %collective-permute-start.14 = (bf16[1,768,2048]{2,1,0:T(8,128)(2,1)}, bf16[1,768,2048]{2,1,0:T(8,128)(2,1)S(1)}, u32[]{:S(2)}, u32[]{:S(2)}) collective-permute-start(bf16[1,768,2048]{2,1,0:T(8,128)(2,1)} %refs_6_.3), channel_id=1, source_target_pairs={{0,1},{1,0},{2,3},{3,2},{4,5},{5,4},{6,7},{7,6},{8,9},{9,8},{10,11... | collective-permute-start | bytes 9437192 | tf_op jit(solution)/shard_map/ppermute | solution.py:547
  67.5 20.3 %collective-permute-start.15 = (bf16[128,2048]{1,0:T(8,128)(2,1)S(1)}, bf16[128,2048]{1,0:T(8,128)(2,1)S(1)}, u32[]{:S(2)}, u32[]{:S(2)}) collective-permute-start(bf16[128,2048]{1,0:T(8,128)(2,1)S(1)} %get-tuple-element.177.x_ref), channel_id=1, source_target_pairs={{0,2},{1,3},{2,6},{3,7},{6,4},{7,5},{4,0},{5,1},{8,10},{9,11},{10,... | collective-permute-start | bytes 1572872 | tf_op jit(solution)/shard_map/ppermute | solution.py:618
  73.1 14.8 %collective-permute-start.17 = (bf16[2,72,1024]{2,1,0:T(8,128)(2,1)S(1)}, bf16[2,72,1024]{2,1,0:T(8,128)(2,1)S(1)}, u32[]{:S(2)}, u32[]{:S(2)}) collective-permute-start(bf16[2,72,1024]{2,1,0:T(8,128)(2,1)S(1)} %get-tuple-element.181), channel_id=1, source_target_pairs={{0,16},{8,24},{16,0},{24,8},{1,17},{9,25},{17,1},{25,9},{2,18},{10... | collective-permute-start | bytes 884744 | tf_op jit(solution)/shard_map/ppermute | solution.py:488
  74.6 13.3 %collective-permute-start.18 = (bf16[2,72,1024]{2,1,0:T(8,128)(2,1)S(1)}, bf16[2,72,1024]{2,1,0:T(8,128)(2,1)S(1)}, u32[]{:S(2)}, u32[]{:S(2)}) collective-permute-start(bf16[2,72,1024]{2,1,0:T(8,128)(2,1)S(1)} %get-tuple-element.182), channel_id=1, source_target_pairs={{0,24},{8,16},{16,8},{24,0},{1,25},{9,17},{17,9},{25,1},{2,26},{10... | collective-permute-start | bytes 884744 | tf_op jit(solution)/shard_map/ppermute | solution.py:488
  87.9 15.7 %collective-permute-start.19 = (bf16[128,2048]{1,0:T(8,128)(2,1)S(1)}, bf16[128,2048]{1,0:T(8,128)(2,1)S(1)}, u32[]{:S(2)}, u32[]{:S(2)}) collective-permute-start(bf16[128,2048]{1,0:T(8,128)(2,1)S(1)} %collective-permute-done.15.x_ref), channel_id=1, source_target_pairs={{0,2},{1,3},{2,6},{3,7},{6,4},{7,5},{4,0},{5,1},{8,10},{9,11},{10,... | collective-permute-start | bytes 1572872 | tf_op jit(solution)/shard_map/ppermute | solution.py:618
  89.9 13.7 %collective-permute-start.21 = (bf16[2,72,1024]{2,1,0:T(8,128)(2,1)S(1)}, bf16[2,72,1024]{2,1,0:T(8,128)(2,1)S(1)}, u32[]{:S(2)}, u32[]{:S(2)}) collective-permute-start(bf16[2,72,1024]{2,1,0:T(8,128)(2,1)S(1)} %get-tuple-element.187), channel_id=1, source_target_pairs={{0,16},{8,24},{16,0},{24,8},{1,17},{9,25},{17,1},{25,9},{2,18},{10... | collective-permute-start | bytes 884744 | tf_op jit(solution)/shard_map/ppermute | solution.py:488
  90.7 12.9 %collective-permute-start.22 = (bf16[2,72,1024]{2,1,0:T(8,128)(2,1)S(1)}, bf16[2,72,1024]{2,1,0:T(8,128)(2,1)S(1)}, u32[]{:S(2)}, u32[]{:S(2)}) collective-permute-start(bf16[2,72,1024]{2,1,0:T(8,128)(2,1)S(1)} %get-tuple-element.188), channel_id=1, source_target_pairs={{0,24},{8,16},{16,8},{24,0},{1,25},{9,17},{17,9},{25,1},{2,26},{10... | collective-permute-start | bytes 884744 | tf_op jit(solution)/shard_map/ppermute | solution.py:488
  103.6 16.1 %collective-permute-start.23 = (bf16[128,2048]{1,0:T(8,128)(2,1)S(1)}, bf16[128,2048]{1,0:T(8,128)(2,1)S(1)}, u32[]{:S(2)}, u32[]{:S(2)}) collective-permute-start(bf16[128,2048]{1,0:T(8,128)(2,1)S(1)} %collective-permute-done.19.x_ref), channel_id=1, source_target_pairs={{0,2},{1,3},{2,6},{3,7},{6,4},{7,5},{4,0},{5,1},{8,10},{9,11},{10,... | collective-permute-start | bytes 1572872 | tf_op jit(solution)/shard_map/ppermute | solution.py:618
  107.1 12.4 %collective-permute-start.25 = (bf16[2,72,1024]{2,1,0:T(8,128)(2,1)S(1)}, bf16[2,72,1024]{2,1,0:T(8,128)(2,1)S(1)}, u32[]{:S(2)}, u32[]{:S(2)}) collective-permute-start(bf16[2,72,1024]{2,1,0:T(8,128)(2,1)S(1)} %get-tuple-element.193), channel_id=1, source_target_pairs={{0,16},{8,24},{16,0},{24,8},{1,17},{9,25},{17,1},{25,9},{2,18},{10... | collective-permute-start | bytes 884744 | tf_op jit(solution)/shard_map/ppermute | solution.py:488
  134.1 12.0 %collective-permute-start.30 = (bf16[2,72,1024]{2,1,0:T(8,128)(2,1)S(1)}, bf16[2,72,1024]{2,1,0:T(8,128)(2,1)S(1)}, u32[]{:S(2)}, u32[]{:S(2)}) collective-permute-start(bf16[2,72,1024]{2,1,0:T(8,128)(2,1)S(1)} %get-tuple-element.218), channel_id=1, source_target_pairs={{0,8},{8,0},{16,24},{24,16},{1,9},{9,1},{17,25},{25,17},{2,10},{10... | collective-permute-start | bytes 884744 | tf_op jit(solution)/shard_map/ppermute | solution.py:488
  147.2 13.7 %collective-permute-start.36 = (bf16[128,2048]{1,0:T(8,128)(2,1)S(1)}, bf16[128,2048]{1,0:T(8,128)(2,1)S(1)}, u32[]{:S(2)}, u32[]{:S(2)}) collective-permute-start(bf16[128,2048]{1,0:T(8,128)(2,1)S(1)} %spread.4), channel_id=1, source_target_pairs={{0,2},{1,3},{2,6},{3,7},{6,4},{7,5},{4,0},{5,1},{8,10},{9,11},{10,... | collective-permute-start | bytes 1572872 | tf_op jit(solution)/shard_map/ppermute | solution.py:628
  148.8 12.0 %collective-permute-start.33 = (bf16[2,72,1024]{2,1,0:T(8,128)(2,1)S(1)}, bf16[2,72,1024]{2,1,0:T(8,128)(2,1)S(1)}, u32[]{:S(2)}, u32[]{:S(2)}) collective-permute-start(bf16[2,72,1024]{2,1,0:T(8,128)(2,1)S(1)} %get-tuple-element.230), channel_id=1, source_target_pairs={{0,8},{8,0},{16,24},{24,16},{1,9},{9,1},{17,25},{25,17},{2,10},{10... | collective-permute-start | bytes 884744 | tf_op jit(solution)/shard_map/ppermute | solution.py:488
  161.9 15.8 %collective-permute-start.40 = (bf16[128,2048]{1,0:T(8,128)(2,1)S(1)}, bf16[128,2048]{1,0:T(8,128)(2,1)S(1)}, u32[]{:S(2)}, u32[]{:S(2)}) collective-permute-start(bf16[128,2048]{1,0:T(8,128)(2,1)S(1)} %spread.5), channel_id=1, source_target_pairs={{0,2},{1,3},{2,6},{3,7},{6,4},{7,5},{4,0},{5,1},{8,10},{9,11},{10,... | collective-permute-start | bytes 1572872 | tf_op jit(solution)/shard_map/ppermute | solution.py:628
  163.9 12.0 %collective-permute-start.37 = (bf16[2,72,1024]{2,1,0:T(8,128)(2,1)S(1)}, bf16[2,72,1024]{2,1,0:T(8,128)(2,1)S(1)}, u32[]{:S(2)}, u32[]{:S(2)}) collective-permute-start(bf16[2,72,1024]{2,1,0:T(8,128)(2,1)S(1)} %get-tuple-element.247), channel_id=1, source_target_pairs={{0,8},{8,0},{16,24},{24,16},{1,9},{9,1},{17,25},{25,17},{2,10},{10... | collective-permute-start | bytes 884744 | tf_op jit(solution)/shard_map/ppermute | solution.py:488
  178.6 12.8 %collective-permute-start.44 = (bf16[128,2048]{1,0:T(8,128)(2,1)S(1)}, bf16[128,2048]{1,0:T(8,128)(2,1)S(1)}, u32[]{:S(2)}, u32[]{:S(2)}) collective-permute-start(bf16[128,2048]{1,0:T(8,128)(2,1)S(1)} %spread.6), channel_id=1, source_target_pairs={{0,2},{1,3},{2,6},{3,7},{6,4},{7,5},{4,0},{5,1},{8,10},{9,11},{10,... | collective-permute-start | bytes 1572872 | tf_op jit(solution)/shard_map/ppermute | solution.py:628
  (49 other events, 482.8 us)

commit v5 on v4

--- a/solution.py
+++ b/solution.py
@@ -37,18 +37,16 @@
     )(*scalars, *operands, *unused)
 
 
-def message_kernel(core_ref, key_ref, value_ref, ids_ref, gates_ref, seg_ref, keep, give):
-    tok = key_ref.shape[0]
+def message_kernel(core_ref, kv_ref, small_ref, keep, give):
+    tok = kv_ref.shape[0]
+    top_count = small_ref.shape[0] // 3
     first = core_ref[0] == 0
-    k0, k1 = (key_ref[:, i * HEAD_SIZE : (i + 1) * HEAD_SIZE] for i in range(2))
-    v0, v1 = (
-        value_ref[:, i * HEAD_SIZE : (i + 1) * HEAD_SIZE].astype(F32).T.astype(BF16)
-        for i in range(2)
-    )
-    share = gates_ref[...] / jnp.sum(gates_ref[...], axis=0, keepdims=True)
+    k0, k1, v0, v1 = (kv_ref[:, i * HEAD_SIZE : (i + 1) * HEAD_SIZE] for i in range(4))
+    v0, v1 = (v.astype(F32).T.astype(BF16) for v in (v0, v1))
+    ids, gates, segs = (small_ref[i * top_count : (i + 1) * top_count] for i in range(3))
+    share = gates / jnp.sum(gates, axis=0, keepdims=True)
     share_hi = share.astype(BF16).astype(F32)
-    segs = jnp.broadcast_to(seg_ref[...].astype(F32), share.shape)
-    left = jnp.concatenate([ids_ref[...].astype(F32), share_hi], axis=0)
+    left = jnp.concatenate([ids, share_hi], axis=0)
     right = jnp.concatenate([share - share_hi, segs], axis=0)
     small = jnp.concatenate([left, right], axis=1).astype(BF16)
     keep[:tok, :HEAD_SIZE] = jnp.where(first, k0, k1)
@@ -99,24 +97,29 @@
         own_ref, near_ref, top_ref, sum_ref, acc_ref, *refs = refs
     else:
         top_ref, sum_ref, acc_ref, *refs = refs
-    seg_ref, pre_ref, table, segs_ref, sem, q_ref = refs
+    seg_ref, pre_ref, table, flags, flags_ref, sem, q_ref = refs
     columns, rows = q_own.shape[1], home_ref.shape[1] - 16
     each = kv_refs[0].shape[0]
     for tile in range(2 + each * len(pieces)):
         ref, at = (home_ref, tile) if tile < 2 else (kv_refs[(tile - 2) // each], (tile - 2) % each)
         seg_ref[tile] = small_part(ref, at, rows)[3]
         table[tile : tile + 1, :] = seg_ref[tile].astype(jnp.int32)
-    copy = pltpu.make_async_copy(table, segs_ref, sem)
+    low, high = table[:, :1], table[:, rows - 1 :]
+    for g in range(2):
+        segs = table[g : g + 1, :]
+        prefix = jnp.zeros_like(segs)
+        for s in range(prefix_ref.shape[0]):
+            prefix = jnp.where(segs == s, prefix_ref[s], prefix)
+        pre_ref[g] = prefix.astype(F32)
+        found = jnp.maximum(
+            jnp.where((segs >= low) & (segs <= high), 1, 0),
+            jnp.where((prefix >= low) & (prefix <= high), 1, 0),
+        )
+        found = jnp.max(found.astype(F32), axis=1, keepdims=True)
+        flags[g] = jnp.broadcast_to(found, table.shape).astype(jnp.int32)
+    copy = pltpu.make_async_copy(flags, flags_ref, sem)
     copy.start()
     copy.wait()
-    for g in range(2):
-
-        def prefixes(s, row, g=g):
-            return jnp.where(seg_ref[g] == s.astype(F32), prefix_ref[s].astype(F32), row)
-
-        pre_ref[g] = lax.fori_loop(
-            segs_ref[g, 0], segs_ref[g, rows - 1] + 1, prefixes, jnp.zeros((1, rows), F32)
-        )
     chips = len(order)
     scale = math.log2(math.e) / math.sqrt(HEAD_SIZE)
     width = 2 * rows
@@ -145,17 +148,8 @@
             at, g = i // 2, i % 2
             tile = 2 + each * number + at
             key_start, query_start = start_of(k + at // 2, m, at % 2), start_of(0, 0, g)
-            low, high = segs_ref[tile, 0], segs_ref[tile, rows - 1]
-            query_low, query_high = segs_ref[g, 0], segs_ref[g, rows - 1]
-
-            def shared(s, found):
-                prefix = prefix_ref[s]
-                return found | ((prefix >= low) & (prefix <= high)).astype(jnp.int32)
-
-            own = ((low <= query_high) & (high >= query_low)).astype(jnp.int32)
-            seen = lax.fori_loop(query_low, query_high + 1, shared, own)
-
-            @pl.when((seen > 0) & (key_start <= query_start))
+
+            @pl.when((flags_ref[g, tile, 0] > 0) & (key_start <= query_start))
             def _():
                 square = (rows, rows)
                 key_pos = key_start + lax.broadcasted_iota(jnp.int32, square, 0)
@@ -201,7 +195,7 @@
     head, columns = q_own.shape
     rows = home.shape[1] - 16
     tiles = 2 + kv_list[0].shape[0] * len(kv_list)
-    first = state is None
+    first = not state
     state_shapes = [
         jax.ShapeDtypeStruct((2, 1, columns), F32),
         jax.ShapeDtypeStruct((2, 1, columns), F32),
@@ -211,7 +205,8 @@
         pltpu.VMEM((tiles, 1, rows), F32),
         pltpu.VMEM((2, 1, rows), F32),
         pltpu.VMEM((tiles, rows), jnp.int32),
-        pltpu.SMEM((tiles, rows), jnp.int32),
+        pltpu.VMEM((2, tiles, rows), jnp.int32),
+        pltpu.SMEM((2, tiles, rows), jnp.int32),
         pltpu.SemaphoreType.DMA,
         pltpu.VMEM((2, head, columns), BF16),
     ]
@@ -227,73 +222,39 @@
         [q_own, q_near, home, *kv_list, *(() if first else state)],
         scalars=scalars,
         scratch=scratch,
-        vmem_mib=5 + len(kv_list) // 2,
+        vmem_mib=5 + len(kv_list) // 4,
         flops=8_000_000_000 if last else 1000,
     )
 
 
 def project_kernel(
-    core_ref, own_ref, got_ref, hidden_ref, gain_ref, weight_hbm, mixed_ref, out_ref, weight_ref, sems
+    core_ref, own_ref, got_ref, weight_ref, hidden_ref, gain_ref, mixed_ref, left_ref, right_ref
 ):
     core = core_ref[0]
     half = own_ref.shape[1]
     width = hidden_ref.shape[1]
-    blocks = sems.shape[0]
-    block = width // blocks
+    block = math.gcd(width, 512)
     own_at = pl.multiple_of(core * half, half)
     got_at = pl.multiple_of((1 - core) * half, half)
-    copies = [
-        pltpu.make_async_copy(
-            weight_hbm.at[:, pl.ds(i * block, block)], weight_ref.at[i], sems.at[i]
-        )
-        for i in range(blocks)
-    ]
-    for copy in copies:
-        copy.start()
     total = jnp.zeros((own_ref.shape[0], 1), F32)
-    for i, copy in enumerate(copies):
-        part = pl.ds(i * block, block)
-        copy.wait()
+    for at in range(0, width, block):
+        part = pl.ds(at, block)
         now = (
             hidden_ref[:, part].astype(F32)
             + jnp.dot(
-                own_ref[...], weight_ref[i, pl.ds(own_at, half), :], preferred_element_type=F32
+                own_ref[...], weight_ref[pl.ds(own_at, half), part], preferred_element_type=F32
             )
             + jnp.dot(
-                got_ref[...], weight_ref[i, pl.ds(got_at, half), :], preferred_element_type=F32
+                got_ref[...], weight_ref[pl.ds(got_at, half), part], preferred_element_type=F32
             )
         )
         mixed_ref[:, part] = now
         total = total + jnp.sum(now * now, axis=1, keepdims=True)
     factor = lax.rsqrt(total / width + 1e-06)
-    out_ref[...] = (mixed_ref[...] * factor * gain_ref[...]).astype(BF16)
-
-
-def fetch_kernel(count, *refs):
-    sources, targets, sems = refs[:count], refs[-count - 1 : -1], refs[-1]
-    copies = [
-        pltpu.make_async_copy(source, target, sems.at[i])
-        for i, (source, target) in enumerate(zip(sources, targets, strict=True))
-    ]
-    for copy in copies:
-        copy.start()
-    for copy in copies:
-        copy.wait()
-
-
-def fetch(arrays, after):
-    count = len(arrays)
-    hbm = pl.BlockSpec(memory_space=pltpu.HBM)
-    return pl.pallas_call(
-        functools.partial(fetch_kernel, count),
-        out_shape=[jax.ShapeDtypeStruct(x.shape, x.dtype) for x in arrays],
-        in_specs=[hbm] * (count + len(after)),
-        out_specs=[pl.BlockSpec(memory_space=pltpu.VMEM)] * count,
-        scratch_shapes=[pltpu.SemaphoreType.DMA((count,))],
-        compiler_params=pltpu.CompilerParams(vmem_limit_bytes=4 * 1024 * 1024),
-        cost_estimate=pl.CostEstimate(flops=1000, bytes_accessed=1000, transcendentals=0),
-        name="fetch",
-    )(*arrays, *after)
+    side = width // 2
+    for at, out_ref in ((0, left_ref), (side, right_ref)):
+        part = pl.ds(at, side)
+        out_ref[...] = (mixed_ref[:, part] * factor * gain_ref[:, part]).astype(BF16)
 
 
 def sort_rows(kv_ref, where_ref, top_count, n_blk, n_uly):
@@ -339,10 +300,10 @@
 
 
 def slots_kernel(top_count, capacity, pack, n_blk, n_uly, where_ref, *refs):
-    chips = (len(refs) - 2) // 2
+    chips = (len(refs) - 3) // 2
     unpack_ref, repack_ref = refs[-2:]
     targets = 2 * n_blk
-    for kv_ref, rank_ref in zip(refs[:chips], refs[chips:-2], strict=True):
+    for kv_ref, rank_ref in zip(refs[:chips], refs[chips + 1 : -2], strict=True):
         rank = sort_rows(kv_ref, where_ref, top_count, n_blk, n_uly)[0].astype(jnp.int32)
         for target in range(targets):
             rank_ref[target] = rank[target : target + 1]
@@ -355,8 +316,9 @@
             ref[part] = jnp.where(same, 1.0, 0.0).astype(BF16)
 
 
-def pick_kernel(capacity, pack, x_ref, rank_ref, *refs):
-    targets, tok = rank_ref.shape[0], x_ref.shape[0]
+def pick_kernel(capacity, pack, left_ref, right_ref, rank_ref, *refs):
+    targets, tok = rank_ref.shape[0], left_ref.shape[0]
+    half = left_ref.shape[1]
     outs = refs[-(targets // 2) :]
     _, slots, width = outs[0].shape
     slot = lax.broadcasted_iota(jnp.int32, (slots, tok), 0)
@@ -372,7 +334,13 @@
     block = math.gcd(width, 512)
     for at in range(0, width, block):
         parts = jnp.concatenate(
-            [x_ref[:, q * width + at : q * width + at + block] for q in range(pack)], axis=0
+            [
+                (left_ref, right_ref)[(q * width + at) // half][
+                    :, (q * width + at) % half : (q * width + at) % half + block
+                ]
+                for q in range(pack)
+            ],
+            axis=0,
         )
         rows = jnp.dot(chosen, parts, preferred_element_type=F32)
         for t in range(targets):
@@ -434,20 +402,27 @@
 
 def spread_kernel(n_blk, pack, added, *refs):
     backs, weight_ref, adds = refs[:n_blk], refs[n_blk], refs[n_blk + 1 : n_blk + 1 + added]
-    out_ref, mail_ref = refs[-2:]
+    *outs, mail_ref = refs[n_blk + 1 + added :]
     _, slots, part_width = backs[0].shape
-    tok = out_ref.shape[0]
+    tok, full = outs[0].shape[0], pack * part_width
     mails = [r[j].astype(F32) for r in backs for j in range(2)]
     mail_ref[...] = jnp.concatenate(mails, axis=0).astype(BF16)
     block = math.gcd(part_width, 512)
+
+    def columns(arrays, at):
+        side = full // len(arrays)
+        return arrays[at // side].at[:, at % side : at % side + block]
+
+    whole = [[r] for r in adds if r.shape[1] == full]
+    halves = [r for r in adds if r.shape[1] < full]
     for q in range(pack):
         for at in range(0, part_width, block):
             both = jnp.dot(weight_ref[q], mail_ref[:, at : at + block], preferred_element_type=F32)
-            to = slice(q * part_width + at, q * part_width + at + block)
-            total = both[:tok] + both[tok:]
-            for ref in adds:
-                total = total + ref[:, to].astype(F32)
-            out_ref[:, to] = total.astype(BF16)
+            to = q * part_width + at
+            sums = both[:tok] + both[tok:]
+            for arrays in whole + ([halves] if halves else []):
+                sums = sums + columns(arrays, to)[...].astype(F32)
+            columns(outs, to)[...] = sums.astype(BF16)
 
 
 def shards(
@@ -498,29 +473,56 @@
         message_kernel,
         "message",
         [shape(tok + 16, 2 * HEAD_SIZE)] * 2,
-        [keys, values, expert_ids.T, gates.T, segment_ids[None, :]],
+        [
+            jnp.concatenate([keys, values], axis=1),
+            jnp.concatenate(
+                [
+                    expert_ids.T.astype(F32),
+                    gates.T,
+                    jnp.broadcast_to(segment_ids.astype(F32), (top_count, tok)),
+                ]
+            ),
+        ],
         scalars=[core_here],
     )
     where = jnp.stack([blk, uly]).astype(jnp.int32)
-    q_keep, q_give = call(
-        turn_kernel, "turn", [shape(HEAD_SIZE, columns)] * 2, [queries], scalars=[core_here]
-    )
+    [keep, give], [where] = tied([keep, give], [where])
     kv_steps = [
         call(pair_kernel, "pair", shape(2, tok + 16, 2 * HEAD_SIZE), [keep, other_core(give)])
     ]
-    groups, kv_far = [], []
-    for k in range(1, chips):
-        kv_next = next_chip(kv_steps[-1])
-        beside = [q_keep, other_core(q_give)] if k == 1 else []
-        kv_next, *beside = lax.optimization_barrier((kv_next, *beside))
-        if k == 1:
-            q_keep, q_near = beside
-        kv_steps.append(kv_next)
-        if k % 2:
-            groups.append(
-                call(pair_kernel, "pair", shape(4, tok + 16, 2 * HEAD_SIZE), kv_steps[-2:])
-            )
-            kv_far.append([other_block(groups[-1], m) for m in range(1, n_blk)])
+    [queries], _ = tied([queries], [kv_steps[0]])
+    q_keep, q_give = call(
+        turn_kernel, "turn", [shape(HEAD_SIZE, columns)] * 2, [queries], scalars=[core_here]
+    )
+    scalars = [where, prefix_ids]
+
+    def attend_some(pieces, state, last):
+        refs = [kv_far[k][m - 1] if m else kv_steps[k] for k, m in pieces]
+        return attend(
+            refs, pieces, order, n_blk, scalars, q_keep, q_near, kv_steps[0], state, last
+        )
+
+    kv_far, mine, near, state = [], [w_gate, w_up, w_down], [], None
+    for k in range(chips):
+        far = [other_block(kv_steps[k], m) for m in range(1, n_blk)]
+        kv_next = [next_chip(kv_steps[k])] if k < chips - 1 else []
+        beside = [q_keep, other_core(q_give)] if k == 0 else []
+        if k >= chips - 2:
+            here = mine[:1] if k == chips - 2 else mine[len(near) :]
+            here, _ = tied(here, [kv_steps[k]])
+            beside = beside + [other_core(w) for w in here]
+        if k > 0:
+            own = [(0, 0), (1, 0)] if k == 1 else [(k, 0)]
+            state = attend_some([*own, *((k - 1, m) for m in range(1, n_blk))], state, False)
+        kv_next, far, beside, state = tied(kv_next, far, beside, state or [])
+        kv_steps += kv_next
+        kv_far.append(far)
+        if k == 0:
+            q_keep, q_near = beside[:2]
+        if k >= chips - 2:
+            near += beside[2:] if k == 0 else beside
+    last_pieces = [(chips - 1, m) for m in range(1, n_blk)]
+    attended, for_near = attend_some(last_pieces, state, True)
     capacity = max(2, 9 * tok * top_count // (8 * experts_all))
     pack = 8 // math.gcd(capacity, 8)
     slots, part_width = capacity * pack, model_width // pack
@@ -533,52 +535,22 @@
         + [shape(pack, half_rows, n_blk * slots), shape(pack, n_blk * slots, half_rows)],
         kv_steps,
         scalars=[where],
+        unused=[for_near],
         vmem_mib=3 + pack * pack // 2,
     )
-    scalars = [where, prefix_ids]
-    pieces = [(k, 0) for k in range(0, chips, 2)]
-    state = attend(
-        groups, pieces, order, n_blk, scalars, q_keep, q_near, kv_steps[0], None, False
-    )
-    *ranks, unpack, repack, a, b, c, x, y, z = lax.optimization_barrier(
-        [*ranks, unpack, repack, *state, w_gate, w_up, w_down]
-    )
-    (x, y, z), *kv_far = tied([x, y, z], *kv_far)
-    mine, near = [x, y, z], [other_core(w) for w in (x, y, z)]
-    pieces = [(k, m) for k in range(0, chips, 2) for m in range(1, n_blk)]
-    attended, for_near = attend(
-        [kv for group in kv_far for kv in group],
-        pieces,
-        order,
-        n_blk,
-        scalars,
-        q_keep,
-        q_near,
-        kv_steps[0],
-        [a, b, c],
-        True,
-    )
-    blocks = max(1, model_width // 512)
-    mixed, normed = call(
+    mixed, *normed = call(
         project_kernel,
         "project",
-        [shape(tok, model_width, dtype=F32), shape(tok, model_width)],
-        [attended, other_core(for_near), hidden_in, post_gain[None, :]],
+        [shape(tok, model_width, dtype=F32)] + [shape(tok, model_width // 2)] * 2,
+        [attended, other_core(for_near), o_weight, hidden_in, post_gain[None, :]],
         scalars=[core_here],
-        unused=[o_weight],
-        scratch=[
-            pltpu.VMEM((blocks, o_weight.shape[0], model_width // blocks), BF16),
-            pltpu.SemaphoreType.DMA((blocks,)),
-        ],
-        vmem_mib=12,
-        flops=4_000_000_000,
     )
 
     halves = shape(2, slots, part_width)
 
     def pick(k, rows):
         kernel = functools.partial(pick_kernel, capacity, pack)
-        return call(kernel, "pick", [halves] * n_blk, [rows, ranks[k]])
+        return call(kernel, "pick", [halves] * n_blk, [*rows, ranks[k]])
 
     def expert(inbox):
         return call(
@@ -595,12 +567,12 @@
             vmem_mib=6 + pack,
         )
 
-    def spread(k, back, adds):
+    def spread(k, back, adds, last):
         return call(
             functools.partial(spread_kernel, n_blk, pack, len(adds)),
             "spread",
-            shape(tok, model_width),
-            [*back, weights[k], *adds],
+            shape(tok, model_width) if last else [shape(tok, model_width // 2)] * 2,
+            [*back, *weights[k], *adds],
             scratch=[pltpu.VMEM((targets * slots, part_width), BF16)],
             vmem_mib=2 + pack,
         )
@@ -609,13 +581,16 @@
         return [other_block(x, m) if m else x for m, x in enumerate(parts)]
 
     way_back = [*range(1, chips), 0]
-    normed, *experts = lax.optimization_barrier([normed, *mine, *near])
+    normed, experts = tied(normed, [*mine, *near])
     rows = {0: normed}
     arrived, answers, back, total, weights = {}, {}, {}, {}, {}
+    tables = dict(
+        rows=rows, arrived=arrived, answers=answers, back=back, total=total, weights=weights
+    )
     for now in range(2 * chips):
         new = {}
         if now + 1 < chips:
-            new["rows", now + 1] = [next_chip(rows[now])]
+            new["rows", now + 1] = [next_chip(x) for x in rows[now]]
         if now < chips:
             picked = pick(now, rows[now])
             new["arrived", now] = exchange(picked)
@@ -624,13 +599,12 @@
             new["back", k] = exchange(answers[k])
         if now > chips:
             k = way_back[now - chips - 1]
-            before = [total[way_back[now - chips - 2]]] if now > chips + 1 else []
-            new["total", k] = [next_chip(spread(k, back[k], before))]
-        if chips - 1 <= now < 2 * chips - 1:
-            k = way_back[now - chips + 1]
-            new["answers", k] = expert(arrived[k])
-        if chips <= now < 2 * chips:
-            k = way_back[now - chips]
+            before = total[way_back[now - chips - 2]] if now > chips + 1 else []
+            new["total", k] = [next_chip(x) for x in spread(k, back[k], before, False)]
+        if 1 <= now <= chips:
+            new["answers", now - 1] = expert(arrived[now - 1])
+        if 0 <= now - 1 - chips // 2 < chips:
+            k = way_back[now - 1 - chips // 2]
             new["weights", k] = [
                 call(
                     functools.partial(weights_kernel, top_count, capacity, pack, n_blk, n_uly),
@@ -638,21 +612,16 @@
                     shape(pack, 2 * tok, targets * slots),
                     [kv_steps[k]],
                     scalars=[where],
-                    unused=[answers[k][0]],
+                    unused=[arrived[min(now, chips) - 1][0]],
                     vmem_mib=3 + pack * pack // 2,
                 )
             ]
         flat = lax.optimization_barrier([x for group in new.values() for x in group])
         for (kind, k), group in new.items():
             group = [flat.pop(0) for _ in group]
-            for name, table in (("arrived", arrived), ("answers", answers), ("back", back)):
-                if kind == name:
-                    table[k] = group
-            for name, table in (("rows", rows), ("total", total), ("weights", weights)):
-                if kind == name:
-                    table[k] = group[0]
-    before = [total[way_back[-2]]] if chips > 1 else []
-    return spread(0, back[0], [*before, mixed])
+            tables[kind][k] = group
+    before = total[way_back[-2]] if chips > 1 else []
+    return spread(0, back[0], [*before, mixed], True)
 
 
 def solution(mesh):

time: 194 us -> 181 us (0.933)
  starting transfers between devices: 53.6 us -> 71.6 us
  waiting for transfers between devices: 67.8 us -> 50.8 us
  local copies, waits for them, and re-layouts: 14.2 us -> 1.74 us
  Pallas kernels: 57 us -> 53.2 us
  other arithmetic: 0.07 us -> 3.3 us
    ppermute x30 -> x36, waiting for transfers between devices: 49.4 us -> 24.4 us  [other_block(): return lax.ppermute(x, 'blk', [(b, b ^ m) for b in range(n_blk)])]
    unnamed x56 -> x18, local copies, waits for them, and re-layouts: 14.2 us -> 1.73 us
    ppermute x13 -> x19, waiting for transfers between devices: 12.7 us -> 24.7 us  [the longest x6 13.1 us: shards(): new['total', k] = [next_chip(x) for x in spread(k, back[k], before, False)]]
    ppermute x13 -> x19, starting transfers between devices: 15.1 us -> 26.6 us  [the longest x6 11.7 us: shards(): new['rows', now + 1] = [next_chip(x) for x in rows[now]]]
    ppermute x30 -> x36, starting transfers between devices: 37.8 us -> 44.4 us  [other_block(): return lax.ppermute(x, 'blk', [(b, b ^ m) for b in range(n_blk)])]
    ppermute x1, waiting for transfers between devices: 4.5 us -> 0.69 us  [shards(): other_core(for_near)]
    pallas_call x25, Pallas kernels: 57 us -> 53.2 us  [call(): pl.pallas_call(kernel, out_shape=out_shape, in_specs=[pl.BlockSpec(memory...]
  transfers between devices with their start and end apart: 45 -> 57, of which waited for: 18 -> 23; matrix products, arithmetic and copies ran while one was open for 0% -> 0% of each run, Pallas kernels for 27% -> 25%
where the time goes in v5:
time: 181 us
  starting transfers between devices  71.6 us (40%)
  Pallas kernels  53.2 us (29%)
  waiting for transfers between devices  50.8 us (28%)
  other arithmetic  3.3 us (2%)
    pallas_call x25, Pallas kernels, call(): pl.pallas_call(kernel, out_shape=out_shape, in_specs=[pl.BlockSpec(memory...  53.2 us
    ppermute x36, starting transfers between devices, other_block(): return lax.ppermute(x, 'blk', [(b, b ^ m) for b in range(n_blk)])  44.4 us
    ppermute x36, waiting for transfers between devices, other_block(): return lax.ppermute(x, 'blk', [(b, b ^ m) for b in range(n_blk)])  24.4 us
    ppermute x6, waiting for transfers between devices, shards(): new['total', k] = [next_chip(x) for x in spread(k, back[k], before, False)]  13.1 us
    ppermute x6, starting transfers between devices, shards(): new['rows', now + 1] = [next_chip(x) for x in rows[now]]  11.7 us
    ppermute x6, waiting for transfers between devices, shards(): new['rows', now + 1] = [next_chip(x) for x in rows[now]]  11.6 us
    ppermute x3, starting transfers between devices, shards(): kv_next = [next_chip(kv_steps[k])] if k < chips - 1 else []  7.15 us
    ppermute x6, starting transfers between devices, shards(): new['total', k] = [next_chip(x) for x in spread(k, back[k], before, False)]  6.67 us
  transfers between devices with their start and end apart: 57, of which 23 were waited for; matrix products, arithmetic and copies ran while one was open for 0% of the time, Pallas kernels for 25%

profile of v5, /device:TPU:0, one launch (start us, length us, event | category | flops | bytes accessed | tf_op | source)
XLA Modules:
  0.0 181.1 jit_solution(14043071828899379556)
XLA Ops:
  6.5 3.6 %collective-permute-start.4 = (bf16[2,144,256]{2,1,0:T(8,128)(2,1)S(1)}, bf16[2,144,256]{2,1,0:T(8,128)(2,1)S(1)}, u32[]{:S(2)}, u32[]{:S(2)}) collective-permute-start(bf16[2,144,256]{2,1,0:T(8,128)(2,1)S(1)} %pair.1.home_ref.refs_0_), channel_id=1, source_target_pairs={{0,24},{8,16},{16,8},{24,0},{1,25},{9,17},{17,9},{25,1},{2,26},{10... | collective-permute-start | bytes 442376 | tf_op jit(solution)/shard_map/ppermute | solution.py:463
  14.8 2.8 %collective-permute-done.3.refs_3_ = bf16[2,144,256]{2,1,0:T(8,128)(2,1)S(1)} collective-permute-done((bf16[2,144,256]{2,1,0:T(8,128)(2,1)S(1)}, bf16[2,144,256]{2,1,0:T(8,128)(2,1)S(1)}, u32[]{:S(2)}, u32[]{:S(2)}) %collective-permute-start.3) | collective-permute-done | bytes 147488 | tf_op jit(solution)/shard_map/ppermute | solution.py:463
  23.7 3.6 %attend_own.3 = (f32[2,1,1024]{2,1,0:T(1,128)S(1)}, f32[2,1,1024]{2,1,0:T(1,128)S(1)}, f32[2,128,1024]{2,1,0:T(8,128)S(1)}) custom-call(s32[2]{0:T(128)S(1)} %pad_add_fusion.where_ref, s32[64]{0:T(128)S(1)} %copy-done.6, bf16[128,1024]{1,0:T(8,128)(2,1)S(1)} %get-tuple-element.183.q_own, bf16[128,1024]{1,0:T(8,128)(2,1)S(1)} %collective-permute-done.5.q_near, ...), custom_call_target="tpu_custom_call" | custom-call | flops 1000 | bytes 1000 | tf_op jit(solution)/shard_map/attend_own/pallas_call | solution.py:26
  31.4 3.5 %collective-permute-start.10 = (bf16[2,144,256]{2,1,0:T(8,128)(2,1)S(1)}, bf16[2,144,256]{2,1,0:T(8,128)(2,1)S(1)}, u32[]{:S(2)}, u32[]{:S(2)}) collective-permute-start(bf16[2,144,256]{2,1,0:T(8,128)(2,1)S(1)} %collective-permute-done.6.refs_0_.refs_2_), channel_id=1, source_target_pairs={{0,2},{1,3},{2,6},{3,7},{6,4},{7,5},{4,0},{5,1},{8,10},{9,11},{10,... | collective-permute-start | bytes 442376 | tf_op jit(solution)/shard_map/ppermute | solution.py:508
  47.0 2.2 %collective-permute-done.16.refs_1_ = bf16[2,144,256]{2,1,0:T(8,128)(2,1)S(1)} collective-permute-done((bf16[2,144,256]{2,1,0:T(8,128)(2,1)S(1)}, bf16[2,144,256]{2,1,0:T(8,128)(2,1)S(1)}, u32[]{:S(2)}, u32[]{:S(2)}) %collective-permute-start.16) | collective-permute-done | bytes 147488 | tf_op jit(solution)/shard_map/ppermute | solution.py:463
  56.6 2.3 %collective-permute-start.24 = (bf16[2,72,1024]{2,1,0:T(8,128)(2,1)S(1)}, bf16[2,72,1024]{2,1,0:T(8,128)(2,1)S(1)}, u32[]{:S(2)}, u32[]{:S(2)}) collective-permute-start(bf16[2,72,1024]{2,1,0:T(8,128)(2,1)S(1)} %get-tuple-element.233), channel_id=1, source_target_pairs={{0,16},{8,24},{16,0},{24,8},{1,17},{9,25},{17,1},{25,9},{2,18},{10... | collective-permute-start | bytes 884744 | tf_op jit(solution)/shard_map/ppermute | solution.py:463
  58.9 3.3 %collective-permute-start.21 = (bf16[128,1024]{1,0:T(8,128)(2,1)S(1)}, bf16[128,1024]{1,0:T(8,128)(2,1)S(1)}, u32[]{:S(2)}, u32[]{:S(2)}) collective-permute-start(bf16[128,1024]{1,0:T(8,128)(2,1)S(1)} %get-tuple-element.228.left_ref), channel_id=1, source_target_pairs={{0,2},{1,3},{2,6},{3,7},{6,4},{7,5},{4,0},{5,1},{8,10},{9,11},{10,... | collective-permute-start | bytes 786440 | tf_op jit(solution)/shard_map/ppermute | solution.py:593
  63.1 6.0 %collective-permute-done.21.left_ref = bf16[128,1024]{1,0:T(8,128)(2,1)S(1)} collective-permute-done((bf16[128,1024]{1,0:T(8,128)(2,1)S(1)}, bf16[128,1024]{1,0:T(8,128)(2,1)S(1)}, u32[]{:S(2)}, u32[]{:S(2)}) %collective-permute-start.21) | collective-permute-done | bytes 262176 | tf_op jit(solution)/shard_map/ppermute | solution.py:593
  69.0 4.2 %collective-permute-done.22.right_ref = bf16[128,1024]{1,0:T(8,128)(2,1)S(1)} collective-permute-done((bf16[128,1024]{1,0:T(8,128)(2,1)S(1)}, bf16[128,1024]{1,0:T(8,128)(2,1)S(1)}, u32[]{:S(2)}, u32[]{:S(2)}) %collective-permute-start.22) | collective-permute-done | bytes 262176 | tf_op jit(solution)/shard_map/ppermute | solution.py:593
  81.1 7.1 %expert.4 = (bf16[2,72,1024]{2,1,0:T(8,128)(2,1)S(1)}, bf16[2,72,1024]{2,1,0:T(8,128)(2,1)S(1)}, bf16[2,72,1024]{2,1,0:T(8,128)(2,1)S(1)}, bf16[2,72,1024]{2,1,0:T(8,128)(2,1)S(1)}) custom-call(bf16[2,72,1024]{2,1,0:T(8,128)(2,1)S(1)} %get-tuple-element.242.refs_0_, bf16[2,72,1024]{2,1,0:T(8,128)(2,1)S(1)} %collective-permute-done.23.refs_1_, ...), custom_call_target="tpu_custom_call" | custom-call | flops 1000 | bytes 1000 | tf_op jit(solution)/shard_map/expert/pallas_call | solution.py:26
  94.7 2.7 %collective-permute-start.35 = (bf16[128,1024]{1,0:T(8,128)(2,1)S(1)}, bf16[128,1024]{1,0:T(8,128)(2,1)S(1)}, u32[]{:S(2)}, u32[]{:S(2)}) collective-permute-start(bf16[128,1024]{1,0:T(8,128)(2,1)S(1)} %collective-permute-done.27.right_ref), channel_id=1, source_target_pairs={{0,2},{1,3},{2,6},{3,7},{6,4},{7,5},{4,0},{5,1},{8,10},{9,11},{10,... | collective-permute-start | bytes 786440 | tf_op jit(solution)/shard_map/ppermute | solution.py:593
  97.4 7.1 %expert.5 = (bf16[2,72,1024]{2,1,0:T(8,128)(2,1)S(1)}, bf16[2,72,1024]{2,1,0:T(8,128)(2,1)S(1)}, bf16[2,72,1024]{2,1,0:T(8,128)(2,1)S(1)}, bf16[2,72,1024]{2,1,0:T(8,128)(2,1)S(1)}) custom-call(bf16[2,72,1024]{2,1,0:T(8,128)(2,1)S(1)} %get-tuple-element.269.refs_0_, bf16[2,72,1024]{2,1,0:T(8,128)(2,1)S(1)} %collective-permute-done.28.refs_1_, ...), custom_call_target="tpu_custom_call" | custom-call | flops 1000 | bytes 1000 | tf_op jit(solution)/shard_map/expert/pallas_call | solution.py:26
  111.2 3.9 %collective-permute-done.42.refs_1_ = bf16[2,72,1024]{2,1,0:T(8,128)(2,1)S(1)} collective-permute-done((bf16[2,72,1024]{2,1,0:T(8,128)(2,1)S(1)}, bf16[2,72,1024]{2,1,0:T(8,128)(2,1)S(1)}, u32[]{:S(2)}, u32[]{:S(2)}) %collective-permute-start.42) | collective-permute-done | bytes 294944 | tf_op jit(solution)/shard_map/ppermute | solution.py:463
  118.5 7.1 %expert.6 = (bf16[2,72,1024]{2,1,0:T(8,128)(2,1)S(1)}, bf16[2,72,1024]{2,1,0:T(8,128)(2,1)S(1)}, bf16[2,72,1024]{2,1,0:T(8,128)(2,1)S(1)}, bf16[2,72,1024]{2,1,0:T(8,128)(2,1)S(1)}) custom-call(bf16[2,72,1024]{2,1,0:T(8,128)(2,1)S(1)} %get-tuple-element.288.refs_0_.refs_1_, bf16[2,72,1024]{2,1,0:T(8,128)(2,1)S(1)} %collective-permute-done.36.refs_1_, ...), custom_call_target="tpu_custom_call" | custom-call | flops 1000 | bytes 1000 | tf_op jit(solution)/shard_map/expert/pallas_call | solution.py:26
  128.1 7.2 %expert.7 = (bf16[2,72,1024]{2,1,0:T(8,128)(2,1)S(1)}, bf16[2,72,1024]{2,1,0:T(8,128)(2,1)S(1)}, bf16[2,72,1024]{2,1,0:T(8,128)(2,1)S(1)}, bf16[2,72,1024]{2,1,0:T(8,128)(2,1)S(1)}) custom-call(bf16[2,72,1024]{2,1,0:T(8,128)(2,1)S(1)} %get-tuple-element.296.refs_0_.refs_1_, bf16[2,72,1024]{2,1,0:T(8,128)(2,1)S(1)} %collective-permute-done.42.refs_1_, ...), custom_call_target="tpu_custom_call" | custom-call | flops 1000 | bytes 1000 | tf_op jit(solution)/shard_map/expert/pallas_call | solution.py:26
  136.3 2.7 %collective-permute-start.52 = (bf16[128,1024]{1,0:T(8,128)(2,1)S(1)}, bf16[128,1024]{1,0:T(8,128)(2,1)S(1)}, u32[]{:S(2)}, u32[]{:S(2)}) collective-permute-start(bf16[128,1024]{1,0:T(8,128)(2,1)S(1)} %get-tuple-element.318), channel_id=1, source_target_pairs={{0,2},{1,3},{2,6},{3,7},{6,4},{7,5},{4,0},{5,1},{8,10},{9,11},{10,... | collective-permute-start | bytes 786440 | tf_op jit(solution)/shard_map/ppermute | solution.py:603
  141.6 2.4 %collective-permute-done.51.refs_5_ = bf16[128,1024]{1,0:T(8,128)(2,1)S(1)} collective-permute-done((bf16[128,1024]{1,0:T(8,128)(2,1)S(1)}, bf16[128,1024]{1,0:T(8,128)(2,1)S(1)}, u32[]{:S(2)}, u32[]{:S(2)}) %collective-permute-start.51) | collective-permute-done | bytes 262176 | tf_op jit(solution)/shard_map/ppermute | solution.py:603
  145.1 4.6 %collective-permute-done.52.refs_6_ = bf16[128,1024]{1,0:T(8,128)(2,1)S(1)} collective-permute-done((bf16[128,1024]{1,0:T(8,128)(2,1)S(1)}, bf16[128,1024]{1,0:T(8,128)(2,1)S(1)}, u32[]{:S(2)}, u32[]{:S(2)}) %collective-permute-start.52) | collective-permute-done | bytes 262176 | tf_op jit(solution)/shard_map/ppermute | solution.py:603
  149.6 2.5 %collective-permute-start.47 = (bf16[2,72,1024]{2,1,0:T(8,128)(2,1)S(1)}, bf16[2,72,1024]{2,1,0:T(8,128)(2,1)S(1)}, u32[]{:S(2)}, u32[]{:S(2)}) collective-permute-start(bf16[2,72,1024]{2,1,0:T(8,128)(2,1)S(1)} %get-tuple-element.307), channel_id=1, source_target_pairs={{0,24},{8,16},{16,8},{24,0},{1,25},{9,17},{17,9},{25,1},{2,26},{10... | collective-permute-start | bytes 884744 | tf_op jit(solution)/shard_map/ppermute | solution.py:463
  153.5 3.5 %collective-permute-done.49.refs_2_ = bf16[2,72,1024]{2,1,0:T(8,128)(2,1)S(1)} collective-permute-done((bf16[2,72,1024]{2,1,0:T(8,128)(2,1)S(1)}, bf16[2,72,1024]{2,1,0:T(8,128)(2,1)S(1)}, u32[]{:S(2)}, u32[]{:S(2)}) %collective-permute-start.49) | collective-permute-done | bytes 294944 | tf_op jit(solution)/shard_map/ppermute | solution.py:463
  161.2 2.7 %collective-permute-done.46.refs_2_ = bf16[2,72,1024]{2,1,0:T(8,128)(2,1)S(1)} collective-permute-done((bf16[2,72,1024]{2,1,0:T(8,128)(2,1)S(1)}, bf16[2,72,1024]{2,1,0:T(8,128)(2,1)S(1)}, u32[]{:S(2)}, u32[]{:S(2)}) %collective-permute-start.46) | collective-permute-done | bytes 294944 | tf_op jit(solution)/shard_map/ppermute | solution.py:463
  171.4 2.4 %collective-permute-done.32.refs_2_ = bf16[2,72,1024]{2,1,0:T(8,128)(2,1)S(1)} collective-permute-done((bf16[2,72,1024]{2,1,0:T(8,128)(2,1)S(1)}, bf16[2,72,1024]{2,1,0:T(8,128)(2,1)S(1)}, u32[]{:S(2)}, u32[]{:S(2)}) %collective-permute-start.32) | collective-permute-done | bytes 294944 | tf_op jit(solution)/shard_map/ppermute | solution.py:463
  173.8 2.7 %collective-permute-done.55.refs_5_ = bf16[128,1024]{1,0:T(8,128)(2,1)S(1)} collective-permute-done((bf16[128,1024]{1,0:T(8,128)(2,1)S(1)}, bf16[128,1024]{1,0:T(8,128)(2,1)S(1)}, u32[]{:S(2)}, u32[]{:S(2)}) %collective-permute-start.55) | collective-permute-done | bytes 262176 | tf_op jit(solution)/shard_map/ppermute | solution.py:603
  176.5 2.8 %collective-permute-done.56.refs_6_ = bf16[128,1024]{1,0:T(8,128)(2,1)S(1)} collective-permute-done((bf16[128,1024]{1,0:T(8,128)(2,1)S(1)}, bf16[128,1024]{1,0:T(8,128)(2,1)S(1)}, u32[]{:S(2)}, u32[]{:S(2)}) %collective-permute-start.56) | collective-permute-done | bytes 262176 | tf_op jit(solution)/shard_map/ppermute | solution.py:603
  (140 shorter events, 87.7 us)
Async XLA Ops:
  6.1 11.8 %collective-permute-start.5 = (bf16[128,1024]{1,0:T(8,128)(2,1)S(1)}, bf16[128,1024]{1,0:T(8,128)(2,1)S(1)}, u32[]{:S(2)}, u32[]{:S(2)}) collective-permute-start(bf16[128,1024]{1,0:T(8,128)(2,1)S(1)} %get-tuple-element.182), channel_id=1, source_target_pairs={{0,1},{1,0},{2,3},{3,2},{4,5},{5,4},{6,7},{7,6},{8,9},{9,8},{10,11... | collective-permute-start | bytes 786440 | tf_op jit(solution)/shard_map/ppermute | solution.py:509
  55.1 18.1 %collective-permute-start.23 = (bf16[2,72,1024]{2,1,0:T(8,128)(2,1)S(1)}, bf16[2,72,1024]{2,1,0:T(8,128)(2,1)S(1)}, u32[]{:S(2)}, u32[]{:S(2)}) collective-permute-start(bf16[2,72,1024]{2,1,0:T(8,128)(2,1)S(1)} %get-tuple-element.232), channel_id=1, source_target_pairs={{0,8},{8,0},{16,24},{24,16},{1,9},{9,1},{17,25},{25,17},{2,10},{10... | collective-permute-start | bytes 884744 | tf_op jit(solution)/shard_map/ppermute | solution.py:463
  56.6 16.6 %collective-permute-start.24 = (bf16[2,72,1024]{2,1,0:T(8,128)(2,1)S(1)}, bf16[2,72,1024]{2,1,0:T(8,128)(2,1)S(1)}, u32[]{:S(2)}, u32[]{:S(2)}) collective-permute-start(bf16[2,72,1024]{2,1,0:T(8,128)(2,1)S(1)} %get-tuple-element.233), channel_id=1, source_target_pairs={{0,16},{8,24},{16,0},{24,8},{1,17},{9,25},{17,1},{25,9},{2,18},{10... | collective-permute-start | bytes 884744 | tf_op jit(solution)/shard_map/ppermute | solution.py:463
  58.9 14.3 %collective-permute-start.25 = (bf16[2,72,1024]{2,1,0:T(8,128)(2,1)S(1)}, bf16[2,72,1024]{2,1,0:T(8,128)(2,1)S(1)}, u32[]{:S(2)}, u32[]{:S(2)}) collective-permute-start(bf16[2,72,1024]{2,1,0:T(8,128)(2,1)S(1)} %get-tuple-element.234), channel_id=1, source_target_pairs={{0,24},{8,16},{16,8},{24,0},{1,25},{9,17},{17,9},{25,1},{2,26},{10... | collective-permute-start | bytes 884744 | tf_op jit(solution)/shard_map/ppermute | solution.py:463
  73.7 16.1 %collective-permute-start.28 = (bf16[2,72,1024]{2,1,0:T(8,128)(2,1)S(1)}, bf16[2,72,1024]{2,1,0:T(8,128)(2,1)S(1)}, u32[]{:S(2)}, u32[]{:S(2)}) collective-permute-start(bf16[2,72,1024]{2,1,0:T(8,128)(2,1)S(1)} %get-tuple-element.239), channel_id=1, source_target_pairs={{0,8},{8,0},{16,24},{24,16},{1,9},{9,1},{17,25},{25,17},{2,10},{10... | collective-permute-start | bytes 884744 | tf_op jit(solution)/shard_map/ppermute | solution.py:463
  75.2 14.6 %collective-permute-start.29 = (bf16[2,72,1024]{2,1,0:T(8,128)(2,1)S(1)}, bf16[2,72,1024]{2,1,0:T(8,128)(2,1)S(1)}, u32[]{:S(2)}, u32[]{:S(2)}) collective-permute-start(bf16[2,72,1024]{2,1,0:T(8,128)(2,1)S(1)} %get-tuple-element.240), channel_id=1, source_target_pairs={{0,16},{8,24},{16,0},{24,8},{1,17},{9,25},{17,1},{25,9},{2,18},{10... | collective-permute-start | bytes 884744 | tf_op jit(solution)/shard_map/ppermute | solution.py:463
  76.9 12.8 %collective-permute-start.30 = (bf16[2,72,1024]{2,1,0:T(8,128)(2,1)S(1)}, bf16[2,72,1024]{2,1,0:T(8,128)(2,1)S(1)}, u32[]{:S(2)}, u32[]{:S(2)}) collective-permute-start(bf16[2,72,1024]{2,1,0:T(8,128)(2,1)S(1)} %get-tuple-element.241), channel_id=1, source_target_pairs={{0,24},{8,16},{16,8},{24,0},{1,25},{9,17},{17,9},{25,1},{2,26},{10... | collective-permute-start | bytes 884744 | tf_op jit(solution)/shard_map/ppermute | solution.py:463
  77.2 11.1 %collective-permute-start.26 = (bf16[128,1024]{1,0:T(8,128)(2,1)S(1)}, bf16[128,1024]{1,0:T(8,128)(2,1)S(1)}, u32[]{:S(2)}, u32[]{:S(2)}) collective-permute-start(bf16[128,1024]{1,0:T(8,128)(2,1)S(1)} %collective-permute-done.21.left_ref), channel_id=1, source_target_pairs={{0,2},{1,3},{2,6},{3,7},{6,4},{7,5},{4,0},{5,1},{8,10},{9,11},{10,... | collective-permute-start | bytes 786440 | tf_op jit(solution)/shard_map/ppermute | solution.py:593
  90.2 14.4 %collective-permute-start.36 = (bf16[2,72,1024]{2,1,0:T(8,128)(2,1)S(1)}, bf16[2,72,1024]{2,1,0:T(8,128)(2,1)S(1)}, u32[]{:S(2)}, u32[]{:S(2)}) collective-permute-start(bf16[2,72,1024]{2,1,0:T(8,128)(2,1)S(1)} %get-tuple-element.266), channel_id=1, source_target_pairs={{0,8},{8,0},{16,24},{24,16},{1,9},{9,1},{17,25},{25,17},{2,10},{10... | collective-permute-start | bytes 884744 | tf_op jit(solution)/shard_map/ppermute | solution.py:463
  91.8 12.8 %collective-permute-start.37 = (bf16[2,72,1024]{2,1,0:T(8,128)(2,1)S(1)}, bf16[2,72,1024]{2,1,0:T(8,128)(2,1)S(1)}, u32[]{:S(2)}, u32[]{:S(2)}) collective-permute-start(bf16[2,72,1024]{2,1,0:T(8,128)(2,1)S(1)} %get-tuple-element.267), channel_id=1, source_target_pairs={{0,16},{8,24},{16,0},{24,8},{1,17},{9,25},{17,1},{25,9},{2,18},{10... | collective-permute-start | bytes 884744 | tf_op jit(solution)/shard_map/ppermute | solution.py:463
  93.2 11.4 %collective-permute-start.38 = (bf16[2,72,1024]{2,1,0:T(8,128)(2,1)S(1)}, bf16[2,72,1024]{2,1,0:T(8,128)(2,1)S(1)}, u32[]{:S(2)}, u32[]{:S(2)}) collective-permute-start(bf16[2,72,1024]{2,1,0:T(8,128)(2,1)S(1)} %get-tuple-element.268), channel_id=1, source_target_pairs={{0,24},{8,16},{16,8},{24,0},{1,25},{9,17},{17,9},{25,1},{2,26},{10... | collective-permute-start | bytes 884744 | tf_op jit(solution)/shard_map/ppermute | solution.py:463
  106.6 19.1 %collective-permute-start.43 = (bf16[2,72,1024]{2,1,0:T(8,128)(2,1)S(1)}, bf16[2,72,1024]{2,1,0:T(8,128)(2,1)S(1)}, u32[]{:S(2)}, u32[]{:S(2)}) collective-permute-start(bf16[2,72,1024]{2,1,0:T(8,128)(2,1)S(1)} %get-tuple-element.286), channel_id=1, source_target_pairs={{0,16},{8,24},{16,0},{24,8},{1,17},{9,25},{17,1},{25,9},{2,18},{10... | collective-permute-start | bytes 884744 | tf_op jit(solution)/shard_map/ppermute | solution.py:463
  107.7 17.9 %collective-permute-start.44 = (bf16[2,72,1024]{2,1,0:T(8,128)(2,1)S(1)}, bf16[2,72,1024]{2,1,0:T(8,128)(2,1)S(1)}, u32[]{:S(2)}, u32[]{:S(2)}) collective-permute-start(bf16[2,72,1024]{2,1,0:T(8,128)(2,1)S(1)} %get-tuple-element.287), channel_id=1, source_target_pairs={{0,24},{8,16},{16,8},{24,0},{1,25},{9,17},{17,9},{25,1},{2,26},{10... | collective-permute-start | bytes 884744 | tf_op jit(solution)/shard_map/ppermute | solution.py:463
  108.7 26.6 %collective-permute-start.39 = (bf16[2,72,1024]{2,1,0:T(8,128)(2,1)S(1)}, bf16[2,72,1024]{2,1,0:T(8,128)(2,1)S(1)}, u32[]{:S(2)}, u32[]{:S(2)}) collective-permute-start(bf16[2,72,1024]{2,1,0:T(8,128)(2,1)S(1)} %get-tuple-element.278), channel_id=1, source_target_pairs={{0,8},{8,0},{16,24},{24,16},{1,9},{9,1},{17,25},{25,17},{2,10},{10... | collective-permute-start | bytes 884744 | tf_op jit(solution)/shard_map/ppermute | solution.py:463
  110.1 25.2 %collective-permute-start.40 = (bf16[2,72,1024]{2,1,0:T(8,128)(2,1)S(1)}, bf16[2,72,1024]{2,1,0:T(8,128)(2,1)S(1)}, u32[]{:S(2)}, u32[]{:S(2)}) collective-permute-start(bf16[2,72,1024]{2,1,0:T(8,128)(2,1)S(1)} %get-tuple-element.279), channel_id=1, source_target_pairs={{0,16},{8,24},{16,0},{24,8},{1,17},{9,25},{17,1},{25,9},{2,18},{10... | collective-permute-start | bytes 884744 | tf_op jit(solution)/shard_map/ppermute | solution.py:463
  115.1 20.2 %collective-permute-start.41 = (bf16[2,72,1024]{2,1,0:T(8,128)(2,1)S(1)}, bf16[2,72,1024]{2,1,0:T(8,128)(2,1)S(1)}, u32[]{:S(2)}, u32[]{:S(2)}) collective-permute-start(bf16[2,72,1024]{2,1,0:T(8,128)(2,1)S(1)} %get-tuple-element.280), channel_id=1, source_target_pairs={{0,24},{8,16},{16,8},{24,0},{1,25},{9,17},{17,9},{25,1},{2,26},{10... | collective-permute-start | bytes 884744 | tf_op jit(solution)/shard_map/ppermute | solution.py:463
  125.7 23.9 %collective-permute-start.48 = (bf16[2,72,1024]{2,1,0:T(8,128)(2,1)S(1)}, bf16[2,72,1024]{2,1,0:T(8,128)(2,1)S(1)}, u32[]{:S(2)}, u32[]{:S(2)}) collective-permute-start(bf16[2,72,1024]{2,1,0:T(8,128)(2,1)S(1)} %get-tuple-element.309), channel_id=1, source_target_pairs={{0,8},{8,0},{16,24},{24,16},{1,9},{9,1},{17,25},{25,17},{2,10},{10... | collective-permute-start | bytes 884744 | tf_op jit(solution)/shard_map/ppermute | solution.py:463
  136.3 13.3 %collective-permute-start.52 = (bf16[128,1024]{1,0:T(8,128)(2,1)S(1)}, bf16[128,1024]{1,0:T(8,128)(2,1)S(1)}, u32[]{:S(2)}, u32[]{:S(2)}) collective-permute-start(bf16[128,1024]{1,0:T(8,128)(2,1)S(1)} %get-tuple-element.318), channel_id=1, source_target_pairs={{0,2},{1,3},{2,6},{3,7},{6,4},{7,5},{4,0},{5,1},{8,10},{9,11},{10,... | collective-permute-start | bytes 786440 | tf_op jit(solution)/shard_map/ppermute | solution.py:603
  139.0 18.1 %collective-permute-start.49 = (bf16[2,72,1024]{2,1,0:T(8,128)(2,1)S(1)}, bf16[2,72,1024]{2,1,0:T(8,128)(2,1)S(1)}, u32[]{:S(2)}, u32[]{:S(2)}) collective-permute-start(bf16[2,72,1024]{2,1,0:T(8,128)(2,1)S(1)} %get-tuple-element.310), channel_id=1, source_target_pairs={{0,16},{8,24},{16,0},{24,8},{1,17},{9,25},{17,1},{25,9},{2,18},{10... | collective-permute-start | bytes 884744 | tf_op jit(solution)/shard_map/ppermute | solution.py:463
  140.2 16.9 %collective-permute-start.50 = (bf16[2,72,1024]{2,1,0:T(8,128)(2,1)S(1)}, bf16[2,72,1024]{2,1,0:T(8,128)(2,1)S(1)}, u32[]{:S(2)}, u32[]{:S(2)}) collective-permute-start(bf16[2,72,1024]{2,1,0:T(8,128)(2,1)S(1)} %get-tuple-element.311), channel_id=1, source_target_pairs={{0,24},{8,16},{16,8},{24,0},{1,25},{9,17},{17,9},{25,1},{2,26},{10... | collective-permute-start | bytes 884744 | tf_op jit(solution)/shard_map/ppermute | solution.py:463
  144.0 15.8 %collective-permute-start.45 = (bf16[2,72,1024]{2,1,0:T(8,128)(2,1)S(1)}, bf16[2,72,1024]{2,1,0:T(8,128)(2,1)S(1)}, u32[]{:S(2)}, u32[]{:S(2)}) collective-permute-start(bf16[2,72,1024]{2,1,0:T(8,128)(2,1)S(1)} %get-tuple-element.305), channel_id=1, source_target_pairs={{0,8},{8,0},{16,24},{24,16},{1,9},{9,1},{17,25},{25,17},{2,10},{10... | collective-permute-start | bytes 884744 | tf_op jit(solution)/shard_map/ppermute | solution.py:463
  149.6 14.3 %collective-permute-start.46 = (bf16[2,72,1024]{2,1,0:T(8,128)(2,1)S(1)}, bf16[2,72,1024]{2,1,0:T(8,128)(2,1)S(1)}, u32[]{:S(2)}, u32[]{:S(2)}) collective-permute-start(bf16[2,72,1024]{2,1,0:T(8,128)(2,1)S(1)} %get-tuple-element.306), channel_id=1, source_target_pairs={{0,16},{8,24},{16,0},{24,8},{1,17},{9,25},{17,1},{25,9},{2,18},{10... | collective-permute-start | bytes 884744 | tf_op jit(solution)/shard_map/ppermute | solution.py:463
  149.6 14.9 %collective-permute-start.47 = (bf16[2,72,1024]{2,1,0:T(8,128)(2,1)S(1)}, bf16[2,72,1024]{2,1,0:T(8,128)(2,1)S(1)}, u32[]{:S(2)}, u32[]{:S(2)}) collective-permute-start(bf16[2,72,1024]{2,1,0:T(8,128)(2,1)S(1)} %get-tuple-element.307), channel_id=1, source_target_pairs={{0,24},{8,16},{16,8},{24,0},{1,25},{9,17},{17,9},{25,1},{2,26},{10... | collective-permute-start | bytes 884744 | tf_op jit(solution)/shard_map/ppermute | solution.py:463
  159.8 11.6 %collective-permute-start.31 = (bf16[2,72,1024]{2,1,0:T(8,128)(2,1)S(1)}, bf16[2,72,1024]{2,1,0:T(8,128)(2,1)S(1)}, u32[]{:S(2)}, u32[]{:S(2)}) collective-permute-start(bf16[2,72,1024]{2,1,0:T(8,128)(2,1)S(1)} %get-tuple-element.259), channel_id=1, source_target_pairs={{0,8},{8,0},{16,24},{24,16},{1,9},{9,1},{17,25},{25,17},{2,10},{10... | collective-permute-start | bytes 884744 | tf_op jit(solution)/shard_map/ppermute | solution.py:463
  (42 other events, 389.7 us)

commit v6 on v5

--- a/solution.py
+++ b/solution.py
@@ -37,13 +37,14 @@
     )(*scalars, *operands, *unused)
 
 
-def message_kernel(core_ref, kv_ref, small_ref, keep, give):
+def message_kernel(core_ref, kv_ref, small_ref, gates_ref, keep, give):
     tok = kv_ref.shape[0]
-    top_count = small_ref.shape[0] // 3
+    top_count = gates_ref.shape[0]
     first = core_ref[0] == 0
     k0, k1, v0, v1 = (kv_ref[:, i * HEAD_SIZE : (i + 1) * HEAD_SIZE] for i in range(4))
     v0, v1 = (v.astype(F32).T.astype(BF16) for v in (v0, v1))
-    ids, gates, segs = (small_ref[i * top_count : (i + 1) * top_count] for i in range(3))
+    ids, segs = (small_ref[i * top_count : (i + 1) * top_count].astype(F32) for i in range(2))
+    gates = gates_ref[...]
     share = gates / jnp.sum(gates, axis=0, keepdims=True)
     share_hi = share.astype(BF16).astype(F32)
     left = jnp.concatenate([ids, share_hi], axis=0)
@@ -475,13 +476,8 @@
         [shape(tok + 16, 2 * HEAD_SIZE)] * 2,
         [
             jnp.concatenate([keys, values], axis=1),
-            jnp.concatenate(
-                [
-                    expert_ids.T.astype(F32),
-                    gates.T,
-                    jnp.broadcast_to(segment_ids.astype(F32), (top_count, tok)),
-                ]
-            ),
+            jnp.concatenate([expert_ids.T, jnp.broadcast_to(segment_ids, (top_count, tok))]),
+            gates.T,
         ],
         scalars=[core_here],
     )

time: 181 us -> 181 us (level)
  starting transfers between devices: 71.6 us -> 69.7 us
    ppermute x6, waiting for transfers between devices: 11.6 us -> 13.9 us  [shards(): new['rows', now + 1] = [next_chip(x) for x in rows[now]]]
    ppermute x6, starting transfers between devices: 11.7 us -> 9.43 us  [shards(): new['rows', now + 1] = [next_chip(x) for x in rows[now]]]
  transfers between devices with their start and end apart: 57 -> 57, of which waited for: 23 -> 22; matrix products, arithmetic and copies ran while one was open for 0% -> 0% of each run, Pallas kernels for 25% -> 25%
where the time goes in v6:
time: 181 us; the launch traced here: 180 us
  starting transfers between devices  69.7 us (39%)
  Pallas kernels  53.2 us (29%)
  waiting for transfers between devices  52.2 us (29%)
  local copies, waits for them, and re-layouts  3.22 us (2%)
    pallas_call x25, Pallas kernels, call(): pl.pallas_call(kernel, out_shape=out_shape, in_specs=[pl.BlockSpec(memory...  53.2 us
    ppermute x36, starting transfers between devices, other_block(): return lax.ppermute(x, 'blk', [(b, b ^ m) for b in range(n_blk)])  44 us
    ppermute x36, waiting for transfers between devices, other_block(): return lax.ppermute(x, 'blk', [(b, b ^ m) for b in range(n_blk)])  23.7 us
    ppermute x6, waiting for transfers between devices, shards(): new['rows', now + 1] = [next_chip(x) for x in rows[now]]  13.9 us
    ppermute x6, waiting for transfers between devices, shards(): new['total', k] = [next_chip(x) for x in spread(k, back[k], before, False)]  12.9 us
    ppermute x6, starting transfers between devices, shards(): new['rows', now + 1] = [next_chip(x) for x in rows[now]]  9.43 us
    ppermute x6, starting transfers between devices, shards(): new['total', k] = [next_chip(x) for x in spread(k, back[k], before, False)]  7.39 us
    ppermute x3, starting transfers between devices, shards(): kv_next = [next_chip(kv_steps[k])] if k < chips - 1 else []  7.24 us
  transfers between devices with their start and end apart: 57, of which 22 were waited for; matrix products, arithmetic and copies ran while one was open for 0% of the time, Pallas kernels for 25%

profile of v6, /device:TPU:0, one launch (start us, length us, event | category | flops | bytes accessed | tf_op | source)
XLA Modules:
  0.0 180.5 jit_solution(5495980183119673078)
XLA Ops:
  6.5 3.6 %collective-permute-start.4 = (bf16[2,144,256]{2,1,0:T(8,128)(2,1)S(1)}, bf16[2,144,256]{2,1,0:T(8,128)(2,1)S(1)}, u32[]{:S(2)}, u32[]{:S(2)}) collective-permute-start(bf16[2,144,256]{2,1,0:T(8,128)(2,1)S(1)} %pair.1.home_ref.refs_0_), channel_id=1, source_target_pairs={{0,24},{8,16},{16,8},{24,0},{1,25},{9,17},{17,9},{25,1},{2,26},{10... | collective-permute-start | bytes 442376 | tf_op jit(solution)/shard_map/ppermute | solution.py:464
  14.8 2.8 %collective-permute-done.3.refs_3_ = bf16[2,144,256]{2,1,0:T(8,128)(2,1)S(1)} collective-permute-done((bf16[2,144,256]{2,1,0:T(8,128)(2,1)S(1)}, bf16[2,144,256]{2,1,0:T(8,128)(2,1)S(1)}, u32[]{:S(2)}, u32[]{:S(2)}) %collective-permute-start.3) | collective-permute-done | bytes 147488 | tf_op jit(solution)/shard_map/ppermute | solution.py:464
  23.6 3.6 %attend_own.3 = (f32[2,1,1024]{2,1,0:T(1,128)S(1)}, f32[2,1,1024]{2,1,0:T(1,128)S(1)}, f32[2,128,1024]{2,1,0:T(8,128)S(1)}) custom-call(s32[2]{0:T(128)S(1)} %pad_add_fusion.1.where_ref, s32[64]{0:T(128)S(1)} %copy-done.6, bf16[128,1024]{1,0:T(8,128)(2,1)S(1)} %get-tuple-element.183.q_own, bf16[128,1024]{1,0:T(8,128)(2,1)S(1)} %collective-permute-done.5.q_near, ...), custom_call_target="tpu_custom_call" | custom-call | flops 1000 | bytes 1000 | tf_op jit(solution)/shard_map/attend_own/pallas_call | solution.py:26
  27.8 2.2 %collective-permute-start.13 = (bf16[2,144,256]{2,1,0:T(8,128)(2,1)S(1)}, bf16[2,144,256]{2,1,0:T(8,128)(2,1)S(1)}, u32[]{:S(2)}, u32[]{:S(2)}) collective-permute-start(bf16[2,144,256]{2,1,0:T(8,128)(2,1)S(1)} %collective-permute-done.6.refs_0_.refs_2_), channel_id=1, source_target_pairs={{0,24},{8,16},{16,8},{24,0},{1,25},{9,17},{17,9},{25,1},{2,26},{10... | collective-permute-start | bytes 442376 | tf_op jit(solution)/shard_map/ppermute | solution.py:464
  31.3 3.6 %collective-permute-start.10 = (bf16[2,144,256]{2,1,0:T(8,128)(2,1)S(1)}, bf16[2,144,256]{2,1,0:T(8,128)(2,1)S(1)}, u32[]{:S(2)}, u32[]{:S(2)}) collective-permute-start(bf16[2,144,256]{2,1,0:T(8,128)(2,1)S(1)} %collective-permute-done.6.refs_0_.refs_2_), channel_id=1, source_target_pairs={{0,2},{1,3},{2,6},{3,7},{6,4},{7,5},{4,0},{5,1},{8,10},{9,11},{10,... | collective-permute-start | bytes 442376 | tf_op jit(solution)/shard_map/ppermute | solution.py:504
  46.3 2.3 %collective-permute-done.16.refs_1_ = bf16[2,144,256]{2,1,0:T(8,128)(2,1)S(1)} collective-permute-done((bf16[2,144,256]{2,1,0:T(8,128)(2,1)S(1)}, bf16[2,144,256]{2,1,0:T(8,128)(2,1)S(1)}, u32[]{:S(2)}, u32[]{:S(2)}) %collective-permute-start.16) | collective-permute-done | bytes 147488 | tf_op jit(solution)/shard_map/ppermute | solution.py:464
  58.7 2.8 %collective-permute-start.21 = (bf16[128,1024]{1,0:T(8,128)(2,1)S(1)}, bf16[128,1024]{1,0:T(8,128)(2,1)S(1)}, u32[]{:S(2)}, u32[]{:S(2)}) collective-permute-start(bf16[128,1024]{1,0:T(8,128)(2,1)S(1)} %get-tuple-element.228.left_ref), channel_id=1, source_target_pairs={{0,2},{1,3},{2,6},{3,7},{6,4},{7,5},{4,0},{5,1},{8,10},{9,11},{10,... | collective-permute-start | bytes 786440 | tf_op jit(solution)/shard_map/ppermute | solution.py:589
  62.2 6.7 %collective-permute-done.21.left_ref = bf16[128,1024]{1,0:T(8,128)(2,1)S(1)} collective-permute-done((bf16[128,1024]{1,0:T(8,128)(2,1)S(1)}, bf16[128,1024]{1,0:T(8,128)(2,1)S(1)}, u32[]{:S(2)}, u32[]{:S(2)}) %collective-permute-start.21) | collective-permute-done | bytes 262176 | tf_op jit(solution)/shard_map/ppermute | solution.py:589
  68.9 4.2 %collective-permute-done.22.right_ref = bf16[128,1024]{1,0:T(8,128)(2,1)S(1)} collective-permute-done((bf16[128,1024]{1,0:T(8,128)(2,1)S(1)}, bf16[128,1024]{1,0:T(8,128)(2,1)S(1)}, u32[]{:S(2)}, u32[]{:S(2)}) %collective-permute-start.22) | collective-permute-done | bytes 262176 | tf_op jit(solution)/shard_map/ppermute | solution.py:589
  80.3 7.1 %expert.4 = (bf16[2,72,1024]{2,1,0:T(8,128)(2,1)S(1)}, bf16[2,72,1024]{2,1,0:T(8,128)(2,1)S(1)}, bf16[2,72,1024]{2,1,0:T(8,128)(2,1)S(1)}, bf16[2,72,1024]{2,1,0:T(8,128)(2,1)S(1)}) custom-call(bf16[2,72,1024]{2,1,0:T(8,128)(2,1)S(1)} %get-tuple-element.242.refs_0_, bf16[2,72,1024]{2,1,0:T(8,128)(2,1)S(1)} %collective-permute-done.23.refs_1_, ...), custom_call_target="tpu_custom_call" | custom-call | flops 1000 | bytes 1000 | tf_op jit(solution)/shard_map/expert/pallas_call | solution.py:26
  87.4 2.2 %collective-permute-done.27.right_ref = bf16[128,1024]{1,0:T(8,128)(2,1)S(1)} collective-permute-done((bf16[128,1024]{1,0:T(8,128)(2,1)S(1)}, bf16[128,1024]{1,0:T(8,128)(2,1)S(1)}, u32[]{:S(2)}, u32[]{:S(2)}) %collective-permute-start.27) | collective-permute-done | bytes 262176 | tf_op jit(solution)/shard_map/ppermute | solution.py:589
  96.5 7.1 %expert.5 = (bf16[2,72,1024]{2,1,0:T(8,128)(2,1)S(1)}, bf16[2,72,1024]{2,1,0:T(8,128)(2,1)S(1)}, bf16[2,72,1024]{2,1,0:T(8,128)(2,1)S(1)}, bf16[2,72,1024]{2,1,0:T(8,128)(2,1)S(1)}) custom-call(bf16[2,72,1024]{2,1,0:T(8,128)(2,1)S(1)} %get-tuple-element.269.refs_0_, bf16[2,72,1024]{2,1,0:T(8,128)(2,1)S(1)} %collective-permute-done.28.refs_1_, ...), custom_call_target="tpu_custom_call" | custom-call | flops 1000 | bytes 1000 | tf_op jit(solution)/shard_map/expert/pallas_call | solution.py:26
  111.1 3.8 %collective-permute-done.42.refs_1_ = bf16[2,72,1024]{2,1,0:T(8,128)(2,1)S(1)} collective-permute-done((bf16[2,72,1024]{2,1,0:T(8,128)(2,1)S(1)}, bf16[2,72,1024]{2,1,0:T(8,128)(2,1)S(1)}, u32[]{:S(2)}, u32[]{:S(2)}) %collective-permute-start.42) | collective-permute-done | bytes 294944 | tf_op jit(solution)/shard_map/ppermute | solution.py:464
  118.4 7.1 %expert.6 = (bf16[2,72,1024]{2,1,0:T(8,128)(2,1)S(1)}, bf16[2,72,1024]{2,1,0:T(8,128)(2,1)S(1)}, bf16[2,72,1024]{2,1,0:T(8,128)(2,1)S(1)}, bf16[2,72,1024]{2,1,0:T(8,128)(2,1)S(1)}) custom-call(bf16[2,72,1024]{2,1,0:T(8,128)(2,1)S(1)} %get-tuple-element.288.refs_0_.refs_1_, bf16[2,72,1024]{2,1,0:T(8,128)(2,1)S(1)} %collective-permute-done.36.refs_1_, ...), custom_call_target="tpu_custom_call" | custom-call | flops 1000 | bytes 1000 | tf_op jit(solution)/shard_map/expert/pallas_call | solution.py:26
  128.0 7.2 %expert.7 = (bf16[2,72,1024]{2,1,0:T(8,128)(2,1)S(1)}, bf16[2,72,1024]{2,1,0:T(8,128)(2,1)S(1)}, bf16[2,72,1024]{2,1,0:T(8,128)(2,1)S(1)}, bf16[2,72,1024]{2,1,0:T(8,128)(2,1)S(1)}) custom-call(bf16[2,72,1024]{2,1,0:T(8,128)(2,1)S(1)} %get-tuple-element.296.refs_0_.refs_1_, bf16[2,72,1024]{2,1,0:T(8,128)(2,1)S(1)} %collective-permute-done.42.refs_1_, ...), custom_call_target="tpu_custom_call" | custom-call | flops 1000 | bytes 1000 | tf_op jit(solution)/shard_map/expert/pallas_call | solution.py:26
  136.3 2.4 %collective-permute-start.52 = (bf16[128,1024]{1,0:T(8,128)(2,1)S(1)}, bf16[128,1024]{1,0:T(8,128)(2,1)S(1)}, u32[]{:S(2)}, u32[]{:S(2)}) collective-permute-start(bf16[128,1024]{1,0:T(8,128)(2,1)S(1)} %get-tuple-element.318), channel_id=1, source_target_pairs={{0,2},{1,3},{2,6},{3,7},{6,4},{7,5},{4,0},{5,1},{8,10},{9,11},{10,... | collective-permute-start | bytes 786440 | tf_op jit(solution)/shard_map/ppermute | solution.py:599
  140.8 3.3 %collective-permute-done.51.refs_5_ = bf16[128,1024]{1,0:T(8,128)(2,1)S(1)} collective-permute-done((bf16[128,1024]{1,0:T(8,128)(2,1)S(1)}, bf16[128,1024]{1,0:T(8,128)(2,1)S(1)}, u32[]{:S(2)}, u32[]{:S(2)}) %collective-permute-start.51) | collective-permute-done | bytes 262176 | tf_op jit(solution)/shard_map/ppermute | solution.py:599
  144.8 4.8 %collective-permute-done.52.refs_6_ = bf16[128,1024]{1,0:T(8,128)(2,1)S(1)} collective-permute-done((bf16[128,1024]{1,0:T(8,128)(2,1)S(1)}, bf16[128,1024]{1,0:T(8,128)(2,1)S(1)}, u32[]{:S(2)}, u32[]{:S(2)}) %collective-permute-start.52) | collective-permute-done | bytes 262176 | tf_op jit(solution)/shard_map/ppermute | solution.py:599
  149.6 2.3 %collective-permute-start.47 = (bf16[2,72,1024]{2,1,0:T(8,128)(2,1)S(1)}, bf16[2,72,1024]{2,1,0:T(8,128)(2,1)S(1)}, u32[]{:S(2)}, u32[]{:S(2)}) collective-permute-start(bf16[2,72,1024]{2,1,0:T(8,128)(2,1)S(1)} %get-tuple-element.307), channel_id=1, source_target_pairs={{0,24},{8,16},{16,8},{24,0},{1,25},{9,17},{17,9},{25,1},{2,26},{10... | collective-permute-start | bytes 884744 | tf_op jit(solution)/shard_map/ppermute | solution.py:464
  153.3 2.9 %collective-permute-done.49.refs_2_ = bf16[2,72,1024]{2,1,0:T(8,128)(2,1)S(1)} collective-permute-done((bf16[2,72,1024]{2,1,0:T(8,128)(2,1)S(1)}, bf16[2,72,1024]{2,1,0:T(8,128)(2,1)S(1)}, u32[]{:S(2)}, u32[]{:S(2)}) %collective-permute-start.49) | collective-permute-done | bytes 294944 | tf_op jit(solution)/shard_map/ppermute | solution.py:464
  160.8 3.2 %collective-permute-done.46.refs_2_ = bf16[2,72,1024]{2,1,0:T(8,128)(2,1)S(1)} collective-permute-done((bf16[2,72,1024]{2,1,0:T(8,128)(2,1)S(1)}, bf16[2,72,1024]{2,1,0:T(8,128)(2,1)S(1)}, u32[]{:S(2)}, u32[]{:S(2)}) %collective-permute-start.46) | collective-permute-done | bytes 294944 | tf_op jit(solution)/shard_map/ppermute | solution.py:464
  168.7 2.3 %collective-permute-start.56 = (bf16[128,1024]{1,0:T(8,128)(2,1)S(1)}, bf16[128,1024]{1,0:T(8,128)(2,1)S(1)}, u32[]{:S(2)}, u32[]{:S(2)}) collective-permute-start(bf16[128,1024]{1,0:T(8,128)(2,1)S(1)} %get-tuple-element.336), channel_id=1, source_target_pairs={{0,2},{1,3},{2,6},{3,7},{6,4},{7,5},{4,0},{5,1},{8,10},{9,11},{10,... | collective-permute-start | bytes 786440 | tf_op jit(solution)/shard_map/ppermute | solution.py:599
  171.0 2.8 %collective-permute-done.32.refs_2_ = bf16[2,72,1024]{2,1,0:T(8,128)(2,1)S(1)} collective-permute-done((bf16[2,72,1024]{2,1,0:T(8,128)(2,1)S(1)}, bf16[2,72,1024]{2,1,0:T(8,128)(2,1)S(1)}, u32[]{:S(2)}, u32[]{:S(2)}) %collective-permute-start.32) | collective-permute-done | bytes 294944 | tf_op jit(solution)/shard_map/ppermute | solution.py:464
  175.9 2.8 %collective-permute-done.56.refs_6_ = bf16[128,1024]{1,0:T(8,128)(2,1)S(1)} collective-permute-done((bf16[128,1024]{1,0:T(8,128)(2,1)S(1)}, bf16[128,1024]{1,0:T(8,128)(2,1)S(1)}, u32[]{:S(2)}, u32[]{:S(2)}) %collective-permute-start.56) | collective-permute-done | bytes 262176 | tf_op jit(solution)/shard_map/ppermute | solution.py:599
  (140 shorter events, 86.9 us)
Async XLA Ops:
  6.0 11.8 %collective-permute-start.5 = (bf16[128,1024]{1,0:T(8,128)(2,1)S(1)}, bf16[128,1024]{1,0:T(8,128)(2,1)S(1)}, u32[]{:S(2)}, u32[]{:S(2)}) collective-permute-start(bf16[128,1024]{1,0:T(8,128)(2,1)S(1)} %get-tuple-element.182), channel_id=1, source_target_pairs={{0,1},{1,0},{2,3},{3,2},{4,5},{5,4},{6,7},{7,6},{8,9},{9,8},{10,11... | collective-permute-start | bytes 786440 | tf_op jit(solution)/shard_map/ppermute | solution.py:505
  54.5 18.6 %collective-permute-start.23 = (bf16[2,72,1024]{2,1,0:T(8,128)(2,1)S(1)}, bf16[2,72,1024]{2,1,0:T(8,128)(2,1)S(1)}, u32[]{:S(2)}, u32[]{:S(2)}) collective-permute-start(bf16[2,72,1024]{2,1,0:T(8,128)(2,1)S(1)} %get-tuple-element.232), channel_id=1, source_target_pairs={{0,8},{8,0},{16,24},{24,16},{1,9},{9,1},{17,25},{25,17},{2,10},{10... | collective-permute-start | bytes 884744 | tf_op jit(solution)/shard_map/ppermute | solution.py:464
  56.7 16.4 %collective-permute-start.24 = (bf16[2,72,1024]{2,1,0:T(8,128)(2,1)S(1)}, bf16[2,72,1024]{2,1,0:T(8,128)(2,1)S(1)}, u32[]{:S(2)}, u32[]{:S(2)}) collective-permute-start(bf16[2,72,1024]{2,1,0:T(8,128)(2,1)S(1)} %get-tuple-element.233), channel_id=1, source_target_pairs={{0,16},{8,24},{16,0},{24,8},{1,17},{9,25},{17,1},{25,9},{2,18},{10... | collective-permute-start | bytes 884744 | tf_op jit(solution)/shard_map/ppermute | solution.py:464
  58.7 14.3 %collective-permute-start.25 = (bf16[2,72,1024]{2,1,0:T(8,128)(2,1)S(1)}, bf16[2,72,1024]{2,1,0:T(8,128)(2,1)S(1)}, u32[]{:S(2)}, u32[]{:S(2)}) collective-permute-start(bf16[2,72,1024]{2,1,0:T(8,128)(2,1)S(1)} %get-tuple-element.234), channel_id=1, source_target_pairs={{0,24},{8,16},{16,8},{24,0},{1,25},{9,17},{17,9},{25,1},{2,26},{10... | collective-permute-start | bytes 884744 | tf_op jit(solution)/shard_map/ppermute | solution.py:464
  61.6 11.5 %collective-permute-start.22 = (bf16[128,1024]{1,0:T(8,128)(2,1)S(1)}, bf16[128,1024]{1,0:T(8,128)(2,1)S(1)}, u32[]{:S(2)}, u32[]{:S(2)}) collective-permute-start(bf16[128,1024]{1,0:T(8,128)(2,1)S(1)} %get-tuple-element.229.right_ref), channel_id=1, source_target_pairs={{0,2},{1,3},{2,6},{3,7},{6,4},{7,5},{4,0},{5,1},{8,10},{9,11},{10,... | collective-permute-start | bytes 786440 | tf_op jit(solution)/shard_map/ppermute | solution.py:589
  73.5 16.1 %collective-permute-start.28 = (bf16[2,72,1024]{2,1,0:T(8,128)(2,1)S(1)}, bf16[2,72,1024]{2,1,0:T(8,128)(2,1)S(1)}, u32[]{:S(2)}, u32[]{:S(2)}) collective-permute-start(bf16[2,72,1024]{2,1,0:T(8,128)(2,1)S(1)} %get-tuple-element.239), channel_id=1, source_target_pairs={{0,8},{8,0},{16,24},{24,16},{1,9},{9,1},{17,25},{25,17},{2,10},{10... | collective-permute-start | bytes 884744 | tf_op jit(solution)/shard_map/ppermute | solution.py:464
  75.1 14.6 %collective-permute-start.29 = (bf16[2,72,1024]{2,1,0:T(8,128)(2,1)S(1)}, bf16[2,72,1024]{2,1,0:T(8,128)(2,1)S(1)}, u32[]{:S(2)}, u32[]{:S(2)}) collective-permute-start(bf16[2,72,1024]{2,1,0:T(8,128)(2,1)S(1)} %get-tuple-element.240), channel_id=1, source_target_pairs={{0,16},{8,24},{16,0},{24,8},{1,17},{9,25},{17,1},{25,9},{2,18},{10... | collective-permute-start | bytes 884744 | tf_op jit(solution)/shard_map/ppermute | solution.py:464
  76.8 12.8 %collective-permute-start.30 = (bf16[2,72,1024]{2,1,0:T(8,128)(2,1)S(1)}, bf16[2,72,1024]{2,1,0:T(8,128)(2,1)S(1)}, u32[]{:S(2)}, u32[]{:S(2)}) collective-permute-start(bf16[2,72,1024]{2,1,0:T(8,128)(2,1)S(1)} %get-tuple-element.241), channel_id=1, source_target_pairs={{0,24},{8,16},{16,8},{24,0},{1,25},{9,17},{17,9},{25,1},{2,26},{10... | collective-permute-start | bytes 884744 | tf_op jit(solution)/shard_map/ppermute | solution.py:464
  90.1 14.4 %collective-permute-start.36 = (bf16[2,72,1024]{2,1,0:T(8,128)(2,1)S(1)}, bf16[2,72,1024]{2,1,0:T(8,128)(2,1)S(1)}, u32[]{:S(2)}, u32[]{:S(2)}) collective-permute-start(bf16[2,72,1024]{2,1,0:T(8,128)(2,1)S(1)} %get-tuple-element.266), channel_id=1, source_target_pairs={{0,8},{8,0},{16,24},{24,16},{1,9},{9,1},{17,25},{25,17},{2,10},{10... | collective-permute-start | bytes 884744 | tf_op jit(solution)/shard_map/ppermute | solution.py:464
  91.7 12.8 %collective-permute-start.37 = (bf16[2,72,1024]{2,1,0:T(8,128)(2,1)S(1)}, bf16[2,72,1024]{2,1,0:T(8,128)(2,1)S(1)}, u32[]{:S(2)}, u32[]{:S(2)}) collective-permute-start(bf16[2,72,1024]{2,1,0:T(8,128)(2,1)S(1)} %get-tuple-element.267), channel_id=1, source_target_pairs={{0,16},{8,24},{16,0},{24,8},{1,17},{9,25},{17,1},{25,9},{2,18},{10... | collective-permute-start | bytes 884744 | tf_op jit(solution)/shard_map/ppermute | solution.py:464
  93.1 11.4 %collective-permute-start.38 = (bf16[2,72,1024]{2,1,0:T(8,128)(2,1)S(1)}, bf16[2,72,1024]{2,1,0:T(8,128)(2,1)S(1)}, u32[]{:S(2)}, u32[]{:S(2)}) collective-permute-start(bf16[2,72,1024]{2,1,0:T(8,128)(2,1)S(1)} %get-tuple-element.268), channel_id=1, source_target_pairs={{0,24},{8,16},{16,8},{24,0},{1,25},{9,17},{17,9},{25,1},{2,26},{10... | collective-permute-start | bytes 884744 | tf_op jit(solution)/shard_map/ppermute | solution.py:464
  106.5 19.1 %collective-permute-start.43 = (bf16[2,72,1024]{2,1,0:T(8,128)(2,1)S(1)}, bf16[2,72,1024]{2,1,0:T(8,128)(2,1)S(1)}, u32[]{:S(2)}, u32[]{:S(2)}) collective-permute-start(bf16[2,72,1024]{2,1,0:T(8,128)(2,1)S(1)} %get-tuple-element.286), channel_id=1, source_target_pairs={{0,16},{8,24},{16,0},{24,8},{1,17},{9,25},{17,1},{25,9},{2,18},{10... | collective-permute-start | bytes 884744 | tf_op jit(solution)/shard_map/ppermute | solution.py:464
  107.7 17.9 %collective-permute-start.44 = (bf16[2,72,1024]{2,1,0:T(8,128)(2,1)S(1)}, bf16[2,72,1024]{2,1,0:T(8,128)(2,1)S(1)}, u32[]{:S(2)}, u32[]{:S(2)}) collective-permute-start(bf16[2,72,1024]{2,1,0:T(8,128)(2,1)S(1)} %get-tuple-element.287), channel_id=1, source_target_pairs={{0,24},{8,16},{16,8},{24,0},{1,25},{9,17},{17,9},{25,1},{2,26},{10... | collective-permute-start | bytes 884744 | tf_op jit(solution)/shard_map/ppermute | solution.py:464
  108.5 26.7 %collective-permute-start.39 = (bf16[2,72,1024]{2,1,0:T(8,128)(2,1)S(1)}, bf16[2,72,1024]{2,1,0:T(8,128)(2,1)S(1)}, u32[]{:S(2)}, u32[]{:S(2)}) collective-permute-start(bf16[2,72,1024]{2,1,0:T(8,128)(2,1)S(1)} %get-tuple-element.278), channel_id=1, source_target_pairs={{0,8},{8,0},{16,24},{24,16},{1,9},{9,1},{17,25},{25,17},{2,10},{10... | collective-permute-start | bytes 884744 | tf_op jit(solution)/shard_map/ppermute | solution.py:464
  110.0 25.2 %collective-permute-start.40 = (bf16[2,72,1024]{2,1,0:T(8,128)(2,1)S(1)}, bf16[2,72,1024]{2,1,0:T(8,128)(2,1)S(1)}, u32[]{:S(2)}, u32[]{:S(2)}) collective-permute-start(bf16[2,72,1024]{2,1,0:T(8,128)(2,1)S(1)} %get-tuple-element.279), channel_id=1, source_target_pairs={{0,16},{8,24},{16,0},{24,8},{1,17},{9,25},{17,1},{25,9},{2,18},{10... | collective-permute-start | bytes 884744 | tf_op jit(solution)/shard_map/ppermute | solution.py:464
  115.0 20.2 %collective-permute-start.41 = (bf16[2,72,1024]{2,1,0:T(8,128)(2,1)S(1)}, bf16[2,72,1024]{2,1,0:T(8,128)(2,1)S(1)}, u32[]{:S(2)}, u32[]{:S(2)}) collective-permute-start(bf16[2,72,1024]{2,1,0:T(8,128)(2,1)S(1)} %get-tuple-element.280), channel_id=1, source_target_pairs={{0,24},{8,16},{16,8},{24,0},{1,25},{9,17},{17,9},{25,1},{2,26},{10... | collective-permute-start | bytes 884744 | tf_op jit(solution)/shard_map/ppermute | solution.py:464
  125.6 24.1 %collective-permute-start.48 = (bf16[2,72,1024]{2,1,0:T(8,128)(2,1)S(1)}, bf16[2,72,1024]{2,1,0:T(8,128)(2,1)S(1)}, u32[]{:S(2)}, u32[]{:S(2)}) collective-permute-start(bf16[2,72,1024]{2,1,0:T(8,128)(2,1)S(1)} %get-tuple-element.309), channel_id=1, source_target_pairs={{0,8},{8,0},{16,24},{24,16},{1,9},{9,1},{17,25},{25,17},{2,10},{10... | collective-permute-start | bytes 884744 | tf_op jit(solution)/shard_map/ppermute | solution.py:464
  136.3 13.4 %collective-permute-start.52 = (bf16[128,1024]{1,0:T(8,128)(2,1)S(1)}, bf16[128,1024]{1,0:T(8,128)(2,1)S(1)}, u32[]{:S(2)}, u32[]{:S(2)}) collective-permute-start(bf16[128,1024]{1,0:T(8,128)(2,1)S(1)} %get-tuple-element.318), channel_id=1, source_target_pairs={{0,2},{1,3},{2,6},{3,7},{6,4},{7,5},{4,0},{5,1},{8,10},{9,11},{10,... | collective-permute-start | bytes 786440 | tf_op jit(solution)/shard_map/ppermute | solution.py:599
  138.7 17.5 %collective-permute-start.49 = (bf16[2,72,1024]{2,1,0:T(8,128)(2,1)S(1)}, bf16[2,72,1024]{2,1,0:T(8,128)(2,1)S(1)}, u32[]{:S(2)}, u32[]{:S(2)}) collective-permute-start(bf16[2,72,1024]{2,1,0:T(8,128)(2,1)S(1)} %get-tuple-element.310), channel_id=1, source_target_pairs={{0,16},{8,24},{16,0},{24,8},{1,17},{9,25},{17,1},{25,9},{2,18},{10... | collective-permute-start | bytes 884744 | tf_op jit(solution)/shard_map/ppermute | solution.py:464
  139.3 16.9 %collective-permute-start.50 = (bf16[2,72,1024]{2,1,0:T(8,128)(2,1)S(1)}, bf16[2,72,1024]{2,1,0:T(8,128)(2,1)S(1)}, u32[]{:S(2)}, u32[]{:S(2)}) collective-permute-start(bf16[2,72,1024]{2,1,0:T(8,128)(2,1)S(1)} %get-tuple-element.311), channel_id=1, source_target_pairs={{0,24},{8,16},{16,8},{24,0},{1,25},{9,17},{17,9},{25,1},{2,26},{10... | collective-permute-start | bytes 884744 | tf_op jit(solution)/shard_map/ppermute | solution.py:464
  144.0 15.6 %collective-permute-start.45 = (bf16[2,72,1024]{2,1,0:T(8,128)(2,1)S(1)}, bf16[2,72,1024]{2,1,0:T(8,128)(2,1)S(1)}, u32[]{:S(2)}, u32[]{:S(2)}) collective-permute-start(bf16[2,72,1024]{2,1,0:T(8,128)(2,1)S(1)} %get-tuple-element.305), channel_id=1, source_target_pairs={{0,8},{8,0},{16,24},{24,16},{1,9},{9,1},{17,25},{25,17},{2,10},{10... | collective-permute-start | bytes 884744 | tf_op jit(solution)/shard_map/ppermute | solution.py:464
  149.6 14.3 %collective-permute-start.46 = (bf16[2,72,1024]{2,1,0:T(8,128)(2,1)S(1)}, bf16[2,72,1024]{2,1,0:T(8,128)(2,1)S(1)}, u32[]{:S(2)}, u32[]{:S(2)}) collective-permute-start(bf16[2,72,1024]{2,1,0:T(8,128)(2,1)S(1)} %get-tuple-element.306), channel_id=1, source_target_pairs={{0,16},{8,24},{16,0},{24,8},{1,17},{9,25},{17,1},{25,9},{2,18},{10... | collective-permute-start | bytes 884744 | tf_op jit(solution)/shard_map/ppermute | solution.py:464
  149.6 14.7 %collective-permute-start.47 = (bf16[2,72,1024]{2,1,0:T(8,128)(2,1)S(1)}, bf16[2,72,1024]{2,1,0:T(8,128)(2,1)S(1)}, u32[]{:S(2)}, u32[]{:S(2)}) collective-permute-start(bf16[2,72,1024]{2,1,0:T(8,128)(2,1)S(1)} %get-tuple-element.307), channel_id=1, source_target_pairs={{0,24},{8,16},{16,8},{24,0},{1,25},{9,17},{17,9},{25,1},{2,26},{10... | collective-permute-start | bytes 884744 | tf_op jit(solution)/shard_map/ppermute | solution.py:464
  159.7 11.4 %collective-permute-start.31 = (bf16[2,72,1024]{2,1,0:T(8,128)(2,1)S(1)}, bf16[2,72,1024]{2,1,0:T(8,128)(2,1)S(1)}, u32[]{:S(2)}, u32[]{:S(2)}) collective-permute-start(bf16[2,72,1024]{2,1,0:T(8,128)(2,1)S(1)} %get-tuple-element.259), channel_id=1, source_target_pairs={{0,8},{8,0},{16,24},{24,16},{1,9},{9,1},{17,25},{25,17},{2,10},{10... | collective-permute-start | bytes 884744 | tf_op jit(solution)/shard_map/ppermute | solution.py:464
  (43 other events, 385.9 us)
